TPU v7x, 32 devices: a whole 2x2x4 slice. The times are simulated.
32 devices in a mesh: series: 4 (over y, core), tm: 8 (over z, x).
Axes of the slice: x: 2, y: 2, z: 4, core: 2. Of those that a mesh axis runs over, the one named last changes fastest.
Arguments:
- inputs: bfloat16 [4, 3072, 512], P('series', 'tm'), may hold values from -6 to 6
- lengths: int32 [4, 4], P('series'), may hold values from 1 to 32, 64 in all within a row
- stride_weight_twelve: bfloat16 [6144, 512], P('tm'), may hold values from -0.078125 to 0.078125
- stride_bias_twelve: float32 [512], replicated, may hold values from -3 to 3
- isometric_weight_twelve: bfloat16 [8192, 512], P('tm'), may hold values from -0.0625 to 0.0625
- isometric_bias_twelve: float32 [512], replicated, may hold values from -3 to 3
- upsample_weight_twelve: bfloat16 [6144, 512], P('tm'), may hold values from -0.25 to 0.25
- upsample_bias_twelve: float32 [512], replicated, may hold values from -3 to 3
- stride_weight_sixteen: bfloat16 [8192, 512], P('tm'), may hold values from -0.0625 to 0.0625
- stride_bias_sixteen: float32 [512], replicated, may hold values from -3 to 3
- isometric_weight_sixteen: bfloat16 [6144, 512], P('tm'), may hold values from -0.078125 to 0.078125
- isometric_bias_sixteen: float32 [512], replicated, may hold values from -3 to 3
- upsample_weight_sixteen: bfloat16 [8192, 512], P('tm'), may hold values from -0.25 to 0.25
- upsample_bias_sixteen: float32 [512], replicated, may hold values from -3 to 3
- mix_gain: float32 [512], replicated, may hold values from 0.5 to 1.5
- mix_shift: float32 [512], replicated, may hold values from -2 to 2
- merge_weight: bfloat16 [1024, 512], P('tm'), may hold values from -0.1875 to 0.1875
- merge_bias: float32 [512], replicated, may hold values from -3 to 3
- feed_gain: float32 [512], replicated, may hold values from 0.5 to 1.5
- feed_shift: float32 [512], replicated, may hold values from -2 to 2
- expand_weight: bfloat16 [2048, 512], P('tm'), may hold values from -0.25 to 0.25
- expand_bias: float32 [2048], replicated, may hold values from -3 to 3
- project_weight: bfloat16 [2048, 512], P('tm'), may hold values from -0.125 to 0.125
- project_bias: float32 [512], replicated, may hold values from -3 to 3
- final_gain: float32 [512], replicated, may hold values from 0.5 to 1.5
- final_shift: float32 [512], replicated, may hold values from -2 to 2
- cotangent: bfloat16 [4, 3072, 512], P('series', 'tm'), may hold values from -6 to 6
Outputs:
- output: bfloat16 [4, 3072, 512], P('series', 'tm')
- input_grad: bfloat16 [4, 3072, 512], P('series', 'tm')
- stride_weight_twelve_grad: float32 [6144, 512], P('tm')
- stride_bias_twelve_grad: float32 [512], replicated
- isometric_weight_twelve_grad: float32 [8192, 512], P('tm')
- isometric_bias_twelve_grad: float32 [512], replicated
- upsample_weight_twelve_grad: float32 [6144, 512], P('tm')
- upsample_bias_twelve_grad: float32 [512], replicated
- stride_weight_sixteen_grad: float32 [8192, 512], P('tm')
- stride_bias_sixteen_grad: float32 [512], replicated
- isometric_weight_sixteen_grad: float32 [6144, 512], P('tm')
- isometric_bias_sixteen_grad: float32 [512], replicated
- upsample_weight_sixteen_grad: float32 [8192, 512], P('tm')
- upsample_bias_sixteen_grad: float32 [512], replicated
- mix_gain_grad: float32 [512], replicated
- mix_shift_grad: float32 [512], replicated
- merge_weight_grad: float32 [1024, 512], P('tm')
- merge_bias_grad: float32 [512], replicated
- feed_gain_grad: float32 [512], replicated
- feed_shift_grad: float32 [512], replicated
- expand_weight_grad: float32 [2048, 512], P('tm')
- expand_bias_grad: float32 [2048], replicated
- project_weight_grad: float32 [2048, 512], P('tm')
- project_bias_grad: float32 [512], replicated
- final_gain_grad: float32 [512], replicated
- final_shift_grad: float32 [512], replicated
Inputs may be any that keep to these rules, and one draw needn't show every extreme that they name: Each row lists the lengths of one group's series in order, in units of 48 time steps; a row sums to 64 and its longest series has exactly 32.
All inputs are finite; a program needn't handle non-finite values.
Results may differ from a plain program's by a relative error of at most 0.017.
Values may be sent and summed in bfloat16 or wider, within the bound.
No kernel may reach another device: no remote copies, remote signals or barrier semaphores. Data moves between devices by JAX's collectives and lax.ppermute only.
A program may use at most 320 MiB of HBM per device.

v0:
```python
import jax
import jax.numpy as jnp
from jax import lax
from jax.sharding import PartitionSpec as P

SCALE_ONE = 12
SCALE_TWO = 16
MA_ONE = 13
MA_TWO = 17
ISO_ONE = 16
ISO_TWO = 12
UNIT = 48


EPSILON = 1e-05


def with_halo(x, sides, width):
    for axis, dim in sides:
        size, length = (lax.axis_size(axis), x.shape[dim])
        up = [(i, (i + 1) % size) for i in range(size - 1)]
        down = [(j, i) for i, j in up]
        last = lax.slice_in_dim(x, length - width, length, axis=dim)
        leading = lax.slice_in_dim(x, 0, width, axis=dim)
        before = lax.ppermute(last, axis, up)
        after = lax.ppermute(leading, axis, down)
        x = jnp.concatenate([before, x, after], axis=dim)
    return x


def passed_along(block, axis, distance):
    devices = range(lax.axis_size(axis))
    route = [(i - distance, i) for i in devices if i - distance in devices]
    return lax.ppermute(block, axis, route)


def layer_norm(values, scale_gain, offset_shift):
    average = jnp.mean(values, axis=-1, keepdims=True)
    centered = values - average
    variance = jnp.mean(centered * centered, axis=-1, keepdims=True)
    return centered * lax.rsqrt(variance + EPSILON) * scale_gain + offset_shift


def exact_gelu(values):
    return jax.nn.gelu(values, approximate=False)


def series_bounds(lengths_row, places):
    ends = UNIT * jnp.cumsum(lengths_row)
    starts = ends - UNIT * lengths_row
    inside = (starts[None, :] <= places[:, None]) & (places[:, None] < ends[None, :])
    zero = jnp.zeros((), jnp.int32)
    series_first = jnp.sum(jnp.where(inside, starts[None, :], zero), axis=1)
    series_last = jnp.sum(jnp.where(inside, ends[None, :], zero), axis=1)
    return (series_first, series_last)


def forward_dot(left, right):
    return jnp.dot(left, right, preferred_element_type=jnp.float32)


def gradient_dot(left, right):
    return lax.dot_general(
        left, right, (((0,), (0,)), ((), ())), preferred_element_type=jnp.float32
    )


def backward_dot(left, right):
    return lax.dot_general(
        left, right, (((1,), (1,)), ((), ())), preferred_element_type=jnp.float32
    )


def trend_of(extended, places, base_row, series_first, series_last, average_kernel, halo_width):
    reach = average_kernel // 2
    total = jnp.zeros((places.shape[0], extended.shape[1]), jnp.float32)
    for offset in range(-reach, reach + 1):
        gather_index = (
            jnp.clip(places + offset, series_first, series_last - 1) - base_row + halo_width
        )
        total = total + jnp.take(extended, gather_index, axis=0)
    return total / average_kernel


def trend_adjoint(
    d_around, places, series_first, series_last, ext_first, average_kernel, halo_width
):
    row_count = places.shape[0]
    reach = average_kernel // 2
    adjoint = jnp.zeros((row_count, d_around.shape[1]), jnp.float32)
    for offset in range(-reach, reach + 1):
        lower_row = halo_width + offset
        same_series = ext_first[lower_row : lower_row + row_count] == series_first
        adjoint = adjoint + jnp.where(
            same_series[:, None], d_around[lower_row : lower_row + row_count], 0.0
        )
    head_sum = jnp.zeros((row_count, d_around.shape[1]), jnp.float32)
    tail_sum = jnp.zeros((row_count, d_around.shape[1]), jnp.float32)
    for lead_step in range(reach):
        head_sum = (
            head_sum
            + (reach - lead_step)
            * d_around[halo_width + lead_step : halo_width + lead_step + row_count]
        )
        tail_sum = (
            tail_sum
            + (reach - lead_step)
            * d_around[halo_width - lead_step : halo_width - lead_step + row_count]
        )
    adjoint = adjoint + jnp.where((places == series_first)[:, None], head_sum, 0.0)
    adjoint = adjoint + jnp.where((places == series_last - 1)[:, None], tail_sum, 0.0)
    return adjoint


def on_device(
    inputs,
    lengths,
    stride_weight_twelve,
    stride_bias_twelve,
    isometric_weight_twelve,
    isometric_bias_twelve,
    upsample_weight_twelve,
    upsample_bias_twelve,
    stride_weight_sixteen,
    stride_bias_sixteen,
    isometric_weight_sixteen,
    isometric_bias_sixteen,
    upsample_weight_sixteen,
    upsample_bias_sixteen,
    mix_gain,
    mix_shift,
    merge_weight,
    merge_bias,
    feed_gain,
    feed_shift,
    expand_weight,
    expand_bias,
    project_weight,
    project_bias,
    final_gain,
    final_shift,
    cotangent,
):
    (
        stride_weight_twelve,
        isometric_weight_twelve,
        upsample_weight_twelve,
        stride_weight_sixteen,
        isometric_weight_sixteen,
        upsample_weight_sixteen,
        merge_weight,
        expand_weight,
        project_weight,
    ) = (
        lax.all_gather(stride_weight_twelve, "tm", axis=0, tiled=True),
        lax.all_gather(isometric_weight_twelve, "tm", axis=0, tiled=True),
        lax.all_gather(upsample_weight_twelve, "tm", axis=0, tiled=True),
        lax.all_gather(stride_weight_sixteen, "tm", axis=0, tiled=True),
        lax.all_gather(isometric_weight_sixteen, "tm", axis=0, tiled=True),
        lax.all_gather(upsample_weight_sixteen, "tm", axis=0, tiled=True),
        lax.all_gather(merge_weight, "tm", axis=0, tiled=True),
        lax.all_gather(expand_weight, "tm", axis=0, tiled=True),
        lax.all_gather(project_weight, "tm", axis=0, tiled=True),
    )
    row_count = inputs.shape[1]
    channels = inputs.shape[2]
    halo_width = max(MA_ONE, MA_TWO) // 2
    scales = (SCALE_ONE, SCALE_TWO)
    averages = (MA_ONE, MA_TWO)
    tap_counts = (ISO_ONE, ISO_TWO)
    stride_weights = (stride_weight_twelve, stride_weight_sixteen)
    stride_biases = (stride_bias_twelve, stride_bias_sixteen)
    iso_weights = (isometric_weight_twelve, isometric_weight_sixteen)
    iso_biases = (isometric_bias_twelve, isometric_bias_sixteen)
    up_weights = (upsample_weight_twelve, upsample_weight_sixteen)
    up_biases = (upsample_bias_twelve, upsample_bias_sixteen)
    lengths_row = lengths[0]
    base_row = lax.axis_index("tm") * row_count
    places = base_row + jnp.arange(row_count, dtype=jnp.int32)
    series_first, series_last = series_bounds(lengths_row, places)
    tokens = inputs[0]
    bf_zero = jnp.zeros((), jnp.bfloat16)
    extended = with_halo(tokens, (("tm", 0),), halo_width).astype(jnp.float32)
    tokens_wide = tokens.astype(jnp.float32)
    seasons = [
        tokens_wide
        - trend_of(
            extended, places, base_row, series_first, series_last, averages[branch], halo_width
        )
        for branch in range(2)
    ]
    season_lows = [season.astype(jnp.bfloat16) for season in seasons]
    halves = [scale // 2 for scale in scales]
    lags = [taps - 1 for taps in tap_counts]
    step_counts = [row_count // scale for scale in scales]
    season_rims = passed_along(
        jnp.concatenate(
            [season_lows[0][row_count - halves[0] :], season_lows[1][row_count - halves[1] :]],
            axis=0,
        ),
        "tm",
        1,
    )
    rim_parts = (season_rims[: halves[0]], season_rims[halves[0] :])
    keep_masks = []
    windows_list = []
    tanh_ones = []
    hidden_ones = []
    hidden_lows = []
    start_steps = []
    for branch in range(2):
        scale = scales[branch]
        half_scale = halves[branch]
        step_count = step_counts[branch]
        padded = jnp.concatenate(
            [rim_parts[branch], season_lows[branch][: row_count - half_scale]], axis=0
        )
        block_first = series_first[::scale]
        at_start = block_first == places[::scale]
        keep_mask = jnp.logical_not(
            at_start[:, None] & (jnp.arange(scale, dtype=jnp.int32)[None, :] < half_scale)
        )
        windows = jnp.where(
            keep_mask[:, :, None], padded.reshape(step_count, scale, channels), bf_zero
        ).reshape(step_count, scale * channels)
        hidden_one, tanh_one = jax.vjp(
            jnp.tanh, forward_dot(windows, stride_weights[branch]) + stride_biases[branch]
        )
        keep_masks.append(keep_mask)
        windows_list.append(windows)
        tanh_ones.append(tanh_one)
        hidden_ones.append(hidden_one)
        hidden_lows.append(hidden_one.astype(jnp.bfloat16))
        start_steps.append((block_first - base_row) // scale)
    iso_rims = passed_along(
        jnp.concatenate(
            [
                hidden_lows[0][step_counts[0] - lags[0] :],
                hidden_lows[1][step_counts[1] - lags[1] :],
            ],
            axis=0,
        ),
        "tm",
        1,
    )
    iso_parts = (iso_rims[: lags[0]], iso_rims[lags[0] :])
    tap_valids = []
    stacked_list = []
    tanh_twos = []
    norm_ones = []
    mixed_lows = []
    tanh_ups = []
    norm_twos = []
    branch_lows = []
    for branch in range(2):
        step_count = step_counts[branch]
        lag = lags[branch]
        hidden_ext = jnp.concatenate([iso_parts[branch], hidden_lows[branch]], axis=0)
        step_index = jnp.arange(step_count, dtype=jnp.int32)
        tap_valid = [
            (step_index - lag + position >= start_steps[branch])[:, None]
            for position in range(tap_counts[branch])
        ]
        stacked = jnp.concatenate(
            [
                jnp.where(
                    tap_valid[position], hidden_ext[position : position + step_count], bf_zero
                )
                for position in range(tap_counts[branch])
            ],
            axis=1,
        )
        hidden_two, tanh_two = jax.vjp(
            jnp.tanh, forward_dot(stacked, iso_weights[branch]) + iso_biases[branch]
        )
        mixed_one, norm_one = jax.vjp(
            layer_norm, hidden_two + hidden_ones[branch], mix_gain, mix_shift
        )
        mixed_low = mixed_one.astype(jnp.bfloat16)
        up_pre = (
            backward_dot(mixed_low, up_weights[branch]).reshape(row_count, channels)
            + up_biases[branch]
        )
        upsampled, tanh_up = jax.vjp(jnp.tanh, up_pre)
        branch_out, norm_two = jax.vjp(layer_norm, upsampled + seasons[branch], mix_gain, mix_shift)
        tap_valids.append(tap_valid)
        stacked_list.append(stacked)
        tanh_twos.append(tanh_two)
        norm_ones.append(norm_one)
        mixed_lows.append(mixed_low)
        tanh_ups.append(tanh_up)
        norm_twos.append(norm_two)
        branch_lows.append(branch_out.astype(jnp.bfloat16))
    merge_in = jnp.concatenate(branch_lows, axis=1)
    merged = forward_dot(merge_in, merge_weight) + merge_bias
    normed, norm_three = jax.vjp(layer_norm, merged, feed_gain, feed_shift)
    normed_low = normed.astype(jnp.bfloat16)
    activ, gelu_back = jax.vjp(exact_gelu, backward_dot(normed_low, expand_weight) + expand_bias)
    activ_low = activ.astype(jnp.bfloat16)
    summed = merged + forward_dot(activ_low, project_weight) + project_bias
    result, norm_four = jax.vjp(layer_norm, summed, final_gain, final_shift)
    d_sum, final_gain_grad, final_shift_grad = norm_four(cotangent[0].astype(jnp.float32))
    d_sum_low = d_sum.astype(jnp.bfloat16)
    project_weight_grad = gradient_dot(activ_low, d_sum_low)
    project_bias_grad = jnp.sum(d_sum, axis=0)
    (d_pre,) = gelu_back(backward_dot(d_sum_low, project_weight))
    d_pre_low = d_pre.astype(jnp.bfloat16)
    expand_weight_grad = gradient_dot(d_pre_low, normed_low)
    expand_bias_grad = jnp.sum(d_pre, axis=0)
    d_merged_part, feed_gain_grad, feed_shift_grad = norm_three(
        forward_dot(d_pre_low, expand_weight)
    )
    d_merged = d_sum + d_merged_part
    d_merged_low = d_merged.astype(jnp.bfloat16)
    merge_weight_grad = gradient_dot(merge_in, d_merged_low)
    merge_bias_grad = jnp.sum(d_merged, axis=0)
    d_merge_in = backward_dot(d_merged_low, merge_weight)
    mix_gain_grad = jnp.zeros_like(mix_gain)
    mix_shift_grad = jnp.zeros_like(mix_shift)
    d_residuals = []
    d_pairs = []
    up_weight_grads = []
    up_bias_grads = []
    iso_weight_grads = []
    iso_bias_grads = []
    d_exts = []
    for branch in range(2):
        scale = scales[branch]
        step_count = step_counts[branch]
        lag = lags[branch]
        d_branch = d_merge_in[:, branch * channels : (branch + 1) * channels]
        d_res, gain_part_two, shift_part_two = norm_twos[branch](d_branch)
        (d_uppre,) = tanh_ups[branch](d_res)
        d_up_low = d_uppre.reshape(step_count, scale * channels).astype(jnp.bfloat16)
        up_weight_grads.append(gradient_dot(d_up_low, mixed_lows[branch]))
        up_bias_grads.append(jnp.sum(d_uppre, axis=0))
        d_pair, gain_part_one, shift_part_one = norm_ones[branch](
            forward_dot(d_up_low, up_weights[branch])
        )
        mix_gain_grad = mix_gain_grad + gain_part_one + gain_part_two
        mix_shift_grad = mix_shift_grad + shift_part_one + shift_part_two
        (d_iso,) = tanh_twos[branch](d_pair)
        d_iso_low = d_iso.astype(jnp.bfloat16)
        iso_weight_grads.append(gradient_dot(stacked_list[branch], d_iso_low))
        iso_bias_grads.append(jnp.sum(d_iso, axis=0))
        d_stacked = backward_dot(d_iso_low, iso_weights[branch])
        d_ext = jnp.zeros((step_count + lag, channels), jnp.float32)
        for position in range(tap_counts[branch]):
            tap_piece = jnp.where(
                tap_valids[branch][position],
                d_stacked[:, position * channels : (position + 1) * channels],
                0.0,
            )
            d_ext = d_ext + jnp.pad(tap_piece, ((position, lag - position), (0, 0)))
        d_residuals.append(d_res)
        d_pairs.append(d_pair)
        d_exts.append(d_ext)
    returned = passed_along(
        jnp.concatenate([d_exts[0][: lags[0]], d_exts[1][: lags[1]]], axis=0).astype(jnp.bfloat16),
        "tm",
        -1,
    ).astype(jnp.float32)
    returned_parts = (returned[: lags[0]], returned[lags[0] :])
    stride_weight_grads = []
    stride_bias_grads = []
    d_paddeds = []
    for branch in range(2):
        scale = scales[branch]
        step_count = step_counts[branch]
        lag = lags[branch]
        d_hidden = (
            d_pairs[branch]
            + d_exts[branch][lag:]
            + jnp.pad(returned_parts[branch], ((step_count - lag, 0), (0, 0)))
        )
        (d_conv,) = tanh_ones[branch](d_hidden)
        d_conv_low = d_conv.astype(jnp.bfloat16)
        stride_weight_grads.append(gradient_dot(windows_list[branch], d_conv_low))
        stride_bias_grads.append(jnp.sum(d_conv, axis=0))
        d_windows = backward_dot(d_conv_low, stride_weights[branch]).reshape(
            step_count, scale, channels
        )
        d_paddeds.append(
            jnp.where(keep_masks[branch][:, :, None], d_windows, 0.0).reshape(row_count, channels)
        )
    back_rims = passed_along(
        jnp.concatenate([d_paddeds[0][: halves[0]], d_paddeds[1][: halves[1]]], axis=0), "tm", -1
    )
    back_parts = (back_rims[: halves[0]], back_rims[halves[0] :])
    d_seasons = [
        d_residuals[branch]
        + jnp.concatenate([d_paddeds[branch][halves[branch] :], back_parts[branch]], axis=0)
        for branch in range(2)
    ]
    d_around = with_halo(
        jnp.stack(d_seasons).astype(jnp.bfloat16), (("tm", 1),), halo_width
    ).astype(jnp.float32)
    ext_places = base_row - halo_width + jnp.arange(row_count + 2 * halo_width, dtype=jnp.int32)
    ext_first, ext_last = series_bounds(lengths_row, ext_places)
    gradient_sum = jnp.zeros((row_count, channels), jnp.float32)
    for branch in range(2):
        adjoint = trend_adjoint(
            d_around[branch],
            places,
            series_first,
            series_last,
            ext_first,
            averages[branch],
            halo_width,
        )
        gradient_sum = gradient_sum + d_seasons[branch] - adjoint / averages[branch]
    input_grad = gradient_sum.astype(jnp.bfloat16)
    (
        stride_bias_twelve_grad,
        isometric_bias_twelve_grad,
        upsample_bias_twelve_grad,
        stride_bias_sixteen_grad,
        isometric_bias_sixteen_grad,
        upsample_bias_sixteen_grad,
        mix_gain_grad,
        mix_shift_grad,
        merge_bias_grad,
        feed_gain_grad,
        feed_shift_grad,
        expand_bias_grad,
        project_bias_grad,
        final_gain_grad,
        final_shift_grad,
    ) = lax.psum(
        (
            stride_bias_grads[0],
            iso_bias_grads[0],
            up_bias_grads[0],
            stride_bias_grads[1],
            iso_bias_grads[1],
            up_bias_grads[1],
            mix_gain_grad,
            mix_shift_grad,
            merge_bias_grad,
            feed_gain_grad,
            feed_shift_grad,
            expand_bias_grad,
            project_bias_grad,
            final_gain_grad,
            final_shift_grad,
        ),
        ("series", "tm"),
    )
    stride_local_twelve, stride_local_sixteen = stride_weight_grads
    iso_local_twelve, iso_local_sixteen = iso_weight_grads
    up_local_twelve, up_local_sixteen = up_weight_grads
    (
        row_stride_twelve,
        row_iso_twelve,
        row_up_twelve,
        row_stride_sixteen,
        row_iso_sixteen,
        row_up_sixteen,
        row_merge,
        row_expand,
        row_project,
    ) = (
        lax.psum_scatter(stride_local_twelve, "tm", scatter_dimension=0, tiled=True),
        lax.psum_scatter(iso_local_twelve, "tm", scatter_dimension=0, tiled=True),
        lax.psum_scatter(up_local_twelve, "tm", scatter_dimension=0, tiled=True),
        lax.psum_scatter(stride_local_sixteen, "tm", scatter_dimension=0, tiled=True),
        lax.psum_scatter(iso_local_sixteen, "tm", scatter_dimension=0, tiled=True),
        lax.psum_scatter(up_local_sixteen, "tm", scatter_dimension=0, tiled=True),
        lax.psum_scatter(merge_weight_grad, "tm", scatter_dimension=0, tiled=True),
        lax.psum_scatter(expand_weight_grad, "tm", scatter_dimension=0, tiled=True),
        lax.psum_scatter(project_weight_grad, "tm", scatter_dimension=0, tiled=True),
    )
    (
        stride_weight_twelve_grad,
        isometric_weight_twelve_grad,
        upsample_weight_twelve_grad,
        stride_weight_sixteen_grad,
        isometric_weight_sixteen_grad,
        upsample_weight_sixteen_grad,
        merge_weight_grad,
        expand_weight_grad,
        project_weight_grad,
    ) = (
        lax.psum(row_stride_twelve.astype(jnp.bfloat16), "series").astype(jnp.float32),
        lax.psum(row_iso_twelve.astype(jnp.bfloat16), "series").astype(jnp.float32),
        lax.psum(row_up_twelve.astype(jnp.bfloat16), "series").astype(jnp.float32),
        lax.psum(row_stride_sixteen.astype(jnp.bfloat16), "series").astype(jnp.float32),
        lax.psum(row_iso_sixteen.astype(jnp.bfloat16), "series").astype(jnp.float32),
        lax.psum(row_up_sixteen.astype(jnp.bfloat16), "series").astype(jnp.float32),
        lax.psum(row_merge.astype(jnp.bfloat16), "series").astype(jnp.float32),
        lax.psum(row_expand.astype(jnp.bfloat16), "series").astype(jnp.float32),
        lax.psum(row_project.astype(jnp.bfloat16), "series").astype(jnp.float32),
    )
    return (
        result.astype(jnp.bfloat16)[None],
        input_grad[None],
        stride_weight_twelve_grad,
        stride_bias_twelve_grad,
        isometric_weight_twelve_grad,
        isometric_bias_twelve_grad,
        upsample_weight_twelve_grad,
        upsample_bias_twelve_grad,
        stride_weight_sixteen_grad,
        stride_bias_sixteen_grad,
        isometric_weight_sixteen_grad,
        isometric_bias_sixteen_grad,
        upsample_weight_sixteen_grad,
        upsample_bias_sixteen_grad,
        mix_gain_grad,
        mix_shift_grad,
        merge_weight_grad,
        merge_bias_grad,
        feed_gain_grad,
        feed_shift_grad,
        expand_weight_grad,
        expand_bias_grad,
        project_weight_grad,
        project_bias_grad,
        final_gain_grad,
        final_shift_grad,
    )


def solution(mesh):
    placed = (
        P("series", "tm", None),
        P("series", None),
        P("tm", None),
        P(),
        P("tm", None),
        P(),
        P("tm", None),
        P(),
        P("tm", None),
        P(),
        P("tm", None),
        P(),
        P("tm", None),
        P(),
        P(),
        P(),
        P("tm", None),
        P(),
        P(),
        P(),
        P("tm", None),
        P(),
        P("tm", None),
        P(),
        P(),
        P(),
        P("series", "tm", None),
    )
    return jax.shard_map(
        on_device,
        mesh=mesh,
        in_specs=placed,
        out_specs=(
            P("series", "tm", None),
            P("series", "tm", None),
            P("tm", None),
            P(),
            P("tm", None),
            P(),
            P("tm", None),
            P(),
            P("tm", None),
            P(),
            P("tm", None),
            P(),
            P("tm", None),
            P(),
            P(),
            P(),
            P("tm", None),
            P(),
            P(),
            P(),
            P("tm", None),
            P(),
            P("tm", None),
            P(),
            P(),
            P(),
        ),
        check_vma=False,
    )
```

profile of v0, /device:TPU:0, one launch (start us, length us, event | category | flops | bytes accessed | tf_op | source)
XLA Modules:
  0.0 2722.7 jit_solution(5075263814316642880)
XLA Ops:
  59.6 6.2 fusion.200
  77.0 35.4 %all-gather.10.cloned.1.call-done = bf16[6144,512]{1,0:T(8,128)(2,1)} async-done(((bf16[768,512]{1,0:T(8,128)(2,1)}), bf16[6144,512]{1,0:T(8,128)(2,1)}) %all-gather.10.cloned.1.call-update) | async-done | bytes 6291472 | tf_op jit(solution)/shard_map/all_gather | solution.py:155
  116.4 121.2 %all-gather.12.cloned.1.call-done = bf16[8192,512]{1,0:T(8,128)(2,1)} async-done(((bf16[1024,512]{1,0:T(8,128)(2,1)}), bf16[8192,512]{1,0:T(8,128)(2,1)}) %all-gather.12.cloned.1.call-update) | async-done | bytes 8388624 | tf_op jit(solution)/shard_map/all_gather | solution.py:158
  247.7 115.2 %all-gather.14.cloned.1.call-done = bf16[8192,512]{1,0:T(8,128)(2,1)} async-done(((bf16[1024,512]{1,0:T(8,128)(2,1)}), bf16[8192,512]{1,0:T(8,128)(2,1)}) %all-gather.14.cloned.1.call-update) | async-done | bytes 8388624 | tf_op jit(solution)/shard_map/all_gather | solution.py:156
  362.9 5.7 fusion.196
  369.4 92.7 %all-gather.16.cloned.1.call-done = bf16[6144,512]{1,0:T(8,128)(2,1)} async-done(((bf16[768,512]{1,0:T(8,128)(2,1)}), bf16[6144,512]{1,0:T(8,128)(2,1)}) %all-gather.16.cloned.1.call-update) | async-done | bytes 6291472 | tf_op jit(solution)/shard_map/all_gather | solution.py:157
  468.4 93.0 %all-gather.18.cloned.1.call-done = bf16[6144,512]{1,0:T(8,128)(2,1)} async-done(((bf16[768,512]{1,0:T(8,128)(2,1)}), bf16[6144,512]{1,0:T(8,128)(2,1)}) %all-gather.18.cloned.1.call-update) | async-done | bytes 6291472 | tf_op jit(solution)/shard_map/all_gather | solution.py:159
  566.7 119.9 %all-gather.20.cloned.1.call-done = bf16[8192,512]{1,0:T(8,128)(2,1)} async-done(((bf16[1024,512]{1,0:T(8,128)(2,1)}), bf16[8192,512]{1,0:T(8,128)(2,1)}) %all-gather.20.cloned.1.call-update) | async-done | bytes 8388624 | tf_op jit(solution)/shard_map/all_gather | solution.py:160
  686.6 5.7 fusion.171
  694.8 32.4 %all-gather.22.cloned.1.call-done = bf16[1024,512]{1,0:T(8,128)(2,1)} async-done(((bf16[128,512]{1,0:T(8,128)(2,1)}), bf16[1024,512]{1,0:T(8,128)(2,1)}) %all-gather.22.cloned.1.call-update) | async-done | bytes 1048592 | tf_op jit(solution)/shard_map/all_gather | solution.py:161
  729.6 47.8 %all-gather.24.cloned.1.call-done = bf16[2048,512]{1,0:T(8,128)(2,1)} async-done(((bf16[256,512]{1,0:T(8,128)(2,1)}), bf16[2048,512]{1,0:T(8,128)(2,1)}) %all-gather.24.cloned.1.call-update) | async-done | bytes 2097168 | tf_op jit(solution)/shard_map/all_gather | solution.py:162
  777.4 11.5 multiply_convert_fusion
  788.9 38.4 %all-gather.26.cloned.1.call-done = bf16[2048,512]{1,0:T(8,128)(2,1)} async-done(((bf16[256,512]{1,0:T(8,128)(2,1)}), bf16[2048,512]{1,0:T(8,128)(2,1)}) %all-gather.26.cloned.1.call-update) | async-done | bytes 2097168 | tf_op jit(solution)/shard_map/all_gather | solution.py:163
  857.7 6.4 fusion.172
  871.2 6.4 fusion.151
  899.4 6.4 fusion.86
  906.8 8.2 fusion.144
  915.1 8.2 fusion.170
  924.9 8.3 fusion.85
  935.9 5.9 fusion.149
  952.0 46.6 %reduce-scatter.24.cloned.1.call-done = f32[256,512]{1,0:T(8,128)} async-done(((f32[2048,512]{1,0:T(8,128)}), f32[256,512]{1,0:T(8,128)}) %reduce-scatter.24.cloned.1.call-update) | async-done | bytes 524304 | tf_op jit(solution)/shard_map/reduce_scatter | solution.py:470
  1000.4 90.0 %reduce-scatter.26.cloned.1.call-done = f32[256,512]{1,0:T(8,128)} async-done(((f32[2048,512]{1,0:T(8,128)}), f32[256,512]{1,0:T(8,128)}) %reduce-scatter.26.cloned.1.call-update) | async-done | bytes 524304 | tf_op jit(solution)/shard_map/reduce_scatter | solution.py:471
  1092.1 208.8 %reduce-scatter.14.cloned.1.call-done = f32[768,512]{1,0:T(8,128)} async-done(((f32[6144,512]{1,0:T(8,128)}), f32[768,512]{1,0:T(8,128)}) %reduce-scatter.14.cloned.1.call-update) | async-done | bytes 1572880 | tf_op jit(solution)/shard_map/reduce_scatter | solution.py:465
  1303.3 207.6 %reduce-scatter.18.cloned.1.call-done = f32[768,512]{1,0:T(8,128)} async-done(((f32[6144,512]{1,0:T(8,128)}), f32[768,512]{1,0:T(8,128)}) %reduce-scatter.18.cloned.1.call-update) | async-done | bytes 1572880 | tf_op jit(solution)/shard_map/reduce_scatter | solution.py:467
  1513.3 207.5 %reduce-scatter.10.cloned.1.call-done = f32[768,512]{1,0:T(8,128)} async-done(((f32[6144,512]{1,0:T(8,128)}), f32[768,512]{1,0:T(8,128)}) %reduce-scatter.10.cloned.1.call-update) | async-done | bytes 1572880 | tf_op jit(solution)/shard_map/reduce_scatter | solution.py:463
  1723.2 283.1 %reduce-scatter.12.cloned.1.call-done = f32[1024,512]{1,0:T(8,128)} async-done(((f32[8192,512]{1,0:T(8,128)}), f32[1024,512]{1,0:T(8,128)}) %reduce-scatter.12.cloned.1.call-update) | async-done | bytes 2097168 | tf_op jit(solution)/shard_map/reduce_scatter | solution.py:464
  2008.9 283.1 %reduce-scatter.20.cloned.1.call-done = f32[1024,512]{1,0:T(8,128)} async-done(((f32[8192,512]{1,0:T(8,128)}), f32[1024,512]{1,0:T(8,128)}) %reduce-scatter.20.cloned.1.call-update) | async-done | bytes 2097168 | tf_op jit(solution)/shard_map/reduce_scatter | solution.py:468
  2294.7 282.8 %reduce-scatter.16.cloned.1.call-done = f32[1024,512]{1,0:T(8,128)} async-done(((f32[8192,512]{1,0:T(8,128)}), f32[1024,512]{1,0:T(8,128)}) %reduce-scatter.16.cloned.1.call-update) | async-done | bytes 2097168 | tf_op jit(solution)/shard_map/reduce_scatter | solution.py:466
  2590.4 5.5 collective-permute-start.6
  2596.5 42.8 %all-reduce.30 = (f32[512]{0:T(512)}, f32[512]{0:T(512)}, f32[512]{0:T(512)}, f32[512]{0:T(512)}, f32[512]{0:T(512)}, /*index=5*/f32[512]{0:T(512)}, f32[512]{0:...) all-reduce(f32[512]{0:T(512)} %get-tuple-element.80, ...), channel_id=1, replica_groups=mesh['series'=4,'tm'=8] {'series','tm'}, use_global_device_ids=true, to_apply=%region_31.33 | all-reduce | flops 9216 | bytes 73728 | tf_op jit(solution)/shard_map/psum | solution.py:429
  2640.6 8.4 fusion.81
  2649.0 52.9 %all-reduce.34.cloned.1.call-done = (bf16[768,512]{1,0:T(8,128)(2,1)}, bf16[1024,512]{1,0:T(8,128)(2,1)}, bf16[768,512]{1,0:T(8,128)(2,1)}, bf16[1024,512]{1,0:T...) async-done(((bf16[768,512]{1,0:T(8,128)(2,1)}, ...) | async-done | bytes 6160400 | tf_op jit(solution)/shard_map/psum | solution.py:484
  (697 shorter events, 211.8 us)
Async XLA Ops:
  7.2 105.1 %all-gather.10.cloned.1.call-start = ((), (), s32[]{:S(2)}) async-start(), calls=%async_computation.9 | async-start | bytes 7077888 | tf_op jit(solution)/shard_map/all_gather | solution.py:155
  8.0 229.7 %all-gather.12.cloned.1.call-start = ((), (), s32[]{:S(2)}) async-start(), calls=%async_computation.10 | async-start | bytes 9437184 | tf_op jit(solution)/shard_map/all_gather | solution.py:158
  8.7 354.2 %all-gather.14.cloned.1.call-start = ((), (), s32[]{:S(2)}) async-start(), calls=%async_computation.11 | async-start | bytes 9437184 | tf_op jit(solution)/shard_map/all_gather | solution.py:156
  9.4 452.7 %all-gather.16.cloned.1.call-start = ((), (), s32[]{:S(2)}) async-start(), calls=%async_computation.12 | async-start | bytes 7077888 | tf_op jit(solution)/shard_map/all_gather | solution.py:157
  10.0 551.5 %all-gather.18.cloned.1.call-start = ((), (), s32[]{:S(2)}) async-start(), calls=%async_computation.13 | async-start | bytes 7077888 | tf_op jit(solution)/shard_map/all_gather | solution.py:159
  10.6 676.0 %all-gather.20.cloned.1.call-start = ((), (), s32[]{:S(2)}) async-start(), calls=%async_computation.14 | async-start | bytes 9437184 | tf_op jit(solution)/shard_map/all_gather | solution.py:160
  11.2 716.0 %all-gather.22.cloned.1.call-start = ((), (), s32[]{:S(2)}) async-start(), calls=%async_computation.15 | async-start | bytes 1179648 | tf_op jit(solution)/shard_map/all_gather | solution.py:161
  11.9 765.4 %all-gather.24.cloned.1.call-start = ((), (), s32[]{:S(2)}) async-start(), calls=%async_computation.16 | async-start | bytes 2359296 | tf_op jit(solution)/shard_map/all_gather | solution.py:162
  12.7 814.6 %all-gather.26.cloned.1.call-start = ((), (), s32[]{:S(2)}) async-start(), calls=%async_computation.17 | async-start | bytes 2359296 | tf_op jit(solution)/shard_map/all_gather | solution.py:163
  12.7 10.4 collective-permute-start.1
  14.0 9.1 collective-permute-start
  19.6 930.8 %reduce-scatter.22.cloned.1.call-start = ((), (), s32[]{:S(2)}) async-start(), calls=%async_computation.24 | async-start | bytes 2359296 | tf_op jit(solution)/shard_map/reduce_scatter | solution.py:469
  22.5 224.9 %copy-start.122 = (pred[32]{0:T(512)(128)(4,1)}, pred[32]{0:T(512)(128)(4,1)S(1)}, u32[]{:S(2)}) copy-start(pred[32]{0:T(512)(128)(4,1)S(1)} %get-tuple-element.241) | copy-start | bytes 100
  22.5 225.0 %copy-start.120 = (pred[32]{0:T(512)(128)(4,1)}, pred[32]{0:T(512)(128)(4,1)S(1)}, u32[]{:S(2)}) copy-start(pred[32]{0:T(512)(128)(4,1)S(1)} %get-tuple-element.240) | copy-start | bytes 100
  22.5 225.1 %copy-start.118 = (pred[32]{0:T(512)(128)(4,1)}, pred[32]{0:T(512)(128)(4,1)S(1)}, u32[]{:S(2)}) copy-start(pred[32]{0:T(512)(128)(4,1)S(1)} %get-tuple-element.239) | copy-start | bytes 100
  69.7 6.4 collective-permute-start.2
  116.4 246.5 %copy-start.51 = (f32[32,512]{1,0:T(8,128)}, f32[32,512]{1,0:T(8,128)S(1)}, u32[]{:S(2)}) copy-start(f32[32,512]{1,0:T(8,128)S(1)} %get-tuple-element.268) | copy-start | bytes 196612
  242.4 319.1 %copy-start.53 = (f32[24,512]{1,0:T(8,128)}, f32[24,512]{1,0:T(8,128)S(1)}, u32[]{:S(2)}) copy-start(f32[24,512]{1,0:T(8,128)S(1)} %get-tuple-element.270) | copy-start | bytes 147460
  242.4 4.1 collective-permute-start.3
  841.3 157.3 %reduce-scatter.24.cloned.1.call-start = ((), (), s32[]{:S(2)}) async-start(), calls=%async_computation.25 | async-start | bytes 4718592 | tf_op jit(solution)/shard_map/reduce_scatter | solution.py:470
  846.2 244.1 %reduce-scatter.26.cloned.1.call-start = ((), (), s32[]{:S(2)}) async-start(), calls=%async_computation.26 | async-start | bytes 4718592 | tf_op jit(solution)/shard_map/reduce_scatter | solution.py:471
  851.7 449.2 %reduce-scatter.14.cloned.1.call-start = ((), (), s32[]{:S(2)}) async-start(), calls=%async_computation.20 | async-start | bytes 14155776 | tf_op jit(solution)/shard_map/reduce_scatter | solution.py:465
  864.2 646.6 %reduce-scatter.18.cloned.1.call-start = ((), (), s32[]{:S(2)}) async-start(), calls=%async_computation.22 | async-start | bytes 14155776 | tf_op jit(solution)/shard_map/reduce_scatter | solution.py:467
  877.8 843.0 %reduce-scatter.10.cloned.1.call-start = ((), (), s32[]{:S(2)}) async-start(), calls=%async_computation.18 | async-start | bytes 14155776 | tf_op jit(solution)/shard_map/reduce_scatter | solution.py:463
  892.7 6.0 collective-permute-start.4
  905.8 1100.4 %reduce-scatter.12.cloned.1.call-start = ((), (), s32[]{:S(2)}) async-start(), calls=%async_computation.19 | async-start | bytes 18874368 | tf_op jit(solution)/shard_map/reduce_scatter | solution.py:464
  915.1 1377.0 %reduce-scatter.20.cloned.1.call-start = ((), (), s32[]{:S(2)}) async-start(), calls=%async_computation.23 | async-start | bytes 18874368 | tf_op jit(solution)/shard_map/reduce_scatter | solution.py:468
  923.3 1654.2 %reduce-scatter.16.cloned.1.call-start = ((), (), s32[]{:S(2)}) async-start(), calls=%async_computation.21 | async-start | bytes 18874368 | tf_op jit(solution)/shard_map/reduce_scatter | solution.py:466
  933.2 1768.6 %all-reduce.34.cloned.1.call-start = ((), (), s32[]{:S(2)}) async-start(), calls=%async_computation.27 | async-start | bytes 12320768 | tf_op jit(solution)/shard_map/psum | solution.py:484
  2581.7 5.8 collective-permute-start.5
  2589.1 50.2 %collective-permute-start.7 = (bf16[2,8,512]{2,1,0:T(8,128)(2,1)}, bf16[2,8,512]{2,1,0:T(8,128)(2,1)}, u32[]{:S(2)}, u32[]{:S(2)}) collective-permute-start(bf16[2,8,512]{2,1,0:T(8,128)(2,1)} %get-tuple-element.171), channel_id=1, source_target_pairs={{1,0},{2,1},{3,2},{4,3},{5,4},{6,5},{7,6},{9,8},{10,9},{11,10},{12... | collective-permute-start | bytes 49160 | tf_op jit(solution)/shard_map/ppermute | solution.py:26
  2590.4 48.9 %collective-permute-start.6 = (bf16[2,8,512]{2,1,0:T(8,128)(2,1)}, bf16[2,8,512]{2,1,0:T(8,128)(2,1)}, u32[]{:S(2)}, u32[]{:S(2)}) collective-permute-start(bf16[2,8,512]{2,1,0:T(8,128)(2,1)} %get-tuple-element.170), channel_id=1, source_target_pairs={{0,1},{1,2},{2,3},{3,4},{4,5},{5,6},{6,7},{8,9},{9,10},{10,11},{11... | collective-permute-start | bytes 49160 | tf_op jit(solution)/shard_map/ppermute | solution.py:25
  (202 other events, 6202.2 us)
Sparse Core Ops, SparseCore 0:
  10.2 102.0 all-gather.9
  114.5 123.1 all-gather.11
  239.8 123.1 all-gather.13
  364.9 97.1 all-gather.15
  464.2 97.2 all-gather.17
  563.4 123.1 all-gather.19
  688.7 38.3 all-gather.21
  729.3 48.0 all-gather.23
  779.5 47.7 all-gather.25
  841.4 66.7 reduce-scatter.21
  911.8 86.7 reduce-scatter.23
  1002.5 87.8 reduce-scatter.25
  1093.9 206.9 reduce-scatter.13
  1304.3 206.4 reduce-scatter.17
  1514.3 206.4 reduce-scatter.9
  1724.4 281.7 reduce-scatter.11
  2010.4 281.6 reduce-scatter.19
  2295.7 281.7 reduce-scatter.15
  2582.5 119.3 all-reduce.33
where the time goes:
time: 2730 us; the launch traced here: 2720 us
  waiting for transfers between devices  2370 us (87%)
  matrix products  135 us (5%)
  other arithmetic  77.6 us (3%)
  local copies, waits for them, and re-layouts  51.7 us (2%)
  blocking collectives  42.8 us (2%)
    reduce_scatter x1, waiting for transfers between devices, on_device(): lax.psum_scatter(up_local_sixteen, 'tm', scatter_dimension=0, tiled=True)  283 us
    reduce_scatter x1, waiting for transfers between devices, on_device(): lax.psum_scatter(iso_local_twelve, 'tm', scatter_dimension=0, tiled=True)  283 us
    reduce_scatter x1, waiting for transfers between devices, on_device(): lax.psum_scatter(stride_local_sixteen, 'tm', scatter_dimension=0, tiled=T...  283 us
    reduce_scatter x1, waiting for transfers between devices, on_device(): lax.psum_scatter(up_local_twelve, 'tm', scatter_dimension=0, tiled=True)  209 us
    reduce_scatter x1, waiting for transfers between devices, on_device(): lax.psum_scatter(iso_local_sixteen, 'tm', scatter_dimension=0, tiled=True)  208 us
    reduce_scatter x1, waiting for transfers between devices, on_device(): lax.psum_scatter(stride_local_twelve, 'tm', scatter_dimension=0, tiled=True)  207 us
    all_gather x1, waiting for transfers between devices, on_device(): lax.all_gather(stride_weight_sixteen, 'tm', axis=0, tiled=True)  121 us
    all_gather x1, waiting for transfers between devices, on_device(): lax.all_gather(upsample_weight_sixteen, 'tm', axis=0, tiled=True)  120 us
  transfers between devices with their start and end apart: 27, of which 22 were waited for; matrix products, arithmetic and copies ran while one was open for 8% of the time, Pallas kernels for 0%

commit v1 on v0

v1 whole, which is shorter than its diff:
```python
import functools
import math

import jax
import jax.numpy as jnp
from jax import lax
from jax.experimental import pallas as pl
from jax.experimental.pallas import tpu as pltpu
from jax.sharding import PartitionSpec as P

SCALES = (12, 16)
AVERAGES = (13, 17)
TAPS = (16, 12)
UNIT = 48
EPSILON = 1e-05
HALO = 16
FFN_CHUNK = 512

BF = jnp.bfloat16
F32 = jnp.float32
I32 = jnp.int32


def dot(left, right):
    return lax.dot_general(left, right, (((1,), (0,)), ((), ())), preferred_element_type=F32)


def dot_nt(left, right):
    return lax.dot_general(left, right, (((1,), (1,)), ((), ())), preferred_element_type=F32)


def dot_tn(left, right):
    return lax.dot_general(left, right, (((0,), (0,)), ((), ())), preferred_element_type=F32)


def kernel_call(body, outs, args, mib, scalars=(), scratch=()):
    specs = [
        pl.BlockSpec(memory_space=pltpu.SMEM if i in scalars else pltpu.VMEM)
        for i in range(len(args))
    ]
    return pl.pallas_call(
        body,
        out_shape=[jax.ShapeDtypeStruct(shape, dtype) for shape, dtype in outs],
        in_specs=specs,
        out_specs=[pl.BlockSpec(memory_space=pltpu.VMEM) for _ in outs],
        scratch_shapes=list(scratch),
        compiler_params=pltpu.CompilerParams(vmem_limit_bytes=mib << 20),
    )(*args)


def tap_to_payload(x, scale, q, n):
    rows, channels = x.shape
    m, h = rows // scale, channels // q
    parts = [x[:, c * q : (c + 1) * q].reshape(scale, 1, m, q) for c in range(h)]
    whole = parts[0] if h == 1 else jnp.concatenate(parts, axis=1)
    return whole.reshape(n, scale * h * m // n, q)


def payload_to_tap(p, scale, channels):
    n, rows, q = p.shape
    h = channels // q
    m = n * rows // (scale * h)
    p = p.reshape(scale, h, m, q)
    parts = [p[:, c].reshape(scale * m, q) for c in range(h)]
    return parts[0] if h == 1 else jnp.concatenate(parts, axis=1)


def payload_units(p, m):
    n, rows, q = p.shape
    p = p.reshape(n, rows // m, m, q)
    return [p[:, i].reshape(n * m, q).astype(BF) for i in range(rows // m)]


def units_to_payload(units, n):
    parts = [u.reshape(n, u.shape[0] // n, u.shape[1]) for u in units]
    return parts[0] if len(parts) == 1 else jnp.concatenate(parts, axis=1)


def store_payload(refs, parts):
    if len(refs) == 1:
        low = parts[0].shape[1]
        refs[0][:, :low, :] = parts[0].astype(BF)
        refs[0][:, low:, :] = parts[1].astype(BF)
    else:
        for ref, part in zip(refs, parts):
            ref[...] = part.astype(BF)


def load_payload(refs, low):
    if len(refs) == 1:
        return [refs[0][:, :low, :].astype(F32), refs[0][:, low:, :].astype(F32)]
    return [ref[...].astype(F32) for ref in refs]


def split_steps(ref, counts):
    whole = ref[...].astype(F32)
    n, _, channels = whole.shape
    first = whole[:, : counts[0], :].reshape(n * counts[0], channels)
    return [first, whole[:, counts[0] :, :].reshape(n * counts[1], channels)]


def join_steps(parts, n):
    return jnp.concatenate([p.reshape(n, p.shape[0] // n, p.shape[1]) for p in parts], axis=1)


def norm_stats(v):
    mean = jnp.mean(v, axis=-1, keepdims=True)
    centered = v - mean
    rstd = lax.rsqrt(jnp.mean(centered * centered, axis=-1, keepdims=True) + EPSILON)
    return centered * rstd, rstd


def norm_back(d, gain, xhat, rstd):
    dg = d * gain
    mean_d = jnp.mean(dg, axis=-1, keepdims=True)
    mean_dx = jnp.mean(dg * xhat, axis=-1, keepdims=True)
    return rstd * (dg - mean_d - xhat * mean_dx)


def column_sum(v):
    return jnp.sum(v, axis=0, keepdims=True)


def average_counts(info, kernel, columns):
    place, first, last = info[:, 0:1], info[:, 1:2], info[:, 2:3]
    reach = kernel // 2
    column = lax.broadcasted_iota(I32, (info.shape[0], columns), 1)
    away = column - place
    inside = (jnp.abs(away) <= reach) & (column >= first) & (column <= last)
    counts = jnp.where(inside, 1, 0)
    counts = counts + jnp.where(column == first, jnp.maximum(reach - (place - first), 0), 0)
    counts = counts + jnp.where(column == last, jnp.maximum(reach - (last - place), 0), 0)
    return counts, away == 0


def season_matrix(info, kernel, columns):
    counts, own = average_counts(info, kernel, columns)
    values = jnp.where(own, kernel, 0) - counts
    values = jnp.where(info[:, 0:1] >= info[:, 1:2], values, 0)
    return values.astype(F32).astype(BF)


def token_order(rows, scale):
    m = rows // scale
    place = lax.broadcasted_iota(I32, (rows, rows), 0)
    column = lax.broadcasted_iota(I32, (rows, rows), 1)
    tap = jnp.zeros_like(column)
    for k in range(1, scale):
        tap = tap + jnp.where(column >= k * m, 1, 0)
    return jnp.where(place == scale * (column - tap * m) + tap, 1.0, 0.0).astype(BF)


def windows_body(geo, tok, left, right, info_one, info_two, *outs):
    x = jnp.concatenate([left[...], tok[...], right[...]], axis=0)
    parts = []
    for b, info in enumerate((info_one, info_two)):
        matrix = season_matrix(info[...], AVERAGES[b], x.shape[0])
        parts.append(dot(matrix, x) * (1.0 / AVERAGES[b]))
    if geo["aligned"]:
        parts = [tap_to_payload(p, SCALES[b], geo["q"][b], geo["n"]) for b, p in enumerate(parts)]
        store_payload(outs, parts)
    else:
        for out, part in zip(outs, parts):
            out[...] = part.astype(BF)


def season_body(tok, left, right, info, out):
    x = jnp.concatenate([left[...], tok[...], right[...]], axis=0)
    wide = tok[...].astype(F32)
    for b in range(2):
        counts, _ = average_counts(info[...], AVERAGES[b], x.shape[0])
        out[b] = wide - dot(counts.astype(F32).astype(BF), x) * (1.0 / AVERAGES[b])


def slab_in_body(geo, transposed, *refs):
    pays, weights, out = refs[: geo["pays"]], refs[-3:-1], refs[-1]
    parts = []
    for b, p in enumerate(load_payload(pays, geo["pay_rows"][0])):
        total = None
        q = geo["q"][b]
        for i, unit in enumerate(payload_units(p, geo["m"][b])):
            term = dot(unit, weights[b][i * q : (i + 1) * q, :])
            total = term if total is None else total + term
        parts.append(total)
    out[...] = join_steps(parts, geo["n"]).astype(BF)


def slab_out_body(geo, steps, weight_one, weight_two, *outs):
    parts = []
    for b, (x, weight) in enumerate(zip(split_steps(steps, geo["m"]), (weight_one, weight_two))):
        q = geo["q"][b]
        low = x.astype(BF)
        units = [
            dot_nt(low, weight[i * q : (i + 1) * q, :]) for i in range(weight.shape[0] // q)
        ]
        parts.append(units_to_payload(units, geo["n"]))
    store_payload(outs, parts)


def slab_grad_body(geo, *refs):
    pays, steps, outs = refs[: geo["pays"]], refs[geo["pays"]], refs[-2:]
    step_parts = split_steps(steps, geo["m"])
    for b, p in enumerate(load_payload(pays, geo["pay_rows"][0])):
        q = geo["q"][b]
        right = step_parts[b].astype(BF)
        for i, unit in enumerate(payload_units(p, geo["m"][b])):
            outs[b][i * q : (i + 1) * q, :] = dot_tn(unit, right).astype(BF)


def tap_inputs(geo, b, shifts, hidden, start):
    count = hidden.shape[0]
    step = lax.broadcasted_iota(I32, (count, 1), 0)
    pieces = []
    for i in range(geo["touched"][b]):
        shift = jnp.maximum(shifts[b] - i, 0)
        moved = pltpu.roll(hidden, shift, 0)
        pieces.append(jnp.where(step - shift >= start, moved, 0.0).astype(BF))
    return pieces


def iso_body(geo, shifts, steps, start_one, start_two, weight_one, weight_two, out):
    parts = []
    hiddens = split_steps(steps, geo["m"])
    for b, (start, weight) in enumerate(((start_one, weight_one), (start_two, weight_two))):
        total = None
        channels = hiddens[b].shape[1]
        for i, piece in enumerate(tap_inputs(geo, b, shifts, hiddens[b], start[...])):
            term = dot(piece, weight[i * channels : (i + 1) * channels, :])
            total = term if total is None else total + term
        parts.append(total)
    out[...] = join_steps(parts, geo["n"]).astype(BF)


def iso_back_body(geo, shifts, d_iso, start_one, start_two, weight_one, weight_two, out):
    parts = []
    for b, (d, start, weight) in enumerate(
        zip(split_steps(d_iso, geo["m"]), (start_one, start_two), (weight_one, weight_two))
    ):
        count, channels = d.shape
        low = d.astype(BF)
        step = lax.broadcasted_iota(I32, (count, 1), 0)
        total = None
        for i in range(geo["touched"][b]):
            shift = jnp.maximum(shifts[b] - i, 0)
            stacked = dot_nt(low, weight[i * channels : (i + 1) * channels, :])
            stacked = jnp.where(step - shift >= start[...], stacked, 0.0)
            moved = pltpu.roll(stacked, lax.rem(count - shift, count), 0)
            total = moved if total is None else total + moved
        parts.append(total)
    out[...] = join_steps(parts, geo["n"]).astype(BF)


def iso_grad_body(geo, shifts, steps, d_iso, start_one, start_two, out_one, out_two):
    hiddens, ds = split_steps(steps, geo["m"]), split_steps(d_iso, geo["m"])
    for b, (start, out) in enumerate(((start_one, out_one), (start_two, out_two))):
        channels = hiddens[b].shape[1]
        right = ds[b].astype(BF)
        for i, piece in enumerate(tap_inputs(geo, b, shifts, hiddens[b], start[...])):
            out[i * channels : (i + 1) * channels, :] = dot_tn(piece, right).astype(BF)


def branch_rows(pair, counts):
    total = sum(counts)
    step = lax.broadcasted_iota(I32, (total, 1), 0)
    return jnp.where(step < counts[0], pair[0:1, :], pair[1:2, :])


def hidden_one_body(geo, parts, bias, hidden, low):
    value = jnp.tanh(jnp.sum(parts[...].astype(F32), axis=0) + branch_rows(bias, geo["m"]))
    hidden[...] = value
    low[...] = value.astype(BF)


def mix_body(geo, parts, bias, hidden_one, gain, shift, hidden, mixed):
    value = jnp.tanh(jnp.sum(parts[...].astype(F32), axis=0) + branch_rows(bias, geo["m"]))
    hidden[...] = value
    xhat, _ = norm_stats(value + hidden_one[...])
    mixed[...] = (xhat * gain[...] + shift[...]).astype(BF)


def mix_back_body(geo, parts, hidden_one, hidden_two, gain, d_pair, d_iso, sums):
    d = jnp.sum(parts[...].astype(F32), axis=0)
    two = hidden_two[...]
    xhat, rstd = norm_stats(two + hidden_one[...])
    pair = norm_back(d, gain[...], xhat, rstd)
    iso = (1.0 - two * two) * pair
    d_pair[...] = pair
    d_iso[...] = iso.astype(BF)
    low = geo["m"][0]
    sums[0:1, :] = column_sum(d * xhat)
    sums[1:2, :] = column_sum(d)
    sums[2:3, :] = column_sum(iso[:low])
    sums[3:4, :] = column_sum(iso[low:])


def conv_back_body(geo, parts, d_pair, hidden_one, d_conv, sums):
    one = hidden_one[...]
    d = (jnp.sum(parts[...].astype(F32), axis=0) + d_pair[...]) * (1.0 - one * one)
    d_conv[...] = d.astype(BF)
    low = geo["m"][0]
    sums[0:1, :] = column_sum(d[:low])
    sums[1:2, :] = column_sum(d[low:])


def head_body(geo, *refs):
    pays = refs[: geo["taps"]]
    (
        season, cotangent, up_bias, mix_gain, mix_shift, merge_weight, merge_bias, feed_gain, feed_shift,
        expand_weight, expand_bias, project_weight, project_bias, final_gain, final_shift,
    ) = refs[geo["taps"] : geo["taps"] + 15]
    outs = refs[geo["taps"] + 15 :]
    d_pays, outs = outs[: geo["taps"]], outs[geo["taps"] :]
    (
        result, d_res_out, merge_in, normed_out, activ_out, d_sum_out, d_pre_out, d_merged_out, sums, expand_sums,
        slope,
    ) = outs
    rows, channels = cotangent.shape
    width = FFN_CHUNK
    chunks = expand_weight.shape[0] // width
    if geo["aligned"]:
        taps = [
            payload_to_tap(p, SCALES[b], channels)
            for b, p in enumerate(load_payload(pays, geo["pay_rows"][0]))
        ]
    else:
        taps = [p[...] for p in pays]
    ups, kept = [], []
    for b in range(2):
        order = token_order(rows, SCALES[b])
        up = jnp.tanh(dot(order, taps[b].astype(BF)) + up_bias[b : b + 1, :])
        xhat, rstd = norm_stats(up + season[b])
        ups.append(up)
        kept.append((xhat, rstd))
        merge_in[:, b * channels : (b + 1) * channels] = (
            xhat * mix_gain[...] + mix_shift[...]
        ).astype(BF)
    merged = dot(merge_in[...], merge_weight[...]) + merge_bias[...]
    feed_hat, feed_rstd = norm_stats(merged)
    normed_out[...] = (feed_hat * feed_gain[...] + feed_shift[...]).astype(BF)

    def forward_chunk(c, total):
        at = pl.ds(pl.multiple_of(c * width, width), width)
        pre = dot_nt(normed_out[...], expand_weight[at, :]) + expand_bias[:, at]
        half = 0.5 + 0.5 * lax.erf(pre * math.sqrt(0.5))
        slope[c] = half + pre * (jnp.exp(-0.5 * pre * pre) * (1.0 / math.sqrt(2.0 * math.pi)))
        activ_out[:, at] = (pre * half).astype(BF)
        return total + dot(activ_out[:, at], project_weight[at, :])

    summed = lax.fori_loop(0, chunks, forward_chunk, merged + project_bias[...])
    final_hat, final_rstd = norm_stats(summed)
    result[...] = (final_hat * final_gain[...] + final_shift[...]).astype(BF)

    d_out = cotangent[...].astype(F32)
    sums[0:1, :] = column_sum(d_out * final_hat)
    sums[1:2, :] = column_sum(d_out)
    d_sum = norm_back(d_out, final_gain[...], final_hat, final_rstd)
    sums[2:3, :] = column_sum(d_sum)
    d_sum_out[...] = d_sum.astype(BF)

    def backward_chunk(c, total):
        at = pl.ds(pl.multiple_of(c * width, width), width)
        d_pre = slope[c] * dot_nt(d_sum_out[...], project_weight[at, :])
        expand_sums[:, at] = column_sum(d_pre)
        d_pre_out[:, at] = d_pre.astype(BF)
        return total + dot(d_pre_out[:, at], expand_weight[at, :])

    d_normed = lax.fori_loop(0, chunks, backward_chunk, jnp.zeros((rows, channels), F32))
    sums[3:4, :] = column_sum(d_normed * feed_hat)
    sums[4:5, :] = column_sum(d_normed)
    d_merged = d_sum + norm_back(d_normed, feed_gain[...], feed_hat, feed_rstd)
    sums[5:6, :] = column_sum(d_merged)
    d_merged_out[...] = d_merged.astype(BF)
    gain_sum, shift_sum = 0.0, 0.0
    d_taps = []
    for b in range(2):
        d = dot_nt(d_merged_out[...], merge_weight[b * channels : (b + 1) * channels, :])
        xhat, rstd = kept[b]
        gain_sum = gain_sum + column_sum(d * xhat)
        shift_sum = shift_sum + column_sum(d)
        d_res = norm_back(d, mix_gain[...], xhat, rstd)
        d_res_out[b] = d_res
        d_up = (1.0 - ups[b] * ups[b]) * d_res
        sums[8 + b : 9 + b, :] = column_sum(d_up)
        d_taps.append(dot_tn(token_order(rows, SCALES[b]), d_up.astype(BF)))
    sums[6:7, :] = gain_sum
    sums[7:8, :] = shift_sum
    if geo["aligned"]:
        d_taps = [tap_to_payload(d, SCALES[b], geo["q"][b], geo["n"]) for b, d in enumerate(d_taps)]
        store_payload(d_pays, d_taps)
    else:
        for out, part in zip(d_pays, d_taps):
            out[...] = part.astype(BF)


def head_grad_body(merge_in, normed, activ, d_sum, d_pre, d_merged, out):
    n = out.shape[0]
    at = 0
    for left, right in ((merge_in, d_merged), (d_pre, normed), (activ, d_sum)):
        grad = dot_tn(left[...], right[...]).astype(BF)
        size = grad.shape[0] // n
        out[:, at : at + size, :] = grad.reshape(n, size, grad.shape[1])
        at += size


def residual_body(d_res, info, out):
    rows = d_res.shape[1]
    columns = rows + 2 * HALO
    total = jnp.zeros((columns, d_res.shape[2]), F32)
    for b in range(2):
        counts, _ = average_counts(info[...], AVERAGES[b], columns)
        adjoint = dot_tn(counts.astype(F32).astype(BF), d_res[b].astype(BF))
        total = total - adjoint * (1.0 / AVERAGES[b])
    out[0:HALO, :] = total[0:HALO]
    out[HALO : HALO + rows, :] = total[HALO : HALO + rows] + d_res[0] + d_res[1]
    out[HALO + rows :, :] = total[HALO + rows :]


def input_back_body(geo, *refs):
    pays = refs[: geo["taps"]]
    info_one, info_two, residual, own, left, right = refs[geo["taps"] :]
    columns, channels = residual.shape
    rows = columns - 2 * HALO
    if geo["aligned"]:
        taps = [
            payload_to_tap(p, SCALES[b], channels)
            for b, p in enumerate(load_payload(pays, geo["pay_rows"][0]))
        ]
    else:
        taps = [p[...] for p in pays]
    total = residual[...]
    for b, info in enumerate((info_one, info_two)):
        matrix = season_matrix(info[...], AVERAGES[b], columns)
        total = total + dot_tn(matrix, taps[b].astype(BF)) * (1.0 / AVERAGES[b])
    left[...] = total[0:HALO]
    own[...] = total[HALO : HALO + rows]
    right[...] = total[HALO + rows :]


def swap(x):
    return lax.all_to_all(x, "tm", 0, 0)


def to_all(x):
    n = lax.axis_size("tm")
    return lax.all_to_all(jnp.broadcast_to(x[None], (n,) + x.shape), "tm", 0, 0)


def neighbours(n):
    up = [(i, i + 1) for i in range(n - 1)]
    return up, [(j, i) for i, j in up]


def on_device(
    inputs, lengths,
    stride_weight_twelve, stride_bias_twelve, isometric_weight_twelve, isometric_bias_twelve,
    upsample_weight_twelve, upsample_bias_twelve,
    stride_weight_sixteen, stride_bias_sixteen, isometric_weight_sixteen, isometric_bias_sixteen,
    upsample_weight_sixteen, upsample_bias_sixteen,
    mix_gain, mix_shift, merge_weight, merge_bias, feed_gain, feed_shift,
    expand_weight, expand_bias, project_weight, project_bias, final_gain, final_shift, cotangent,
):
    n = lax.axis_size("tm")
    me = lax.axis_index("tm")
    rows, channels = inputs.shape[1:]
    stride_weights = (stride_weight_twelve, stride_weight_sixteen)
    iso_weights = (isometric_weight_twelve, isometric_weight_sixteen)
    up_weights = (upsample_weight_twelve, upsample_weight_sixteen)
    m = [rows // s for s in SCALES]
    slab = [w.shape[0] for w in stride_weights]
    q = [math.gcd(*slab, channels)] * 2
    pay_rows = [slab[b] // q[b] * m[b] for b in range(2)]
    combined = q[0] == q[1]
    iso_slab = [w.shape[0] for w in iso_weights]
    iso_q = [math.gcd(r, channels) for r in iso_slab]
    touched = [-(-(iso_slab[b] + channels - iso_q[b]) // channels) for b in range(2)]
    geo = {
        "n": n, "m": m, "q": q, "pay_rows": pay_rows, "pays": 1 if combined else 2,
        "aligned": combined and q[0] % 128 == 0, "touched": touched,
    }
    if combined:
        pay_outs = [((n, sum(pay_rows), q[0]), BF)]
    else:
        pay_outs = [((n, pay_rows[b], q[b]), BF) for b in range(2)]
    tap_outs = pay_outs if geo["aligned"] else [((rows, channels), BF)] * 2
    geo["taps"] = len(tap_outs)

    def as_payload(parts):
        if geo["aligned"]:
            return parts
        parts = [tap_to_payload(p, SCALES[b], q[b], n) for b, p in enumerate(parts)]
        return [jnp.concatenate(parts, axis=1)] if combined else parts

    def as_taps(parts):
        if geo["aligned"]:
            return parts
        if combined:
            parts = [parts[0][:, : pay_rows[0]], parts[0][:, pay_rows[0] :]]
        return [payload_to_tap(p, SCALES[b], channels) for b, p in enumerate(parts)]

    lengths_row = lengths[0]
    count = lengths_row.shape[0]
    upto = jnp.arange(count)[None, :] <= jnp.arange(count)[:, None]
    ends = UNIT * jnp.sum(jnp.where(upto, lengths_row[None, :], 0), axis=1)
    starts = ends - UNIT * lengths_row

    def bounds(places):
        inside = (starts[None, :] <= places[:, None]) & (places[:, None] < ends[None, :])
        first = jnp.sum(jnp.where(inside, starts[None, :], 0), axis=1)
        return first, jnp.sum(jnp.where(inside, ends[None, :], 0), axis=1)

    base = me * rows
    local = jnp.arange(rows, dtype=I32)

    def info_of(places, anchors):
        first, last = bounds(anchors + base)
        shift = base - HALO
        return jnp.stack([places + HALO, first - shift, last - 1 - shift], axis=1)

    token_info = info_of(local, local)
    window_infos, step_starts = [], []
    for b in range(2):
        tap, step = local // m[b], local % m[b]
        anchor = SCALES[b] * step
        window_infos.append(info_of(anchor - SCALES[b] // 2 + tap, anchor))
        all_steps = jnp.arange(n * m[b], dtype=I32)
        step_starts.append((bounds(SCALES[b] * all_steps)[0] // SCALES[b])[:, None])

    head_rows = [w.shape[0] for w in (merge_weight, expand_weight, project_weight)]
    head_all = lax.all_gather(
        jnp.concatenate([merge_weight, expand_weight, project_weight], axis=0), "tm", axis=0
    )
    head_parts, at = [], 0
    for size in head_rows:
        head_parts.append(head_all[:, at : at + size].reshape(n * size, channels))
        at += size
    merge_all, expand_all, project_all = head_parts

    iso_first = [(iso_slab[b] * me) // channels for b in range(2)]
    iso_offset = [iso_slab[b] * me - iso_first[b] * channels for b in range(2)]
    iso_wide = []
    for b in range(2):
        if touched[b] * channels == iso_slab[b]:
            iso_wide.append(iso_weights[b])
        else:
            blank = jnp.zeros((touched[b] * channels, channels), BF)
            iso_wide.append(lax.dynamic_update_slice(blank, iso_weights[b], (iso_offset[b], 0)))
    shifts = jnp.stack([TAPS[b] - 1 - iso_first[b] for b in range(2)]).astype(I32)

    def row(v):
        return v[None, :]

    up_route, down_route = neighbours(n)
    tokens = inputs[0]
    left = lax.ppermute(tokens[rows - HALO :], "tm", up_route)
    right = lax.ppermute(tokens[:HALO], "tm", down_route)
    windows = kernel_call(
        functools.partial(windows_body, geo), tap_outs, (tokens, left, right, *window_infos), 24
    )
    windows = [swap(w) for w in as_payload(windows)]
    (season,) = kernel_call(
        season_body, [((2, rows, channels), F32)], (tokens, left, right, token_info), 24
    )
    step_block = [((n, sum(m), channels), BF)]
    own_steps = (sum(m), channels)
    (partial,) = kernel_call(
        functools.partial(slab_in_body, geo, False), step_block, (*windows, *stride_weights), 24
    )
    hidden_one, hidden_low = kernel_call(
        functools.partial(hidden_one_body, geo),
        [(own_steps, F32), (own_steps, BF)],
        (swap(partial), jnp.stack([stride_bias_twelve, stride_bias_sixteen])),
        8,
    )
    hidden_all = to_all(hidden_low)
    (partial,) = kernel_call(
        functools.partial(iso_body, geo),
        step_block,
        (shifts, hidden_all, *step_starts, *iso_wide),
        32,
        scalars=(0,),
    )
    hidden_two, mixed_low = kernel_call(
        functools.partial(mix_body, geo),
        [(own_steps, F32), (own_steps, BF)],
        (
            swap(partial),
            jnp.stack([isometric_bias_twelve, isometric_bias_sixteen]),
            hidden_one,
            row(mix_gain),
            row(mix_shift),
        ),
        8,
    )
    mixed_all = to_all(mixed_low)
    ups = kernel_call(
        functools.partial(slab_out_body, geo), pay_outs, (mixed_all, *up_weights), 24
    )
    ups = as_taps([swap(u) for u in ups])
    hidden_units = expand_all.shape[0]
    head = kernel_call(
        functools.partial(head_body, geo),
        [
            *tap_outs,
            ((rows, channels), BF),
            ((2, rows, channels), F32),
            ((rows, 2 * channels), BF),
            ((rows, channels), BF),
            ((rows, hidden_units), BF),
            ((rows, channels), BF),
            ((rows, hidden_units), BF),
            ((rows, channels), BF),
            ((10, channels), F32),
            ((1, hidden_units), F32),
        ],
        (
            *ups, season, cotangent[0], jnp.stack([upsample_bias_twelve, upsample_bias_sixteen]),
            row(mix_gain), row(mix_shift), merge_all, row(merge_bias), row(feed_gain), row(feed_shift),
            expand_all, row(expand_bias), project_all, row(project_bias), row(final_gain), row(final_shift),
        ),
        48,
        scratch=[pltpu.VMEM((hidden_units // FFN_CHUNK, rows, FFN_CHUNK), F32)],
    )
    d_ups, head = head[: len(tap_outs)], head[len(tap_outs) :]
    result, d_res, merge_in, normed_low, activ_low, d_sum_low, d_pre_low, d_merged_low, head_sums, expand_sums = head

    d_ups = [swap(d) for d in as_payload(d_ups)]
    (head_grad,) = kernel_call(
        head_grad_body,
        [((n, sum(head_rows), channels), BF)],
        (merge_in, normed_low, activ_low, d_sum_low, d_pre_low, d_merged_low),
        32,
    )
    head_grad = lax.psum_scatter(head_grad, "tm", scatter_dimension=0)
    head_grad = lax.psum(head_grad, "series").astype(F32)
    (residual,) = kernel_call(
        residual_body, [((rows + 2 * HALO, channels), F32)], (d_res, token_info), 24
    )
    (partial,) = kernel_call(
        functools.partial(slab_in_body, geo, True), step_block, (*d_ups, *up_weights), 24
    )
    d_pair, d_iso, mix_sums = kernel_call(
        functools.partial(mix_back_body, geo),
        [(own_steps, F32), (own_steps, BF), ((4, channels), F32)],
        (swap(partial), hidden_one, hidden_two, row(mix_gain)),
        8,
    )
    slab_outs = [((slab[b], channels), BF) for b in range(2)]
    up_grads = kernel_call(
        functools.partial(slab_grad_body, geo), slab_outs, (*d_ups, mixed_all), 24
    )
    d_iso_all = to_all(d_iso)
    (partial,) = kernel_call(
        functools.partial(iso_back_body, geo),
        step_block,
        (shifts, d_iso_all, *step_starts, *iso_wide),
        32,
        scalars=(0,),
    )
    d_conv, conv_sums = kernel_call(
        functools.partial(conv_back_body, geo),
        [(own_steps, BF), ((2, channels), F32)],
        (swap(partial), d_pair, hidden_one),
        8,
    )
    iso_grads = kernel_call(
        functools.partial(iso_grad_body, geo),
        [((touched[b] * channels, channels), BF) for b in range(2)],
        (shifts, hidden_all, d_iso_all, *step_starts),
        32,
        scalars=(0,),
    )
    iso_grads = [
        g
        if g.shape[0] == iso_slab[b]
        else lax.dynamic_slice(g, (iso_offset[b], 0), (iso_slab[b], channels))
        for b, g in enumerate(iso_grads)
    ]
    d_conv_all = to_all(d_conv)
    d_windows = kernel_call(
        functools.partial(slab_out_body, geo), pay_outs, (d_conv_all, *stride_weights), 24
    )
    d_windows = as_taps([swap(d) for d in d_windows])
    stride_grads = kernel_call(
        functools.partial(slab_grad_body, geo), slab_outs, (*windows, d_conv_all), 24
    )
    edge = ((HALO, channels), F32)
    own, to_left, to_right = kernel_call(
        functools.partial(input_back_body, geo),
        [((rows, channels), F32), edge, edge],
        (*d_windows, *window_infos, residual),
        24,
    )
    from_right = lax.ppermute(to_left, "tm", down_route)
    from_left = lax.ppermute(to_right, "tm", up_route)
    input_grad = jnp.concatenate(
        [own[:HALO] + from_left, own[HALO : rows - HALO], own[rows - HALO :] + from_right], axis=0
    ).astype(BF)

    sums = lax.psum(
        jnp.concatenate([conv_sums, mix_sums, head_sums, expand_sums.reshape(-1, channels)], axis=0),
        ("series", "tm"),
    )
    up_grads = [lax.psum(g, "series").astype(F32) for g in up_grads]
    iso_grads = [lax.psum(g, "series").astype(F32) for g in iso_grads]
    stride_grads = [lax.psum(g, "series").astype(F32) for g in stride_grads]
    head_grads, at = [], 0
    for size in head_rows:
        head_grads.append(head_grad[at : at + size])
        at += size
    return (
        result[None],
        input_grad[None],
        stride_grads[0], sums[0], iso_grads[0], sums[4], up_grads[0], sums[14],
        stride_grads[1], sums[1], iso_grads[1], sums[5], up_grads[1], sums[15],
        sums[2] + sums[12], sums[3] + sums[13],
        head_grads[0], sums[11], sums[9], sums[10],
        head_grads[1], sums[16:].reshape(-1), head_grads[2], sums[8], sums[6], sums[7],
    )


def solution(mesh):
    tokens, weight, whole = P("series", "tm", None), P("tm", None), P()
    pair = (weight, whole)
    return jax.shard_map(
        on_device,
        mesh=mesh,
        in_specs=(
            tokens, P("series", None), *(pair * 6), whole, whole, *pair, whole, whole, *pair, *pair, whole, whole,
            tokens,
        ),
        out_specs=(tokens, tokens, *(pair * 6), whole, whole, *pair, whole, whole, *pair, *pair, whole, whole),
        check_vma=False,
    )
```

time: 2730 us -> 502 us (0.18)
  waiting for transfers between devices: 2370 us -> 192 us
  matrix products: 135 us -> 0 us
  blocking collectives: 42.8 us -> 158 us
  other arithmetic: 77.6 us -> 16.2 us
  Pallas kernels: 0 us -> 42.8 us
    reduce_scatter x9 -> x1, waiting for transfers between devices: 1610 us -> 11.6 us  [on_device(): head_grad = lax.psum_scatter(head_grad, 'tm', scatter_dimension=0)]
    all_gather x9 -> x1, waiting for transfers between devices: 696 us -> 0.01 us  [on_device(): lax.all_gather(jnp.concatenate([merge_weight, expand_weight, project_weig...]
    dot_general x27 -> x0, matrix products: 135 us -> none  [the longest x9 55.5 us: gradient_dot(): lax.dot_general(left, right, (((0,), (0,)), ((), ())), preferred_element_...]
    all_to_all x0 -> x7, waiting for transfers between devices: none -> 119 us  [the longest x5 83 us: swap(): return lax.all_to_all(x, 'tm', 0, 0)]
    all_to_all x0 -> x5, blocking collectives: none -> 114 us  [the longest x3 84.4 us: swap(): return lax.all_to_all(x, 'tm', 0, 0)]
    pallas_call x0 -> x19, Pallas kernels: none -> 42.8 us  [kernel_call(): pl.pallas_call(body, out_shape=[jax.ShapeDtypeStruct(shape, dtype) for sh...]
    convert_element_type x23 -> x6, other arithmetic: 46.2 us -> 8.91 us  [the longest x2 2.97 us: on_device(): iso_grads = [lax.psum(g, 'series').astype(F32) for g in iso_grads]]
    gather x17 -> x0, local copies, waits for them, and re-layouts: 36.2 us -> none  [trend_of(): total = total + jnp.take(extended, gather_index, axis=0)]
  transfers between devices with their start and end apart: 27 -> 14, of which waited for: 22 -> 11; matrix products, arithmetic and copies ran while one was open for 8% -> 3% of each run, Pallas kernels for 0% -> 5%
where the time goes in v1:
time: 502 us; the launch traced here: 500 us
  waiting for transfers between devices  192 us (38%)
  blocking collectives  158 us (31%)
  Pallas kernels  42.8 us (9%)
  starting transfers between devices  40.5 us (8%)
  local copies, waits for them, and re-layouts  35.9 us (7%)
  other arithmetic  16.2 us (3%)
  between operations  14.7 us (3%)
    all_to_all x3, blocking collectives, swap(): return lax.all_to_all(x, 'tm', 0, 0)  84.4 us
    all_to_all x5, waiting for transfers between devices, swap(): return lax.all_to_all(x, 'tm', 0, 0)  83 us
    psum x1, waiting for transfers between devices, on_device(): stride_grads = [lax.psum(g, 'series').astype(F32) for g in stride_grads]  52.8 us
    psum x1, blocking collectives, on_device(): lax.psum(jnp.concatenate([conv_sums, mix_sums, head_sums, expand_sums.res...  44 us
    pallas_call x19, Pallas kernels, kernel_call(): pl.pallas_call(body, out_shape=[jax.ShapeDtypeStruct(shape, dtype) for sh...  42.8 us
    all_to_all x2, waiting for transfers between devices, to_all(): return lax.all_to_all(jnp.broadcast_to(x[None], (n,) + x.shape), 'tm', 0, 0)  36.2 us
    all_to_all x2, blocking collectives, to_all(): return lax.all_to_all(jnp.broadcast_to(x[None], (n,) + x.shape), 'tm', 0, 0)  30 us
    all_to_all x5, starting transfers between devices, swap(): return lax.all_to_all(x, 'tm', 0, 0)  21.8 us
  transfers between devices with their start and end apart: 14, of which 11 were waited for; matrix products, arithmetic and copies ran while one was open for 3% of the time, Pallas kernels for 5%

profile of v1, /device:TPU:0, one launch (start us, length us, event | category | flops | bytes accessed | tf_op | source)
XLA Modules:
  0.0 500.2 jit_solution(12900892004599183993)
XLA Ops:
  9.3 4.8 collective-permute-start
  16.2 3.6 collective-permute-done.1.right
  19.8 2.9 shard_map.458
  22.7 5.8 %all-to-all-start = ((bf16[8,192,256]{2,1,0:T(8,128)(2,1)}), bf16[8,192,256]{2,1,0:T(8,128)(2,1)S(1)}, u32[]{:S(2)}, u32[]{:S(2)}) async-start(bf16[8,192,256]{2,1,0:T(8,128)(2,1)} %shard_map.458), calls=%async_computation | async-start | bytes 1572864 | tf_op jit(solution)/shard_map/all_to_all | solution.py:440
  28.5 35.3 %all-to-all-done.refs_0_ = bf16[8,192,256]{2,1,0:T(8,128)(2,1)S(1)} async-done(((bf16[8,192,256]{2,1,0:T(8,128)(2,1)}), bf16[8,192,256]{2,1,0:T(8,128)(2,1)S(1)}, u32[]{:S(2)}, u32[]{:S(2)}) %all-to-all-start) | async-done | bytes 786464 | tf_op jit(solution)/shard_map/all_to_all | solution.py:440
  65.1 3.6 all-to-all-start.1
  69.0 26.6 %all-to-all-done.1.parts = bf16[8,56,512]{2,1,0:T(8,128)(2,1)S(1)} async-done(((bf16[8,56,512]{2,1,0:T(8,128)(2,1)}), bf16[8,56,512]{2,1,0:T(8,128)(2,1)S(1)}, u32[]{:S(2)}, u32[]{:S(2)}) %all-to-all-start.1) | async-done | bytes 458784 | tf_op jit(solution)/shard_map/all_to_all | solution.py:440
  96.5 3.5 all-to-all-start.2
  104.4 21.4 %all-to-all-done.2.steps = bf16[8,56,512]{2,1,0:T(8,128)(2,1)S(1)} async-done(((bf16[8,56,512]{2,1,0:T(8,128)(2,1)}), bf16[8,56,512]{2,1,0:T(8,128)(2,1)S(1)}, u32[]{:S(2)}, u32[]{:S(2)}) %all-to-all-start.2) | async-done | bytes 458784 | tf_op jit(solution)/shard_map/all_to_all | solution.py:445
  129.2 4.3 all-to-all-start.3
  133.5 11.6 %all-to-all-done.3.parts = bf16[8,56,512]{2,1,0:T(8,128)(2,1)} async-done(((bf16[8,56,512]{2,1,0:T(8,128)(2,1)}), bf16[8,56,512]{2,1,0:T(8,128)(2,1)}, u32[]{:S(2)}, u32[]{:S(2)}) %all-to-all-start.3) | async-done | bytes 458784 | tf_op jit(solution)/shard_map/all_to_all | solution.py:440
  148.0 15.9 %all_to_all.60.steps.refs_1_ = bf16[8,56,512]{2,1,0:T(8,128)(2,1)S(1)} all-to-all(bf16[8,56,512]{2,1,0:T(8,128)(2,1)S(1)} %broadcast_in_dim.167), channel_id=1, replica_groups=mesh['series'=4,'tm'=8] {'tm'}, dimensions={0} | all-to-all | bytes 917504 | tf_op jit(solution)/shard_map/all_to_all | solution.py:445
  166.3 4.3 all-to-all-start.5
  175.6 4.6 fusion.24
  180.3 9.5 %all-to-all-done.5.refs_0_ = bf16[8,192,256]{2,1,0:T(8,128)(2,1)} async-done(((bf16[8,192,256]{2,1,0:T(8,128)(2,1)}), bf16[8,192,256]{2,1,0:T(8,128)(2,1)}, u32[]{:S(2)}, u32[]{:S(2)}) %all-to-all-start.5) | async-done | bytes 786464 | tf_op jit(solution)/shard_map/all_to_all | solution.py:440
  192.1 15.6 %shard_map.465 = (bf16[8,192,256]{2,1,0:T(8,128)(2,1)S(1)}, bf16[384,512]{1,0:T(8,128)(2,1)}, f32[2,384,512]{2,1,0:T(8,128)}, bf16[384,1024]{1,0:T(8,128)(2,1)S(...) custom-call(bf16[8,192,256]{2,1,0:T(8,128)(2,1)} %all-to-all-done.5., ...), custom_call_target="tpu_custom_call" | custom-call | tf_op jit(solution)/shard_map/pallas_call | solution.py:41
  211.4 2.9 shard_map.476
  214.3 2.3 copy-done
  216.7 42.5 %all_to_all.61.refs_0_ = bf16[8,192,256]{2,1,0:T(8,128)(2,1)S(1)} all-to-all(bf16[8,192,256]{2,1,0:T(8,128)(2,1)} %copy-done.36), channel_id=1, replica_groups=mesh['series'=4,'tm'=8] {'tm'}, dimensions={0} | all-to-all | bytes 1572864 | tf_op jit(solution)/shard_map/all_to_all | solution.py:440
  261.0 27.0 %all_to_all.62.parts = bf16[8,56,512]{2,1,0:T(8,128)(2,1)S(1)} all-to-all(bf16[8,56,512]{2,1,0:T(8,128)(2,1)S(1)} %shard_map.466), channel_id=1, replica_groups=mesh['series'=4,'tm'=8] {'tm'}, dimensions={0} | all-to-all | bytes 917504 | tf_op jit(solution)/shard_map/all_to_all | solution.py:440
  288.3 14.0 %all_to_all.63.d_iso = bf16[8,56,512]{2,1,0:T(8,128)(2,1)S(1)} all-to-all(bf16[8,56,512]{2,1,0:T(8,128)(2,1)S(1)} %broadcast_in_dim.176), channel_id=1, replica_groups=mesh['series'=4,'tm'=8] {'tm'}, dimensions={0} | all-to-all | bytes 917504 | tf_op jit(solution)/shard_map/all_to_all | solution.py:445
  304.0 14.9 %all_to_all.64.parts = bf16[8,56,512]{2,1,0:T(8,128)(2,1)S(1)} all-to-all(bf16[8,56,512]{2,1,0:T(8,128)(2,1)S(1)} %shard_map.468), channel_id=1, replica_groups=mesh['series'=4,'tm'=8] {'tm'}, dimensions={0} | all-to-all | bytes 917504 | tf_op jit(solution)/shard_map/all_to_all | solution.py:440
  319.9 3.5 all-to-all-start.10
  326.1 2.7 shard_map.474
  329.7 14.8 %all-to-all-done.10.steps.refs_1_ = bf16[8,56,512]{2,1,0:T(8,128)(2,1)S(1)} async-done(((bf16[8,56,512]{2,1,0:T(8,128)(2,1)}), bf16[8,56,512]{2,1,0:T(8,128)(2,1)S(1)}, u32[]{:S(2)}, u32[]{:S(2)}) %all-to-all-start.10) | async-done | bytes 458784 | tf_op jit(solution)/shard_map/all_to_all | solution.py:445
  346.1 11.6 %reduce-scatter.2.cloned.1.call-done = bf16[1,640,512]{2,1,0:T(8,128)(2,1)} async-done(((bf16[8,640,512]{2,1,0:T(8,128)(2,1)}), bf16[1,640,512]{2,1,0:T(8,128)(2,1)}) %reduce-scatter.2.cloned.1.call-update) | async-done | bytes 655376 | tf_op jit(solution)/shard_map/reduce_scatter | solution.py:633
  360.9 3.8 all-to-all-start.11
  369.7 44.0 %psum.57 = f32[20,512]{1,0:T(8,128)S(1)} all-reduce(f32[20,512]{1,0:T(8,128)S(1)} %pad_maximum_fusion.2), channel_id=1, replica_groups=mesh['series'=4,'tm'=8] {'series','tm'}, use_global_device_ids=true, to_apply=%region_10.11 | all-reduce | flops 10240 | bytes 81920 | tf_op jit(solution)/shard_map/psum | solution.py:699
  414.9 2.5 shard_map.472
  417.4 4.1 collective-permute-start.2
  423.1 4.2 collective-permute-done.3
  428.1 52.8 %all-reduce.3.cloned.1.call-done = (bf16[768,512]{1,0:T(8,128)(2,1)}, bf16[1024,512]{1,0:T(8,128)(2,1)}, bf16[768,512]{1,0:T(8,128)(2,1)}, bf16[1024,512]{1,0:T(...) async-done(((bf16[768,512]{1,0:T(8,128)(2,1)}, bf16[1024,512]{1,0:T(8,128)(2,1)}, bf16[768,512]{1,0:T(8,128)(2,1)}, ...) | async-done | bytes 6160400 | tf_op jit(solution)/shard_map/psum | solution.py:705
  (220 shorter events, 64.7 us)
Async XLA Ops:
  7.2 167.0 %all-gather.3.cloned.1.call-start = ((), (), s32[]{:S(2)}) async-start(), calls=%async_computation.14 | async-start | bytes 5898240 | tf_op jit(solution)/shard_map/all_gather | solution.py:529
  9.3 6.9 %collective-permute-start = (bf16[16,512]{1,0:T(8,128)(2,1)S(1)}, bf16[16,512]{1,0:T(8,128)(2,1)S(1)}, u32[]{:S(2)}, u32[]{:S(2)}) collective-permute-start(bf16[16,512]{1,0:T(8,128)(2,1)S(1)} %get-tuple-element.108), channel_id=1, source_target_pairs={{0,1},{1,2},{2,3},{3,4},{4,5},{5,6},{6,7},{8,9},{9,10},{10,11},{11... | collective-permute-start | bytes 49160 | tf_op jit(solution)/shard_map/ppermute | solution.py:554
  14.1 5.6 %collective-permute-start.1 = (bf16[16,512]{1,0:T(8,128)(2,1)S(1)}, bf16[16,512]{1,0:T(8,128)(2,1)S(1)}, u32[]{:S(2)}, u32[]{:S(2)}) collective-permute-start(bf16[16,512]{1,0:T(8,128)(2,1)S(1)} %get-tuple-element.107), channel_id=1, source_target_pairs={{1,0},{2,1},{3,2},{4,3},{5,4},{6,5},{7,6},{9,8},{10,9},{11,10},{12... | collective-permute-start | bytes 49160 | tf_op jit(solution)/shard_map/ppermute | solution.py:555
  19.8 44.0 %copy-start.4 = (bf16[1024,512]{1,0:T(8,128)(2,1)S(1)}, bf16[1024,512]{1,0:T(8,128)(2,1)}, u32[]{:S(2)}) copy-start(bf16[1024,512]{1,0:T(8,128)(2,1)} %weight_two.3) | copy-start | bytes 3145732
  19.8 44.0 %copy-start.17 = (bf16[768,512]{1,0:T(8,128)(2,1)S(1)}, bf16[768,512]{1,0:T(8,128)(2,1)}, u32[]{:S(2)}) copy-start(bf16[768,512]{1,0:T(8,128)(2,1)} %weight_one.7) | copy-start | bytes 2359300
  22.7 41.1 %all-to-all-start = ((bf16[8,192,256]{2,1,0:T(8,128)(2,1)}), bf16[8,192,256]{2,1,0:T(8,128)(2,1)S(1)}, u32[]{:S(2)}, u32[]{:S(2)}) async-start(bf16[8,192,256]{2,1,0:T(8,128)(2,1)} %shard_map.458), calls=%async_computation | async-start | bytes 1572864 | tf_op jit(solution)/shard_map/all_to_all | solution.py:440
  28.5 40.3 %copy-start.56 = (f32[512]{0:T(512)S(1)}, f32[512]{0:T(512)}, u32[]{:S(2)}) copy-start(f32[512]{0:T(512)} %param.36) | copy-start | bytes 6148
  28.5 40.3 %copy-start.57 = (f32[512]{0:T(512)S(1)}, f32[512]{0:T(512)}, u32[]{:S(2)}) copy-start(f32[512]{0:T(512)} %param.30) | copy-start | bytes 6148
  65.1 30.5 %all-to-all-start.1 = ((bf16[8,56,512]{2,1,0:T(8,128)(2,1)}), bf16[8,56,512]{2,1,0:T(8,128)(2,1)S(1)}, u32[]{:S(2)}, u32[]{:S(2)}) async-start(bf16[8,56,512]{2,1,0:T(8,128)(2,1)} %shard_map.459), calls=%async_computation.1 | async-start | bytes 917504 | tf_op jit(solution)/shard_map/all_to_all | solution.py:440
  69.0 56.8 %copy-start.6 = (bf16[1024,512]{1,0:T(8,128)(2,1)S(1)}, bf16[1024,512]{1,0:T(8,128)(2,1)}, u32[]{:S(2)}) copy-start(bf16[1024,512]{1,0:T(8,128)(2,1)} %weight_one.6) | copy-start | bytes 3145732
  96.5 29.3 %all-to-all-start.2 = ((bf16[8,56,512]{2,1,0:T(8,128)(2,1)}), bf16[8,56,512]{2,1,0:T(8,128)(2,1)S(1)}, u32[]{:S(2)}, u32[]{:S(2)}) async-start(bf16[8,56,512]{2,1,0:T(8,128)(2,1)} %broadcast_in_dim.161), calls=%async_computation.2 | async-start | bytes 917504 | tf_op jit(solution)/shard_map/all_to_all | solution.py:445
  126.7 18.4 %copy-start.40 = (f32[512]{0:T(512)S(1)}, f32[512]{0:T(512)}, u32[]{:S(2)}) copy-start(f32[512]{0:T(512)} %param.41) | copy-start | bytes 6148
  126.7 18.4 %copy-start.41 = (f32[512]{0:T(512)S(1)}, f32[512]{0:T(512)}, u32[]{:S(2)}) copy-start(f32[512]{0:T(512)} %param.42) | copy-start | bytes 6148
  129.2 34.8 %copy-start.2 = (bf16[1024,512]{1,0:T(8,128)(2,1)S(1)}, bf16[1024,512]{1,0:T(8,128)(2,1)}, u32[]{:S(2)}) copy-start(bf16[1024,512]{1,0:T(8,128)(2,1)} %refs_2_.3) | copy-start | bytes 3145732
  129.2 15.9 %all-to-all-start.3 = ((bf16[8,56,512]{2,1,0:T(8,128)(2,1)}), bf16[8,56,512]{2,1,0:T(8,128)(2,1)}, u32[]{:S(2)}, u32[]{:S(2)}) async-start(bf16[8,56,512]{2,1,0:T(8,128)(2,1)} %copy-done.19), calls=%async_computation.3 | async-start | bytes 917504 | tf_op jit(solution)/shard_map/all_to_all | solution.py:440
  145.1 18.9 %copy-start.15 = (bf16[768,512]{1,0:T(8,128)(2,1)S(1)}, bf16[768,512]{1,0:T(8,128)(2,1)}, u32[]{:S(2)}) copy-start(bf16[768,512]{1,0:T(8,128)(2,1)} %refs_1_.3) | copy-start | bytes 2359300
  166.3 23.5 %all-to-all-start.5 = ((bf16[8,192,256]{2,1,0:T(8,128)(2,1)}), bf16[8,192,256]{2,1,0:T(8,128)(2,1)}, u32[]{:S(2)}, u32[]{:S(2)}) async-start(bf16[8,192,256]{2,1,0:T(8,128)(2,1)} %copy-done.14), calls=%async_computation.5 | async-start | bytes 1572864 | tf_op jit(solution)/shard_map/all_to_all | solution.py:440
  170.6 187.1 %reduce-scatter.2.cloned.1.call-start = ((), (), s32[]{:S(2)}) async-start(), calls=%async_computation.13 | async-start | bytes 5898240 | tf_op jit(solution)/shard_map/reduce_scatter | solution.py:633
  175.6 14.2 %copy-start.42 = (f32[2048]{0:T(1024)S(1)}, f32[2048]{0:T(1024)}, u32[]{:S(2)}) copy-start(f32[2048]{0:T(1024)} %param.48) | copy-start | bytes 24580
  216.7 42.5 %copy-start.3 = (bf16[1024,512]{1,0:T(8,128)(2,1)S(1)}, bf16[1024,512]{1,0:T(8,128)(2,1)}, u32[]{:S(2)}) copy-start(bf16[1024,512]{1,0:T(8,128)(2,1)} %refs_2_.3) | copy-start | bytes 3145732
  260.4 27.6 %copy-start.35 = (f32[56,512]{1,0:T(8,128)S(1)}, f32[56,512]{1,0:T(8,128)}, u32[]{:S(2)}) copy-start(f32[56,512]{1,0:T(8,128)} %copy-done.33) | copy-start | bytes 344068
  260.4 27.6 %copy-start.39 = (f32[56,512]{1,0:T(8,128)S(1)}, f32[56,512]{1,0:T(8,128)}, u32[]{:S(2)}) copy-start(f32[56,512]{1,0:T(8,128)} %copy-done.38) | copy-start | bytes 344068
  261.0 41.4 %copy-start.7 = (bf16[1024,512]{1,0:T(8,128)(2,1)S(1)}, bf16[1024,512]{1,0:T(8,128)(2,1)}, u32[]{:S(2)}) copy-start(bf16[1024,512]{1,0:T(8,128)(2,1)} %weight_one.6) | copy-start | bytes 3145732
  261.0 41.4 %copy-start.29 = (s32[192,1]{1,0:T(8,128)S(1)}, s32[192,1]{1,0:T(8,128)}, u32[]{:S(2)}) copy-start(s32[192,1]{1,0:T(8,128)} %add_select_fusion.1.start_two) | copy-start | bytes 2308
  304.0 19.4 %copy-start.9 = (bf16[8,56,512]{2,1,0:T(8,128)(2,1)S(1)}, bf16[8,56,512]{2,1,0:T(8,128)(2,1)}, u32[]{:S(2)}) copy-start(bf16[8,56,512]{2,1,0:T(8,128)(2,1)} %copy-done.8) | copy-start | bytes 1376260
  319.9 24.6 %all-to-all-start.10 = ((bf16[8,56,512]{2,1,0:T(8,128)(2,1)}), bf16[8,56,512]{2,1,0:T(8,128)(2,1)S(1)}, u32[]{:S(2)}, u32[]{:S(2)}) async-start(bf16[8,56,512]{2,1,0:T(8,128)(2,1)} %broadcast_in_dim.177), calls=%async_computation.10 | async-start | bytes 917504 | tf_op jit(solution)/shard_map/all_to_all | solution.py:445
  323.3 157.5 %all-reduce.3.cloned.1.call-start = ((), (), s32[]{:S(2)}) async-start(), calls=%async_computation.15 | async-start | bytes 12320768 | tf_op jit(solution)/shard_map/psum | solution.py:705
  360.9 54.0 %all-to-all-start.11 = ((bf16[8,192,256]{2,1,0:T(8,128)(2,1)}), bf16[8,192,256]{2,1,0:T(8,128)(2,1)S(1)}, u32[]{:S(2)}, u32[]{:S(2)}) async-start(bf16[8,192,256]{2,1,0:T(8,128)(2,1)} %shard_map.470), calls=%async_computation.11 | async-start | bytes 1572864 | tf_op jit(solution)/shard_map/all_to_all | solution.py:440
  364.7 50.2 %copy-start.23 = (s32[384,3]{1,0:T(8,128)S(1)}, s32[384,3]{1,0:T(8,128)}, u32[]{:S(2)}) copy-start(s32[384,3]{1,0:T(8,128)} %copy-done.22) | copy-start | bytes 13828
  364.7 50.2 %copy-start.25 = (s32[384,3]{1,0:T(8,128)S(1)}, s32[384,3]{1,0:T(8,128)}, u32[]{:S(2)}) copy-start(s32[384,3]{1,0:T(8,128)} %copy-done.24) | copy-start | bytes 13828
  417.4 5.6 %collective-permute-start.2 = (f32[16,512]{1,0:T(8,128)S(1)}, f32[16,512]{1,0:T(8,128)S(1)}, u32[]{:S(2)}, u32[]{:S(2)}) collective-permute-start(f32[16,512]{1,0:T(8,128)S(1)} %get-tuple-element.66), channel_id=1, source_target_pairs={{0,1},{1,2},{2,3},{3,4},{4,5},{5,6},{6,7},{8,9},{9,10},{10,11},{11... | collective-permute-start | bytes 98312 | tf_op jit(solution)/shard_map/ppermute | solution.py:694
  421.5 5.8 %collective-permute-start.3 = (f32[16,512]{1,0:T(8,128)S(1)}, f32[16,512]{1,0:T(8,128)S(1)}, u32[]{:S(2)}, u32[]{:S(2)}) collective-permute-start(f32[16,512]{1,0:T(8,128)S(1)} %get-tuple-element.67), channel_id=1, source_target_pairs={{1,0},{2,1},{3,2},{4,3},{5,4},{6,5},{7,6},{9,8},{10,9},{11,10},{12... | collective-permute-start | bytes 98312 | tf_op jit(solution)/shard_map/ppermute | solution.py:693
  (45 other events, 175.2 us)
Sparse Core Ops, SparseCore 0:
  10.8 122.5 all-gather.2
  216.8 140.8 reduce-scatter.1
  361.8 119.0 all-reduce.2

commit v2 on v1

v2 whole, which is shorter than its diff:
```python
import functools
import math

import jax
import jax.numpy as jnp
from jax import lax
from jax.experimental import pallas as pl
from jax.experimental.pallas import tpu as pltpu
from jax.sharding import PartitionSpec as P

SCALES = (12, 16)
AVERAGES = (13, 17)
TAPS = (16, 12)
UNIT = 48
EPSILON = 1e-05
HALO = 16
FFN_CHUNK = 512
SUM_ROWS = 16

BF = jnp.bfloat16
F32 = jnp.float32
I32 = jnp.int32


def dot(left, right):
    return lax.dot_general(left, right, (((1,), (0,)), ((), ())), preferred_element_type=F32)


def dot_nt(left, right):
    return lax.dot_general(left, right, (((1,), (1,)), ((), ())), preferred_element_type=F32)


def dot_tn(left, right):
    return lax.dot_general(left, right, (((0,), (0,)), ((), ())), preferred_element_type=F32)


def kernel_call(body, outs, args, mib, scalars=(), scratch=()):
    specs = [
        pl.BlockSpec(memory_space=pltpu.SMEM if i in scalars else pltpu.VMEM)
        for i in range(len(args))
    ]
    return pl.pallas_call(
        body,
        out_shape=[jax.ShapeDtypeStruct(shape, dtype) for shape, dtype in outs],
        in_specs=specs,
        out_specs=[pl.BlockSpec(memory_space=pltpu.VMEM) for _ in outs],
        scratch_shapes=list(scratch),
        compiler_params=pltpu.CompilerParams(vmem_limit_bytes=mib << 20),
    )(*args)


def tap_to_payload(x, scale, q, n):
    rows, channels = x.shape
    m, h = rows // scale, channels // q
    parts = [x[:, c * q : (c + 1) * q].reshape(scale, 1, m, q) for c in range(h)]
    whole = parts[0] if h == 1 else jnp.concatenate(parts, axis=1)
    return whole.reshape(n, scale * h * m // n, q)


def payload_to_tap(p, scale, channels):
    n, rows, q = p.shape
    h = channels // q
    m = n * rows // (scale * h)
    p = p.reshape(scale, h, m, q)
    parts = [p[:, c].reshape(scale * m, q) for c in range(h)]
    return parts[0] if h == 1 else jnp.concatenate(parts, axis=1)


def payload_units(p, m):
    n, rows, q = p.shape
    p = p.reshape(n, rows // m, m, q)
    return [p[:, i].reshape(n * m, q).astype(BF) for i in range(rows // m)]


def units_to_payload(units, n):
    parts = [u.reshape(n, u.shape[0] // n, u.shape[1]) for u in units]
    return parts[0] if len(parts) == 1 else jnp.concatenate(parts, axis=1)


def split_steps(ref, counts):
    whole = ref[...].astype(F32)
    n, _, channels = whole.shape
    first = whole[:, : counts[0], :].reshape(n * counts[0], channels)
    return [first, whole[:, counts[0] : sum(counts), :].reshape(n * counts[1], channels)]


def join_steps(parts, n):
    return jnp.concatenate([p.reshape(n, p.shape[0] // n, p.shape[1]) for p in parts], axis=1)


def norm_stats(v):
    mean = jnp.mean(v, axis=-1, keepdims=True)
    centered = v - mean
    rstd = lax.rsqrt(jnp.mean(centered * centered, axis=-1, keepdims=True) + EPSILON)
    return centered * rstd, rstd


def norm_back(d, gain, xhat, rstd):
    dg = d * gain
    mean_d = jnp.mean(dg, axis=-1, keepdims=True)
    mean_dx = jnp.mean(dg * xhat, axis=-1, keepdims=True)
    return rstd * (dg - mean_d - xhat * mean_dx)


def column_sum(v):
    return jnp.sum(v, axis=0, keepdims=True)


def average_counts(info, kernel, columns):
    place, first, last = info[:, 0:1], info[:, 1:2], info[:, 2:3]
    reach = kernel // 2
    column = lax.broadcasted_iota(I32, (info.shape[0], columns), 1)
    away = column - place
    inside = (jnp.abs(away) <= reach) & (column >= first) & (column <= last)
    counts = jnp.where(inside, 1, 0)
    counts = counts + jnp.where(column == first, jnp.maximum(reach - (place - first), 0), 0)
    counts = counts + jnp.where(column == last, jnp.maximum(reach - (last - place), 0), 0)
    return counts, away == 0


def season_matrix(info, kernel, columns):
    counts, own = average_counts(info, kernel, columns)
    values = jnp.where(own, kernel, 0) - counts
    values = jnp.where(info[:, 0:1] >= info[:, 1:2], values, 0)
    return values.astype(F32).astype(BF)


def token_order(rows, scale):
    m = rows // scale
    place = lax.broadcasted_iota(I32, (rows, rows), 0)
    column = lax.broadcasted_iota(I32, (rows, rows), 1)
    tap = jnp.zeros_like(column)
    for k in range(1, scale):
        tap = tap + jnp.where(column >= k * m, 1, 0)
    return jnp.where(place == scale * (column - tap * m) + tap, 1.0, 0.0).astype(BF)


def join_payload(geo, taps):
    return jnp.concatenate(
        [tap_to_payload(t, SCALES[b], geo["q"], geo["n"]) for b, t in enumerate(taps)], axis=1
    )


def split_payload(geo, payload, channels):
    low = geo["pay_rows"][0]
    parts = (payload[:, :low], payload[:, low:])
    return [payload_to_tap(p, SCALES[b], channels) for b, p in enumerate(parts)]


def store_taps(geo, outs, taps):
    if not geo["aligned"]:
        for out, tap in zip(outs, taps):
            out[...] = tap.astype(BF)
        return
    outs[0][...] = join_payload(geo, taps).astype(BF)


def load_taps(geo, pays, channels):
    if not geo["aligned"]:
        return [p[...] for p in pays]
    whole = pays[0][...].astype(F32)
    return [t.astype(BF) for t in split_payload(geo, whole, channels)]


def windows_body(geo, tok, left, right, info_one, info_two, *outs):
    x = jnp.concatenate([left[...], tok[...], right[...]], axis=0)
    parts = []
    for b, info in enumerate((info_one, info_two)):
        matrix = season_matrix(info[...], AVERAGES[b], x.shape[0])
        parts.append(dot(matrix, x) * (1.0 / AVERAGES[b]))
    store_taps(geo, outs, parts)


def season_body(tok, left, right, info, out):
    x = jnp.concatenate([left[...], tok[...], right[...]], axis=0)
    wide = tok[...].astype(F32)
    for b in range(2):
        counts, _ = average_counts(info[...], AVERAGES[b], x.shape[0])
        out[b] = wide - dot(counts.astype(F32).astype(BF), x) * (1.0 / AVERAGES[b])


def slab_starts(geo):
    return (0, geo["slab"][0])


def units_against(geo, payload, weight, totals):
    low = geo["pay_rows"][0]
    for b, p in enumerate((payload[:, :low], payload[:, low:])):
        q, start = geo["q"], slab_starts(geo)[b]
        for i, unit in enumerate(payload_units(p, geo["m"][b])):
            term = dot(unit, weight[start + i * q : start + (i + 1) * q, :])
            totals[b] = term if totals[b] is None else totals[b] + term


def slab_in_body(geo, payload, weight, out):
    totals = [None, None]
    units_against(geo, payload[...].astype(F32), weight, totals)
    out[...] = join_steps(totals, geo["n"]).astype(BF)


def steps_against(geo, lows, weight, n):
    q = geo["q"]
    parts = []
    for b, low in enumerate(lows):
        start = slab_starts(geo)[b]
        units = [
            dot_nt(low, weight[start + i * q : start + (i + 1) * q, :])
            for i in range(geo["slab"][b] // q)
        ]
        parts.append(units_to_payload(units, n))
    return jnp.concatenate(parts, axis=1).astype(BF)


def slab_out_body(geo, steps, own, out):
    lows = [x.astype(BF) for x in split_steps(steps, geo["m"])]
    out[...] = steps_against(geo, lows, own, geo["n"])


def store_halved(out, start, size, at, value):
    step = math.gcd(value.shape[0], size // 2)
    for i in range(0, value.shape[0], step):
        h, r = divmod(at + i, size // 2)
        out[h, start + r : start + r + step, :] = value[i : i + step].astype(BF)


def store_core_parts(core, halves, rows, own, sent):
    blank = jnp.zeros((SUM_ROWS - len(rows), halves.shape[2]), F32)
    halves[0, halves.shape[1] - SUM_ROWS :, :] = jnp.concatenate([*rows, blank], axis=0).astype(BF)
    halves[1, halves.shape[1] - SUM_ROWS :, :] = jnp.zeros((SUM_ROWS, halves.shape[2]), BF)
    own[...] = halves[core]
    sent[...] = halves[1 - core]


def slab_grad_body(geo, core, payload, steps, own, sent, halves):
    low, q, slab = geo["pay_rows"][0], geo["q"], geo["slab"]
    rights = split_steps(steps, geo["m"])
    wide = payload[...].astype(F32)
    for b in range(2):
        right = rights[b].astype(BF)
        part = wide[:, :low] if b == 0 else wide[:, low:]
        for i, unit in enumerate(payload_units(part, geo["m"][b])):
            store_halved(halves, slab_starts(geo)[b] // 2, slab[b], i * q, dot_tn(unit, right))
    store_core_parts(core[0], halves, [column_sum(r) for r in rights], own, sent)


def join_body(core, part, got, out_one, out_two, sums):
    at = 0
    for out in (out_one, out_two, sums):
        rows = out.shape[0] // 2
        for which, value in ((core[0], part), (1 - core[0], got)):
            begin = pl.multiple_of(which * rows, math.gcd(rows, 512))
            out[pl.ds(begin, rows), :] = value[at : at + rows, :].astype(F32)
        at += rows


def tap_inputs(geo, b, shifts, hidden, start):
    count = hidden.shape[0]
    step = lax.broadcasted_iota(I32, (count, 1), 0)
    pieces = []
    for i in range(geo["touched"][b]):
        shift = jnp.maximum(shifts[b] - i, 0)
        moved = pltpu.roll(hidden, shift, 0)
        pieces.append(jnp.where(step - shift >= start, moved, 0.0).astype(BF))
    return pieces


def iso_body(geo, shifts, steps, start_one, start_two, weight_one, weight_two, out):
    parts = []
    hiddens = split_steps(steps, geo["m"])
    for b, (start, weight) in enumerate(((start_one, weight_one), (start_two, weight_two))):
        total = None
        channels = hiddens[b].shape[1]
        for i, piece in enumerate(tap_inputs(geo, b, shifts, hiddens[b], start[...])):
            term = dot(piece, weight[i * channels : (i + 1) * channels, :])
            total = term if total is None else total + term
        parts.append(total)
    out[...] = join_steps(parts, geo["n"]).astype(BF)


def iso_back_body(geo, shifts, d_iso, start_one, start_two, weight_one, weight_two, out):
    parts = []
    for b, (d, start, weight) in enumerate(
        zip(split_steps(d_iso, geo["m"]), (start_one, start_two), (weight_one, weight_two))
    ):
        count, channels = d.shape
        low = d.astype(BF)
        step = lax.broadcasted_iota(I32, (count, 1), 0)
        total = None
        for i in range(geo["touched"][b]):
            shift = jnp.maximum(shifts[b] - i, 0)
            stacked = dot_nt(low, weight[i * channels : (i + 1) * channels, :])
            stacked = jnp.where(step - shift >= start[...], stacked, 0.0)
            moved = pltpu.roll(stacked, lax.rem(count - shift, count), 0)
            total = moved if total is None else total + moved
        parts.append(total)
    out[...] = join_steps(parts, geo["n"]).astype(BF)


def iso_grad_body(geo, shifts, steps, d_iso, start_one, start_two, own, sent, wide_one, wide_two, halves):
    hiddens, ds = split_steps(steps, geo["m"]), split_steps(d_iso, geo["m"])
    begin = 0
    for b, (start, wide) in enumerate(((start_one, wide_one), (start_two, wide_two))):
        channels = hiddens[b].shape[1]
        right = ds[b].astype(BF)
        for i, piece in enumerate(tap_inputs(geo, b, shifts, hiddens[b], start[...])):
            wide[i * channels : (i + 1) * channels, :] = dot_tn(piece, right)
        part = geo["iso_slab"][b] // 2
        for h in range(2):
            at = pl.multiple_of(shifts[2 + b] + h * part, math.gcd(geo["iso_q"][b], part))
            halves[h, begin : begin + part, :] = wide[pl.ds(at, part), :].astype(BF)
        begin += part
    at = sum(geo["m"])
    norm_sums = jnp.sum(d_iso[:, at:, :].astype(F32), axis=0)
    rows = [*(column_sum(d) for d in ds), norm_sums[0:1], norm_sums[1:2]]
    store_core_parts(shifts[4], halves, rows, own, sent)


def branch_rows(pair, counts):
    total = sum(counts)
    step = lax.broadcasted_iota(I32, (total, 1), 0)
    return jnp.where(step < counts[0], pair[0:1, :], pair[1:2, :])


def hidden_one_body(geo, parts, bias, hidden, low):
    value = jnp.tanh(jnp.sum(parts[...].astype(F32), axis=0) + branch_rows(bias, geo["m"]))
    hidden[...] = value
    low[...] = jnp.broadcast_to(value.astype(BF)[None], low.shape)


def mix_body(geo, parts, bias, hidden_one, gain, shift, hidden, mixed):
    value = jnp.tanh(jnp.sum(parts[...].astype(F32), axis=0) + branch_rows(bias, geo["m"]))
    hidden[...] = value
    xhat, _ = norm_stats(value + hidden_one[...])
    low = (xhat * gain[...] + shift[...]).astype(BF)
    mixed[...] = jnp.broadcast_to(low[None], mixed.shape)


def mix_back_body(geo, parts, hidden_one, hidden_two, gain, d_pair, d_iso):
    d = jnp.sum(parts[...].astype(F32), axis=0)
    two = hidden_two[...]
    xhat, rstd = norm_stats(two + hidden_one[...])
    pair = norm_back(d, gain[...], xhat, rstd)
    iso = (1.0 - two * two) * pair
    d_pair[...] = pair
    blank = jnp.zeros((d_iso.shape[1] - iso.shape[0] - 2, iso.shape[1]), F32)
    low = jnp.concatenate([iso, column_sum(d * xhat), column_sum(d), blank], axis=0).astype(BF)
    d_iso[...] = jnp.broadcast_to(low[None], d_iso.shape)


def conv_back_body(geo, parts, d_pair, hidden_one, d_conv):
    one = hidden_one[...]
    d = (jnp.sum(parts[...].astype(F32), axis=0) + d_pair[...]) * (1.0 - one * one)
    d_conv[...] = jnp.broadcast_to(d.astype(BF)[None], d_conv.shape)


def place_head(geo, order, pieces, merge, expand, project):
    m_rows, h_rows = geo["quarter_rows"][:2]
    for first, begin, piece in pieces:
        for i in range(piece.shape[0]):
            block = first + 2 * (begin + i)
            at = pl.multiple_of(order[block] * m_rows, m_rows)
            merge[pl.ds(at, m_rows), :] = piece[i, :m_rows, :]
            at = pl.ds(pl.multiple_of(order[block] * h_rows, h_rows), h_rows)
            expand[at, :] = piece[i, m_rows : m_rows + h_rows, :]
            project[at, :] = piece[i, m_rows + h_rows :, :]


def head_body(geo, *refs):
    taps = geo["taps"]
    pays, refs = refs[:taps], refs[taps:]
    (
        season, cotangent, up_bias, mix_gain, mix_shift, merge_bias, feed_gain, feed_shift,
        expand_bias, project_bias, final_gain, final_shift,
    ) = refs[:12]
    refs = refs[12:]
    if geo["fits"]:
        order, pieces, refs = refs[0], refs[1 : 1 + geo["pieces"]], refs[1 + geo["pieces"] :]
        merge_weight, expand_weight, project_weight = refs[-3:]
        refs = refs[:-3]
        pieces = [(*at, piece) for at, piece in zip(geo["piece_starts"], pieces)]
        place_head(geo, order, pieces, merge_weight, expand_weight, project_weight)
    else:
        (merge_weight, expand_weight, project_weight), refs = refs[:3], refs[3:]
    d_pays, outs = refs[:taps], refs[taps:]
    (
        result, d_res_out, merge_in, normed_out, activ_out, d_sum_out, d_pre_out, d_merged_out, sums, expand_sums,
        slope,
    ) = outs
    rows, channels = cotangent.shape
    width = FFN_CHUNK
    chunks = expand_weight.shape[0] // width
    taps = load_taps(geo, pays, channels)
    ups, kept = [], []
    for b in range(2):
        order = token_order(rows, SCALES[b])
        up = jnp.tanh(dot(order, taps[b]) + up_bias[b : b + 1, :])
        xhat, rstd = norm_stats(up + season[b])
        ups.append(up)
        kept.append((xhat, rstd))
        merge_in[:, b * channels : (b + 1) * channels] = (
            xhat * mix_gain[...] + mix_shift[...]
        ).astype(BF)
    merged = dot(merge_in[...], merge_weight[...]) + merge_bias[...]
    feed_hat, feed_rstd = norm_stats(merged)
    normed_out[...] = (feed_hat * feed_gain[...] + feed_shift[...]).astype(BF)

    def forward_chunk(c, total):
        at = pl.ds(pl.multiple_of(c * width, width), width)
        pre = dot_nt(normed_out[...], expand_weight[at, :]) + expand_bias[:, at]
        half = 0.5 + 0.5 * lax.erf(pre * math.sqrt(0.5))
        slope[c] = half + pre * (jnp.exp(-0.5 * pre * pre) * (1.0 / math.sqrt(2.0 * math.pi)))
        activ_out[:, at] = (pre * half).astype(BF)
        return total + dot(activ_out[:, at], project_weight[at, :])

    summed = lax.fori_loop(0, chunks, forward_chunk, merged + project_bias[...])
    final_hat, final_rstd = norm_stats(summed)
    result[...] = (final_hat * final_gain[...] + final_shift[...]).astype(BF)

    d_out = cotangent[...].astype(F32)
    sums[0:1, :] = column_sum(d_out * final_hat)
    sums[1:2, :] = column_sum(d_out)
    d_sum = norm_back(d_out, final_gain[...], final_hat, final_rstd)
    sums[2:3, :] = column_sum(d_sum)
    d_sum_out[...] = d_sum.astype(BF)

    def backward_chunk(c, total):
        at = pl.ds(pl.multiple_of(c * width, width), width)
        d_pre = slope[c] * dot_nt(d_sum_out[...], project_weight[at, :])
        expand_sums[:, at] = column_sum(d_pre)
        d_pre_out[:, at] = d_pre.astype(BF)
        return total + dot(d_pre_out[:, at], expand_weight[at, :])

    d_normed = lax.fori_loop(0, chunks, backward_chunk, jnp.zeros((rows, channels), F32))
    sums[3:4, :] = column_sum(d_normed * feed_hat)
    sums[4:5, :] = column_sum(d_normed)
    d_merged = d_sum + norm_back(d_normed, feed_gain[...], feed_hat, feed_rstd)
    sums[5:6, :] = column_sum(d_merged)
    d_merged_out[...] = d_merged.astype(BF)
    gain_sum, shift_sum = 0.0, 0.0
    d_taps = []
    for b in range(2):
        d = dot_nt(d_merged_out[...], merge_weight[b * channels : (b + 1) * channels, :])
        xhat, rstd = kept[b]
        gain_sum = gain_sum + column_sum(d * xhat)
        shift_sum = shift_sum + column_sum(d)
        d_res = norm_back(d, mix_gain[...], xhat, rstd)
        d_res_out[b] = d_res
        d_up = (1.0 - ups[b] * ups[b]) * d_res
        sums[8 + b : 9 + b, :] = column_sum(d_up)
        d_taps.append(dot_tn(token_order(rows, SCALES[b]), d_up.astype(BF)))
    sums[6:7, :] = gain_sum
    sums[7:8, :] = shift_sum
    store_taps(geo, d_pays, d_taps)


def head_grad_body(geo, *refs):
    lefts = refs[:6]
    merge_in, normed, activ, d_sum, d_pre, d_merged = lefts
    pairs = ((merge_in, d_merged), (d_pre, normed), (activ, d_sum))
    if not geo["fits"]:
        for out, (left, right) in zip(refs[6:], pairs):
            out[...] = dot_tn(left[...], right[...]).astype(BF)
        return
    sums, expand_sums, order, own, other, merge, hidden = refs[6:]
    blocks, _, channels = own.shape
    m_rows, h_rows = geo["quarter_rows"][:2]
    at = m_rows + 2 * h_rows
    count = sums.shape[0] + expand_sums.shape[0]
    rows = jnp.concatenate(
        [sums[...], expand_sums[...], jnp.zeros((SUM_ROWS - count, channels), F32)], axis=0
    ).astype(BF)
    start = 0
    for (left, right), grads, size in zip(pairs, (merge, hidden, hidden), (m_rows, h_rows, h_rows)):
        grads[...] = dot_tn(left[...], right[...]).astype(BF)
        for h, out in enumerate((own, other)):
            for i in range(blocks):
                begin = pl.multiple_of(order[h * blocks + i] * size, size)
                out[i, start : start + size, :] = grads[pl.ds(begin, size), :]
        start += size
    for out in (own, other):
        out[:, at:, :] = jnp.broadcast_to(rows, (blocks, *rows.shape))


def residual_body(d_res, info, out):
    rows = d_res.shape[1]
    columns = rows + 2 * HALO
    total = jnp.zeros((columns, d_res.shape[2]), F32)
    for b in range(2):
        counts, _ = average_counts(info[...], AVERAGES[b], columns)
        adjoint = dot_tn(counts.astype(F32).astype(BF), d_res[b].astype(BF))
        total = total - adjoint * (1.0 / AVERAGES[b])
    out[0:HALO, :] = total[0:HALO]
    out[HALO : HALO + rows, :] = total[HALO : HALO + rows] + d_res[0] + d_res[1]
    out[HALO + rows :, :] = total[HALO + rows :]


def input_back_body(geo, *refs):
    pays = refs[: geo["taps"]]
    info_one, info_two, residual, own, left, right = refs[geo["taps"] :]
    columns, channels = residual.shape
    rows = columns - 2 * HALO
    taps = load_taps(geo, pays, channels)
    total = residual[...]
    for b, info in enumerate((info_one, info_two)):
        matrix = season_matrix(info[...], AVERAGES[b], columns)
        total = total + dot_tn(matrix, taps[b]) * (1.0 / AVERAGES[b])
    left[...] = total[0:HALO]
    own[...] = total[HALO : HALO + rows]
    right[...] = total[HALO + rows :]


def swap(x):
    return lax.all_to_all(x, "tm", 0, 0)


def together(*values):
    return lax.optimization_barrier(values)


def after(x, dep):
    return lax.optimization_barrier((x, dep))[0]


def across(x, axis, bit):
    return lax.ppermute(x, axis, [(i, i ^ bit) for i in range(lax.axis_size(axis))])


def bit_of(axis, bit):
    return (lax.axis_index(axis) & bit) // bit


def by_replica(x):
    x = jnp.where(bit_of("series", 1) == 1, x[::-1], x)
    return jnp.where(bit_of("series", 2) == 1, x[:, :, ::-1], x)


def summed(*parts):
    return sum(p.astype(F32) for p in parts).astype(BF)


def neighbours(n):
    up = [(i, i + 1) for i in range(n - 1)]
    return up, [(j, i) for i, j in up]


def on_device(
    inputs, lengths,
    stride_weight_twelve, stride_bias_twelve, isometric_weight_twelve, isometric_bias_twelve,
    upsample_weight_twelve, upsample_bias_twelve,
    stride_weight_sixteen, stride_bias_sixteen, isometric_weight_sixteen, isometric_bias_sixteen,
    upsample_weight_sixteen, upsample_bias_sixteen,
    mix_gain, mix_shift, merge_weight, merge_bias, feed_gain, feed_shift,
    expand_weight, expand_bias, project_weight, project_bias, final_gain, final_shift, cotangent,
):
    n = lax.axis_size("tm")
    me = lax.axis_index("tm")
    rows, channels = inputs.shape[1:]
    stride_weights = (stride_weight_twelve, stride_weight_sixteen)
    iso_weights = (isometric_weight_twelve, isometric_weight_sixteen)
    up_weights = (upsample_weight_twelve, upsample_weight_sixteen)
    m = [rows // s for s in SCALES]
    slab = [w.shape[0] for w in stride_weights]
    q = math.gcd(*slab, channels)
    pay_rows = [slab[b] // q * m[b] for b in range(2)]
    iso_slab = [w.shape[0] for w in iso_weights]
    iso_q = [math.gcd(r, channels) for r in iso_slab]
    touched = [-(-(iso_slab[b] + channels - iso_q[b]) // channels) for b in range(2)]
    half = n // 2
    geo = {
        "n": n, "half": half, "m": m, "q": q, "slab": slab, "pay_rows": pay_rows, "touched": touched,
        "iso_slab": iso_slab, "iso_q": iso_q,
        "aligned": q % 128 == 0,
    }
    geo["taps"] = 1 if geo["aligned"] else 2
    pay_shape = (n, sum(pay_rows), q)
    pay_outs = [(pay_shape, BF)] if geo["aligned"] else [((rows, channels), BF)] * 2

    def as_payload(parts):
        return parts[0] if geo["aligned"] else join_payload(geo, parts)

    def as_taps(payload):
        return [payload] if geo["aligned"] else split_payload(geo, payload, channels)

    def row(v):
        return v[None, :]

    lengths_row = lengths[0]
    count = lengths_row.shape[0]
    upto = jnp.arange(count)[None, :] <= jnp.arange(count)[:, None]
    ends = UNIT * jnp.sum(jnp.where(upto, lengths_row[None, :], 0), axis=1)
    starts = ends - UNIT * lengths_row

    def bounds(places):
        inside = (starts[None, :] <= places[:, None]) & (places[:, None] < ends[None, :])
        first = jnp.sum(jnp.where(inside, starts[None, :], 0), axis=1)
        return first, jnp.sum(jnp.where(inside, ends[None, :], 0), axis=1)

    base = me * rows
    local = jnp.arange(rows, dtype=I32)

    def info_of(places, anchors):
        first, last = bounds(anchors + base)
        shift = base - HALO
        return jnp.stack([places + HALO, first - shift, last - 1 - shift], axis=1)

    token_info = info_of(local, local)
    window_infos, step_starts = [], []
    for b in range(2):
        tap, step = local // m[b], local % m[b]
        anchor = SCALES[b] * step
        window_infos.append(info_of(anchor - SCALES[b] // 2 + tap, anchor))
        all_steps = jnp.arange(n * m[b], dtype=I32)
        step_starts.append((bounds(SCALES[b] * all_steps)[0] // SCALES[b])[:, None])

    replica = lax.axis_index("series")

    head_weights = (merge_weight, expand_weight, project_weight)
    head_rows = [w.shape[0] for w in head_weights]
    quarter_rows = [r // 4 for r in head_rows]
    geo["quarter_rows"] = quarter_rows
    geo["fits"] = all(r % 16 == 0 for r in quarter_rows)
    quarter = jnp.concatenate(
        [lax.dynamic_slice_in_dim(w, replica * r, r) for w, r in zip(head_weights, quarter_rows)], axis=0
    )
    stride_own = jnp.concatenate(stride_weights, axis=0)
    up_own = jnp.concatenate(up_weights, axis=0)

    devices = jnp.arange(n, dtype=I32)
    offset = jnp.asarray([[0, 2], [1, 3]], I32) ^ replica
    order = (4 * devices[None, :, None] + offset[:, None, :]).reshape(-1)
    iso_first = [(iso_slab[b] * me) // channels for b in range(2)]
    iso_offset = [iso_slab[b] * me - iso_first[b] * channels for b in range(2)]
    iso_wide = []
    for b in range(2):
        if touched[b] * channels == iso_slab[b]:
            iso_wide.append(iso_weights[b])
        else:
            blank = jnp.zeros((touched[b] * channels, channels), BF)
            iso_wide.append(lax.dynamic_update_slice(blank, iso_weights[b], (iso_offset[b], 0)))
    shifts = jnp.stack([*(TAPS[b] - 1 - iso_first[b] for b in range(2)), *iso_offset, replica & 1]).astype(I32)

    up_route, down_route = neighbours(n)
    tokens = inputs[0]
    step_block = [((n, sum(m), channels), BF)]
    own_steps = (sum(m), channels)
    left = lax.ppermute(tokens[rows - HALO :], "tm", up_route)
    right = lax.ppermute(tokens[:HALO], "tm", down_route)
    windows = kernel_call(
        functools.partial(windows_body, geo), pay_outs, (tokens, left, right, *window_infos), 24
    )
    windows = swap(as_payload(windows))
    (partial,) = kernel_call(
        functools.partial(slab_in_body, geo), step_block, (windows, stride_own), 24
    )
    partial = swap(partial)
    hidden_one, hidden_low = kernel_call(
        functools.partial(hidden_one_body, geo),
        [(own_steps, F32), ((n, *own_steps), BF)],
        (partial, jnp.stack([stride_bias_twelve, stride_bias_sixteen])),
        8,
    )
    blocks = lax.all_gather(quarter, "tm", axis=0)
    hidden_all, blocks = together(swap(hidden_low), blocks)
    (partial,) = kernel_call(
        functools.partial(iso_body, geo),
        step_block,
        (shifts, hidden_all, *step_starts, *iso_wide),
        32,
        scalars=(0,),
    )
    partial, blocks_a = together(swap(partial), across(blocks[:half], "series", 2))
    hidden_two, mixed_low = kernel_call(
        functools.partial(mix_body, geo),
        [(own_steps, F32), ((n, *own_steps), BF)],
        (
            partial,
            jnp.stack([isometric_bias_twelve, isometric_bias_sixteen]),
            hidden_one,
            row(mix_gain),
            row(mix_shift),
        ),
        8,
    )
    (season,) = kernel_call(
        season_body, [((2, rows, channels), F32)], (tokens, left, right, token_info), 24
    )
    mixed_all, season, blocks_b, blocks_core = together(
        swap(mixed_low), season, across(blocks[half:], "series", 2), across(blocks, "series", 1)
    )
    (ups,) = kernel_call(
        functools.partial(slab_out_body, geo), [(pay_shape, BF)], (mixed_all, up_own), 24
    )
    ups, core_a, core_b = together(
        swap(ups), across(blocks_a, "series", 1), across(blocks_b, "series", 1)
    )
    head_pieces = [blocks, blocks_a, blocks_b, blocks_core, core_a, core_b]
    geo["piece_starts"] = [(0, 0), (1, 0), (1, half), (2 * n, 0), (2 * n + 1, 0), (2 * n + 1, half)]
    geo["pieces"] = len(head_pieces)
    hidden_units = 4 * n * quarter_rows[1]
    head_args = [
        *as_taps(ups), season, cotangent[0], jnp.stack([upsample_bias_twelve, upsample_bias_sixteen]),
        row(mix_gain), row(mix_shift), row(merge_bias), row(feed_gain), row(feed_shift),
        row(expand_bias), row(project_bias), row(final_gain), row(final_shift),
    ]
    head_scratch = [pltpu.VMEM((hidden_units // FFN_CHUNK, rows, FFN_CHUNK), F32)]
    scalars = ()
    if geo["fits"]:
        scalars = (len(head_args),)
        head_args += [order, *head_pieces]
        head_scratch += [pltpu.VMEM((2 * channels, channels), BF)]
        head_scratch += [pltpu.VMEM((hidden_units, channels), BF)] * 2
    else:
        whole = [
            jnp.stack([own, jnp.concatenate(other)], axis=1)
            for own, *other in (head_pieces[:3], head_pieces[3:])
        ]
        whole = by_replica(jnp.stack(whole))
        whole = jnp.moveaxis(whole, 0, 2).reshape(4 * n, *blocks.shape[1:])
        cuts = [quarter_rows[0], sum(quarter_rows[:2])]
        head_args += [w.reshape(-1, channels) for w in jnp.split(whole, cuts, axis=1)]
    head = kernel_call(
        functools.partial(head_body, geo),
        [
            *pay_outs,
            ((rows, channels), BF),
            ((2, rows, channels), F32),
            ((rows, 2 * channels), BF),
            ((rows, channels), BF),
            ((rows, hidden_units), BF),
            ((rows, channels), BF),
            ((rows, hidden_units), BF),
            ((rows, channels), BF),
            ((10, channels), F32),
            ((1, hidden_units), F32),
        ],
        head_args,
        44,
        scalars=scalars,
        scratch=head_scratch,
    )
    d_ups, head = head[: geo["taps"]], head[geo["taps"] :]
    result, d_res, *head_lefts, head_sums, expand_sums = head
    merge_in, normed_low, activ_low, d_sum_low, d_pre_low, d_merged_low = head_lefts

    expand_sums = expand_sums.reshape(-1, channels)
    half_blocks = (2 * n, sum(quarter_rows) + SUM_ROWS, channels)
    if geo["fits"]:
        head_own, head_other = kernel_call(
            functools.partial(head_grad_body, geo),
            [(half_blocks, BF)] * 2,
            (*head_lefts, head_sums, expand_sums, order),
            28,
            scalars=(8,),
            scratch=[
                pltpu.VMEM((2 * channels, channels), BF),
                pltpu.VMEM((hidden_units, channels), BF),
            ],
        )
    else:
        whole = kernel_call(
            functools.partial(head_grad_body, geo), [((4 * r * n, channels), BF) for r in quarter_rows],
            head_lefts, 48,
        )
        whole = [jnp.moveaxis(g.reshape(n, 2, 2, -1, channels), 2, 0) for g in whole]
        whole = [by_replica(g).reshape(4 * n, -1, channels) for g in whole]
        extra = jnp.concatenate([head_sums, expand_sums], axis=0).astype(BF)
        extra = jnp.pad(extra, ((0, SUM_ROWS - extra.shape[0]), (0, 0)))
        whole.append(jnp.broadcast_to(extra, (4 * n, *extra.shape)))
        head_own, head_other = jnp.split(jnp.concatenate(whole, axis=1), 2)
    (residual,) = kernel_call(
        residual_body, [((rows + 2 * HALO, channels), F32)], (d_res, token_info), 24
    )
    d_ups, head_own, head_other, residual = together(
        swap(as_payload(d_ups)), head_own, head_other, residual
    )
    core = (replica & 1).reshape(1)

    def slab_grads(payload, steps):
        part = (sum(slab) // 2 + SUM_ROWS, channels)
        return kernel_call(
            functools.partial(slab_grad_body, geo),
            [(part, BF)] * 2,
            (core, payload, steps),
            24,
            scalars=(0,),
            scratch=[pltpu.VMEM((2, *part), BF)],
        )

    def cut(x):
        at = x.shape[0] * 2 // 48 * 16
        return x[:at], x[at:]

    (partial,) = kernel_call(
        functools.partial(slab_in_body, geo), step_block, (d_ups, up_own), 24
    )
    up_mine, up_sent = slab_grads(d_ups, mixed_all)
    partial, up_got, head_got, up_mine = together(
        swap(partial), across(up_sent, "series", 1), across(head_other, "series", 1), up_mine
    )
    d_pair, d_iso = kernel_call(
        functools.partial(mix_back_body, geo),
        [(own_steps, F32), ((n, sum(m) + 8, channels), BF)],
        (partial, hidden_one, hidden_two, row(mix_gain)),
        8,
    )
    up_part = summed(up_mine, up_got)
    head_sum = summed(after(head_own, d_iso), head_got).reshape(n, 2, *half_blocks[1:])
    head_sum = lax.psum_scatter(head_sum, "tm", scatter_dimension=0)
    d_iso_all, up_got = together(swap(d_iso), across(up_part, "series", 2))
    (partial,) = kernel_call(
        functools.partial(iso_back_body, geo),
        step_block,
        (shifts, d_iso_all, *step_starts, *iso_wide),
        32,
        scalars=(0,),
    )
    part = (sum(iso_slab) // 2 + SUM_ROWS, channels)
    iso_mine, iso_sent = kernel_call(
        functools.partial(iso_grad_body, geo),
        [(part, BF)] * 2,
        (shifts, hidden_all, d_iso_all, *step_starts),
        32,
        scalars=(0,),
        scratch=[
            *(pltpu.VMEM((touched[b] * channels, channels), F32) for b in range(2)),
            pltpu.VMEM((2, *part), BF),
        ],
    )
    up_part = summed(up_part, up_got)
    partial, iso_got, up_got, iso_mine = together(
        swap(partial),
        across(iso_sent, "series", 1),
        across(up_part, "series", 1),
        iso_mine,
    )
    (d_conv,) = kernel_call(
        functools.partial(conv_back_body, geo), [((n, *own_steps), BF)], (partial, d_pair, hidden_one), 8
    )
    iso_part = summed(iso_mine, iso_got)

    def grads_of(part, got, sizes):
        return kernel_call(
            join_body,
            [((size, channels), F32) for size in (*sizes, 2 * SUM_ROWS)],
            (core, part, got),
            24,
            scalars=(0,),
        )

    ups = grads_of(after(up_part, d_conv), up_got, slab)
    d_conv_all, iso_a, *ups = together(
        swap(d_conv), across(cut(iso_part)[0], "series", 2), *ups
    )
    (d_windows,) = kernel_call(
        functools.partial(slab_out_body, geo), [(pay_shape, BF)], (d_conv_all, stride_own), 24
    )
    stride_mine, stride_sent = slab_grads(windows, d_conv_all)
    stride_part = summed(stride_mine, across(stride_sent, "series", 1))
    d_windows, iso_b, stride_a = together(
        swap(d_windows),
        across(cut(iso_part)[1], "series", 2),
        across(cut(stride_part)[0], "series", 2),
    )
    edge = ((HALO, channels), F32)
    own, to_left, to_right = kernel_call(
        functools.partial(input_back_body, geo),
        [((rows, channels), F32), edge, edge],
        (*as_taps(d_windows), *window_infos, residual),
        24,
    )
    iso_part = summed(after(iso_part, own), jnp.concatenate([iso_a, iso_b]))
    from_right, from_left, stride_b, iso_got, head_got = together(
        lax.ppermute(to_left, "tm", down_route),
        lax.ppermute(to_right, "tm", up_route),
        across(cut(stride_part)[1], "series", 2),
        across(iso_part, "series", 1),
        across(head_sum[1], "series", 2),
    )
    input_grad = jnp.concatenate(
        [own[:HALO] + from_left, own[HALO : rows - HALO], own[rows - HALO :] + from_right], axis=0
    ).astype(BF)
    stride_part = summed(stride_part, jnp.concatenate([stride_a, stride_b]))
    stride_got = across(stride_part, "series", 1)
    head_mine = summed(head_sum[0], head_got)
    at = sum(quarter_rows)
    head_y = across(head_mine[:at], "series", 2)
    head_y = jnp.where(
        bit_of("series", 2) == 0, jnp.stack([head_mine[:at], head_y]), jnp.stack([head_y, head_mine[:at]])
    )
    head_got = across(head_y, "series", 1)
    head_grad = jnp.where(
        bit_of("series", 1) == 0, jnp.stack([head_y, head_got], axis=1), jnp.stack([head_got, head_y], axis=1)
    )
    head_grad = head_grad.reshape(4, *head_grad.shape[2:]).astype(F32)
    head_grads = [
        g.reshape(-1, channels)
        for g in jnp.split(head_grad, [quarter_rows[0], sum(quarter_rows[:2])], axis=1)
    ]
    sums = head_mine[at:].astype(F32)
    count = expand_bias.shape[0] // channels
    expand_grad = sums[10 : 10 + count].reshape(-1)

    strides = grads_of(stride_part, stride_got, slab)
    isos = grads_of(iso_part, iso_got, iso_slab)
    return (
        result[None],
        input_grad[None],
        strides[0], strides[2][0], isos[0], isos[2][0], ups[0], sums[8],
        strides[1], strides[2][1], isos[1], isos[2][1], ups[1], sums[9],
        isos[2][2] + sums[6], isos[2][3] + sums[7],
        head_grads[0], sums[5], sums[3], sums[4],
        head_grads[1], expand_grad, head_grads[2], sums[2], sums[0], sums[1],
    )


def solution(mesh):
    tokens, weight, whole = P("series", "tm", None), P("tm", None), P()
    pair = (weight, whole)
    return jax.shard_map(
        on_device,
        mesh=mesh,
        in_specs=(
            tokens, P("series", None), *(pair * 6), whole, whole, *pair, whole, whole, *pair, *pair, whole, whole,
            tokens,
        ),
        out_specs=(tokens, tokens, *(pair * 6), whole, whole, *pair, whole, whole, *pair, *pair, whole, whole),
        check_vma=False,
    )
```

time: 502 us -> 398 us (0.79)
  blocking collectives: 158 us -> 65.6 us
  waiting for transfers between devices: 192 us -> 116 us
  starting transfers between devices: 40.5 us -> 67.3 us
  local copies, waits for them, and re-layouts: 35.9 us -> 58.1 us
  Pallas kernels: 42.8 us -> 54.8 us
    psum x1 -> x0, waiting for transfers between devices: 52.8 us -> none  [on_device(): stride_grads = [lax.psum(g, 'series').astype(F32) for g in stride_grads]]
    ppermute x2 -> x22, waiting for transfers between devices: 4.45 us -> 57.1 us  [the longest x20 57.1 us: across(): lax.ppermute(x, axis, [(i, i ^ bit) for i in range(lax.axis_size(axis))])]
    psum x1 -> x0, blocking collectives: 44 us -> none  [on_device(): lax.psum(jnp.concatenate([conv_sums, mix_sums, head_sums, expand_sums.res...]
    all_to_all x2 -> x0, waiting for transfers between devices: 36.2 us -> none  [to_all(): return lax.all_to_all(jnp.broadcast_to(x[None], (n,) + x.shape), 'tm', 0, 0)]
    all_to_all x2 -> x0, blocking collectives: 30 us -> none  [to_all(): return lax.all_to_all(jnp.broadcast_to(x[None], (n,) + x.shape), 'tm', 0, 0)]
    all_to_all x5 -> x9, waiting for transfers between devices: 83 us -> 56.5 us  [swap(): return lax.all_to_all(x, 'tm', 0, 0)]
    unnamed x128 -> x170, local copies, waits for them, and re-layouts: 20.8 us -> 42 us
    all_to_all x5 -> x9, starting transfers between devices: 21.8 us -> 41.4 us  [swap(): return lax.all_to_all(x, 'tm', 0, 0)]
  transfers between devices with their start and end apart: 14 -> 35, of which waited for: 11 -> 15; matrix products, arithmetic and copies ran while one was open for 3% -> 8% of each run, Pallas kernels for 5% -> 7%
where the time goes in v2:
time: 398 us; the launch traced here: 395 us
  waiting for transfers between devices  116 us (29%)
  starting transfers between devices  67.3 us (17%)
  blocking collectives  65.6 us (16%)
  local copies, waits for them, and re-layouts  58.1 us (15%)
  Pallas kernels  54.8 us (14%)
  other arithmetic  18.5 us (5%)
  between operations  15.2 us (4%)
    all_to_all x3, blocking collectives, swap(): return lax.all_to_all(x, 'tm', 0, 0)  65.6 us
    ppermute x20, waiting for transfers between devices, across(): lax.ppermute(x, axis, [(i, i ^ bit) for i in range(lax.axis_size(axis))])  57.1 us
    all_to_all x9, waiting for transfers between devices, swap(): return lax.all_to_all(x, 'tm', 0, 0)  56.5 us
    pallas_call x22, Pallas kernels, kernel_call(): pl.pallas_call(body, out_shape=[jax.ShapeDtypeStruct(shape, dtype) for sh...  54.8 us
    unnamed x170, local copies, waits for them, and re-layouts  42 us
    all_to_all x9, starting transfers between devices, swap(): return lax.all_to_all(x, 'tm', 0, 0)  41.4 us
    ppermute x20, starting transfers between devices, across(): lax.ppermute(x, axis, [(i, i ^ bit) for i in range(lax.axis_size(axis))])  13.6 us
    convert_element_type x8, other arithmetic, summed(): return sum((p.astype(F32) for p in parts)).astype(BF)  12 us
  transfers between devices with their start and end apart: 35, of which 15 were waited for; matrix products, arithmetic and copies ran while one was open for 8% of the time, Pallas kernels for 7%

profile of v2, /device:TPU:0, one launch (start us, length us, event | category | flops | bytes accessed | tf_op | source)
XLA Modules:
  0.0 395.2 jit_solution(12353666682367650395)
XLA Ops:
  8.0 4.8 %collective-permute-start = (bf16[16,512]{1,0:T(8,128)(2,1)S(1)}, bf16[16,512]{1,0:T(8,128)(2,1)S(1)}, u32[]{:S(2)}, u32[]{:S(2)}) collective-permute-start(bf16[16,512]{1,0:T(8,128)(2,1)S(1)} %get-tuple-element.195), channel_id=1, source_target_pairs={{0,1},{1,2},{2,3},{3,4},{4,5},{5,6},{6,7},{8,9},{9,10},{10,11},{11... | collective-permute-start | bytes 49160 | tf_op jit(solution)/shard_map/ppermute | solution.py:646
  16.2 2.3 collective-permute-done.1.right
  19.5 2.9 shard_map.467
  22.4 5.8 %all-to-all-start = ((bf16[8,192,256]{2,1,0:T(8,128)(2,1)}), bf16[8,192,256]{2,1,0:T(8,128)(2,1)S(1)}, u32[]{:S(2)}, u32[]{:S(2)}) async-start(bf16[8,192,256]{2,1,0:T(8,128)(2,1)} %shard_map.467), calls=%async_computation | async-start | bytes 1572864 | tf_op jit(solution)/shard_map/all_to_all | solution.py:513
  32.3 17.0 %all-to-all-done.payload = bf16[8,192,256]{2,1,0:T(8,128)(2,1)S(1)} async-done(((bf16[8,192,256]{2,1,0:T(8,128)(2,1)}), bf16[8,192,256]{2,1,0:T(8,128)(2,1)S(1)}, u32[]{:S(2)}, u32[]{:S(2)}) %all-to-all-start) | async-done | bytes 786464 | tf_op jit(solution)/shard_map/all_to_all | solution.py:513
  50.7 3.5 all-to-all-start.1
  55.5 17.8 %all-to-all-done.1.parts = bf16[8,56,512]{2,1,0:T(8,128)(2,1)S(1)} async-done(((bf16[8,56,512]{2,1,0:T(8,128)(2,1)}), bf16[8,56,512]{2,1,0:T(8,128)(2,1)S(1)}, u32[]{:S(2)}, u32[]{:S(2)}) %all-to-all-start.1) | async-done | bytes 458784 | tf_op jit(solution)/shard_map/all_to_all | solution.py:513
  74.8 3.9 all-to-all-start.2
  80.7 8.1 %all-to-all-done.2.steps = bf16[8,56,512]{2,1,0:T(8,128)(2,1)S(1)} async-done(((bf16[8,56,512]{2,1,0:T(8,128)(2,1)}), bf16[8,56,512]{2,1,0:T(8,128)(2,1)S(1)}, u32[]{:S(2)}, u32[]{:S(2)}) %all-to-all-start.2) | async-done | bytes 458784 | tf_op jit(solution)/shard_map/all_to_all | solution.py:513
  93.5 4.3 %all-to-all-start.3 = ((bf16[8,56,512]{2,1,0:T(8,128)(2,1)}), bf16[8,56,512]{2,1,0:T(8,128)(2,1)}, u32[]{:S(2)}, u32[]{:S(2)}) async-start(bf16[8,56,512]{2,1,0:T(8,128)(2,1)} %copy-done.17), calls=%async_computation.3 | async-start | bytes 917504 | tf_op jit(solution)/shard_map/all_to_all | solution.py:513
  97.7 2.2 fusion.27
  101.8 12.8 %collective-permute-done.2.refs_15_ = bf16[4,160,512]{2,1,0:T(8,128)(2,1)} collective-permute-done((bf16[4,160,512]{2,1,0:T(8,128)(2,1)S(1)}, bf16[4,160,512]{2,1,0:T(8,128)(2,1)}, u32[]{:S(2)}, u32[]{:S(2)}) %collective-permute-start.2) | collective-permute-done | bytes 655392 | tf_op jit(solution)/shard_map/ppermute | solution.py:525
  118.2 5.7 %all-to-all-start.4 = ((bf16[8,56,512]{2,1,0:T(8,128)(2,1)}), bf16[8,56,512]{2,1,0:T(8,128)(2,1)}, u32[]{:S(2)}, u32[]{:S(2)}) async-start(bf16[8,56,512]{2,1,0:T(8,128)(2,1)} %copy-done.46), calls=%async_computation.4 | async-start | bytes 917504 | tf_op jit(solution)/shard_map/all_to_all | solution.py:513
  133.5 3.9 collective-permute-done.3.refs_16_
  141.6 5.7 %all-to-all-start.5 = ((bf16[8,192,256]{2,1,0:T(8,128)(2,1)}), bf16[8,192,256]{2,1,0:T(8,128)(2,1)}, u32[]{:S(2)}, u32[]{:S(2)}) async-start(bf16[8,192,256]{2,1,0:T(8,128)(2,1)} %copy-done.14), calls=%async_computation.5 | async-start | bytes 1572864 | tf_op jit(solution)/shard_map/all_to_all | solution.py:513
  150.7 12.5 %all-to-all-done.5.refs_0_ = bf16[8,192,256]{2,1,0:T(8,128)(2,1)} async-done(((bf16[8,192,256]{2,1,0:T(8,128)(2,1)}), bf16[8,192,256]{2,1,0:T(8,128)(2,1)}, u32[]{:S(2)}, u32[]{:S(2)}) %all-to-all-start.5) | async-done | bytes 786464 | tf_op jit(solution)/shard_map/all_to_all | solution.py:513
  166.2 16.6 %shard_map.474 = (bf16[8,192,256]{2,1,0:T(8,128)(2,1)S(1)}, bf16[384,512]{1,0:T(8,128)(2,1)}, f32[2,384,512]{2,1,0:T(8,128)}, bf16[384,1024]{1,0:T(8,128)(2,1)S(...) custom-call(bf16[8,192,256]{2,1,0:T(8,128)(2,1)} %all-to-all-done.5., ...), custom_call_target="tpu_custom_call" | custom-call | tf_op jit(solution)/shard_map/pallas_call | solution.py:42
  186.9 4.2 %all-to-all-start.6 = ((bf16[8,192,256]{2,1,0:T(8,128)(2,1)}), bf16[8,192,256]{2,1,0:T(8,128)(2,1)}, u32[]{:S(2)}, u32[]{:S(2)}) async-start(bf16[8,192,256]{2,1,0:T(8,128)(2,1)} %copy-done.41), calls=%async_computation.6 | async-start | bytes 1572864 | tf_op jit(solution)/shard_map/all_to_all | solution.py:513
  202.0 3.8 shard_map.475
  209.0 2.1 shard_map.478
  215.8 18.8 %all_to_all.60.parts = bf16[8,56,512]{2,1,0:T(8,128)(2,1)S(1)} all-to-all(bf16[8,56,512]{2,1,0:T(8,128)(2,1)S(1)} %shard_map.477), channel_id=1, replica_groups=mesh['series'=4,'tm'=8] {'tm'}, dimensions={0} | all-to-all | bytes 917504 | tf_op jit(solution)/shard_map/all_to_all | solution.py:513
  237.0 2.5 add_convert_fusion
  243.0 30.7 %all_to_all.61.d_iso = bf16[8,64,512]{2,1,0:T(8,128)(2,1)S(1)} all-to-all(bf16[8,64,512]{2,1,0:T(8,128)(2,1)S(1)} %copy-done.45), channel_id=1, replica_groups=mesh['series'=4,'tm'=8] {'tm'}, dimensions={0} | all-to-all | bytes 1048576 | tf_op jit(solution)/shard_map/all_to_all | solution.py:513
  274.2 2.3 shard_map.481
  278.7 16.1 %all_to_all.62.parts = bf16[8,56,512]{2,1,0:T(8,128)(2,1)S(1)} all-to-all(bf16[8,56,512]{2,1,0:T(8,128)(2,1)S(1)} %shard_map.480), channel_id=1, replica_groups=mesh['series'=4,'tm'=8] {'tm'}, dimensions={0} | all-to-all | bytes 917504 | tf_op jit(solution)/shard_map/all_to_all | solution.py:513
  297.5 3.7 all-to-all-start.10
  306.2 13.3 %collective-permute-done.12 = bf16[608,512]{1,0:T(8,128)(2,1)} collective-permute-done((bf16[608,512]{1,0:T(8,128)(2,1)S(1)}, bf16[608,512]{1,0:T(8,128)(2,1)}, u32[]{:S(2)}, u32[]{:S(2)}) %collective-permute-start.12) | collective-permute-done | bytes 622624 | tf_op jit(solution)/shard_map/ppermute | solution.py:525
  324.8 4.7 %all-to-all-start.11 = ((bf16[8,192,256]{2,1,0:T(8,128)(2,1)}), bf16[8,192,256]{2,1,0:T(8,128)(2,1)S(1)}, u32[]{:S(2)}, u32[]{:S(2)}) async-start(bf16[8,192,256]{2,1,0:T(8,128)(2,1)} %shard_map.484), calls=%async_computation.11 | async-start | bytes 1572864 | tf_op jit(solution)/shard_map/all_to_all | solution.py:513
  334.3 19.9 %collective-permute-done.13 = bf16[304,512]{1,0:T(8,128)(2,1)} collective-permute-done((bf16[304,512]{1,0:T(8,128)(2,1)S(1)}, bf16[304,512]{1,0:T(8,128)(2,1)}, u32[]{:S(2)}, u32[]{:S(2)}) %collective-permute-start.13) | collective-permute-done | bytes 311328 | tf_op jit(solution)/shard_map/ppermute | solution.py:525
  354.2 2.5 shard_map.486
  362.4 4.5 %collective-permute-start.17 = (f32[16,512]{1,0:T(8,128)S(1)}, f32[16,512]{1,0:T(8,128)S(1)}, u32[]{:S(2)}, u32[]{:S(2)}) collective-permute-start(f32[16,512]{1,0:T(8,128)S(1)} %copy-done.69), channel_id=1, source_target_pairs={{0,1},{1,2},{2,3},{3,4},{4,5},{5,6},{6,7},{8,9},{9,10},{10,11},{11... | collective-permute-start | bytes 98312 | tf_op jit(solution)/shard_map/ppermute | solution.py:874
  370.8 3.6 collective-permute-done.20
  (317 shorter events, 117.6 us)
Async XLA Ops:
  8.0 8.2 %collective-permute-start = (bf16[16,512]{1,0:T(8,128)(2,1)S(1)}, bf16[16,512]{1,0:T(8,128)(2,1)S(1)}, u32[]{:S(2)}, u32[]{:S(2)}) collective-permute-start(bf16[16,512]{1,0:T(8,128)(2,1)S(1)} %get-tuple-element.195), channel_id=1, source_target_pairs={{0,1},{1,2},{2,3},{3,4},{4,5},{5,6},{6,7},{8,9},{9,10},{10,11},{11... | collective-permute-start | bytes 49160 | tf_op jit(solution)/shard_map/ppermute | solution.py:646
  12.8 5.6 %collective-permute-start.1 = (bf16[16,512]{1,0:T(8,128)(2,1)S(1)}, bf16[16,512]{1,0:T(8,128)(2,1)S(1)}, u32[]{:S(2)}, u32[]{:S(2)}) collective-permute-start(bf16[16,512]{1,0:T(8,128)(2,1)S(1)} %get-tuple-element.194), channel_id=1, source_target_pairs={{1,0},{2,1},{3,2},{4,3},{5,4},{6,5},{7,6},{9,8},{10,9},{11,10},{12... | collective-permute-start | bytes 49160 | tf_op jit(solution)/shard_map/ppermute | solution.py:647
  22.4 27.0 %all-to-all-start = ((bf16[8,192,256]{2,1,0:T(8,128)(2,1)}), bf16[8,192,256]{2,1,0:T(8,128)(2,1)S(1)}, u32[]{:S(2)}, u32[]{:S(2)}) async-start(bf16[8,192,256]{2,1,0:T(8,128)(2,1)} %shard_map.467), calls=%async_computation | async-start | bytes 1572864 | tf_op jit(solution)/shard_map/all_to_all | solution.py:513
  28.1 52.6 %all-gather.3.cloned.1.call-start = ((), (), s32[]{:S(2)}) async-start(), calls=%async_computation.14 | async-start | bytes 1474560 | tf_op jit(solution)/shard_map/all_gather | solution.py:662
  50.7 22.6 %all-to-all-start.1 = ((bf16[8,56,512]{2,1,0:T(8,128)(2,1)}), bf16[8,56,512]{2,1,0:T(8,128)(2,1)S(1)}, u32[]{:S(2)}, u32[]{:S(2)}) async-start(bf16[8,56,512]{2,1,0:T(8,128)(2,1)} %shard_map.468), calls=%async_computation.1 | async-start | bytes 917504 | tf_op jit(solution)/shard_map/all_to_all | solution.py:513
  74.8 14.1 %all-to-all-start.2 = ((bf16[8,56,512]{2,1,0:T(8,128)(2,1)}), bf16[8,56,512]{2,1,0:T(8,128)(2,1)S(1)}, u32[]{:S(2)}, u32[]{:S(2)}) async-start(bf16[8,56,512]{2,1,0:T(8,128)(2,1)} %get-tuple-element.102), calls=%async_computation.2 | async-start | bytes 917504 | tf_op jit(solution)/shard_map/all_to_all | solution.py:513
  93.5 21.1 %all-to-all-start.3 = ((bf16[8,56,512]{2,1,0:T(8,128)(2,1)}), bf16[8,56,512]{2,1,0:T(8,128)(2,1)}, u32[]{:S(2)}, u32[]{:S(2)}) async-start(bf16[8,56,512]{2,1,0:T(8,128)(2,1)} %copy-done.17), calls=%async_computation.3 | async-start | bytes 917504 | tf_op jit(solution)/shard_map/all_to_all | solution.py:513
  100.0 14.7 %collective-permute-start.2 = (bf16[4,160,512]{2,1,0:T(8,128)(2,1)S(1)}, bf16[4,160,512]{2,1,0:T(8,128)(2,1)}, u32[]{:S(2)}, u32[]{:S(2)}) collective-permute-start(bf16[4,160,512]{2,1,0:T(8,128)(2,1)S(1)} %get-tuple-element.191), channel_id=1, source_target_pairs={{0,16},{8,24},{16,0},{24,8},{1,17},{9,25},{17,1},{25,9},{2,18},{10... | collective-permute-start | bytes 1966088 | tf_op jit(solution)/shard_map/ppermute | solution.py:525
  101.7 35.8 %collective-permute-start.4 = (bf16[8,160,512]{2,1,0:T(8,128)(2,1)}, bf16[8,160,512]{2,1,0:T(8,128)(2,1)}, u32[]{:S(2)}, u32[]{:S(2)}) collective-permute-start(bf16[8,160,512]{2,1,0:T(8,128)(2,1)} %bitcast.13.refs_14_), channel_id=1, source_target_pairs={{0,8},{8,0},{16,24},{24,16},{1,9},{9,1},{17,25},{25,17},{2,10},{10... | collective-permute-start | bytes 3932168 | tf_op jit(solution)/shard_map/ppermute | solution.py:525
  118.2 19.3 %all-to-all-start.4 = ((bf16[8,56,512]{2,1,0:T(8,128)(2,1)}), bf16[8,56,512]{2,1,0:T(8,128)(2,1)}, u32[]{:S(2)}, u32[]{:S(2)}) async-start(bf16[8,56,512]{2,1,0:T(8,128)(2,1)} %copy-done.46), calls=%async_computation.4 | async-start | bytes 917504 | tf_op jit(solution)/shard_map/all_to_all | solution.py:513
  124.0 13.5 %collective-permute-start.3 = (bf16[4,160,512]{2,1,0:T(8,128)(2,1)}, bf16[4,160,512]{2,1,0:T(8,128)(2,1)}, u32[]{:S(2)}, u32[]{:S(2)}) collective-permute-start(bf16[4,160,512]{2,1,0:T(8,128)(2,1)} %get-tuple-element.190), channel_id=1, source_target_pairs={{0,16},{8,24},{16,0},{24,8},{1,17},{9,25},{17,1},{25,9},{2,18},{10... | collective-permute-start | bytes 1966088 | tf_op jit(solution)/shard_map/ppermute | solution.py:525
  141.6 21.6 %all-to-all-start.5 = ((bf16[8,192,256]{2,1,0:T(8,128)(2,1)}), bf16[8,192,256]{2,1,0:T(8,128)(2,1)}, u32[]{:S(2)}, u32[]{:S(2)}) async-start(bf16[8,192,256]{2,1,0:T(8,128)(2,1)} %copy-done.14), calls=%async_computation.5 | async-start | bytes 1572864 | tf_op jit(solution)/shard_map/all_to_all | solution.py:513
  186.9 22.1 %all-to-all-start.6 = ((bf16[8,192,256]{2,1,0:T(8,128)(2,1)}), bf16[8,192,256]{2,1,0:T(8,128)(2,1)}, u32[]{:S(2)}, u32[]{:S(2)}) async-start(bf16[8,192,256]{2,1,0:T(8,128)(2,1)} %copy-done.41), calls=%async_computation.6 | async-start | bytes 1572864 | tf_op jit(solution)/shard_map/all_to_all | solution.py:513
  191.1 175.9 %reduce-scatter.2.cloned.1.call-start = ((), (), s32[]{:S(2)}) async-start(), calls=%async_computation.13 | async-start | bytes 3244032 | tf_op jit(solution)/shard_map/reduce_scatter | solution.py:808
  209.0 25.7 %collective-permute-start.8 = (bf16[16,176,512]{2,1,0:T(8,128)(2,1)}, bf16[16,176,512]{2,1,0:T(8,128)(2,1)S(1)}, u32[]{:S(2)}, u32[]{:S(2)}) collective-permute-start(bf16[16,176,512]{2,1,0:T(8,128)(2,1)} %copy-done.67), channel_id=1, source_target_pairs={{0,8},{8,0},{16,24},{24,16},{1,9},{9,1},{17,25},{25,17},{2,10},{10... | collective-permute-start | bytes 8650760 | tf_op jit(solution)/shard_map/ppermute | solution.py:525
  212.0 22.7 %collective-permute-start.7 = (bf16[912,512]{1,0:T(8,128)(2,1)S(1)}, bf16[912,512]{1,0:T(8,128)(2,1)S(1)}, u32[]{:S(2)}, u32[]{:S(2)}) collective-permute-start(bf16[912,512]{1,0:T(8,128)(2,1)S(1)} %get-tuple-element.130), channel_id=1, source_target_pairs={{0,8},{8,0},{16,24},{24,16},{1,9},{9,1},{17,25},{25,17},{2,10},{10... | collective-permute-start | bytes 2801672 | tf_op jit(solution)/shard_map/ppermute | solution.py:525
  241.3 32.5 %collective-permute-start.9 = (bf16[912,512]{1,0:T(8,128)(2,1)S(1)}, bf16[912,512]{1,0:T(8,128)(2,1)S(1)}, u32[]{:S(2)}, u32[]{:S(2)}) collective-permute-start(bf16[912,512]{1,0:T(8,128)(2,1)S(1)} %add_convert_fusion.6), channel_id=1, source_target_pairs={{0,16},{8,24},{16,0},{24,8},{1,17},{9,25},{17,1},{25,9},{2,18},{10... | collective-permute-start | bytes 2801672 | tf_op jit(solution)/shard_map/ppermute | solution.py:525
  274.1 20.7 %collective-permute-start.11 = (bf16[912,512]{1,0:T(8,128)(2,1)S(1)}, bf16[912,512]{1,0:T(8,128)(2,1)S(1)}, u32[]{:S(2)}, u32[]{:S(2)}) collective-permute-start(bf16[912,512]{1,0:T(8,128)(2,1)S(1)} %add_convert_fusion.5.part), channel_id=1, source_target_pairs={{0,8},{8,0},{16,24},{24,16},{1,9},{9,1},{17,25},{25,17},{2,10},{10... | collective-permute-start | bytes 2801672 | tf_op jit(solution)/shard_map/ppermute | solution.py:525
  276.5 19.2 %collective-permute-start.10 = (bf16[912,512]{1,0:T(8,128)(2,1)S(1)}, bf16[912,512]{1,0:T(8,128)(2,1)S(1)}, u32[]{:S(2)}, u32[]{:S(2)}) collective-permute-start(bf16[912,512]{1,0:T(8,128)(2,1)S(1)} %get-tuple-element.139), channel_id=1, source_target_pairs={{0,8},{8,0},{16,24},{24,16},{1,9},{9,1},{17,25},{25,17},{2,10},{10... | collective-permute-start | bytes 2801672 | tf_op jit(solution)/shard_map/ppermute | solution.py:525
  297.5 23.1 %all-to-all-start.10 = ((bf16[8,56,512]{2,1,0:T(8,128)(2,1)}), bf16[8,56,512]{2,1,0:T(8,128)(2,1)S(1)}, u32[]{:S(2)}, u32[]{:S(2)}) async-start(bf16[8,56,512]{2,1,0:T(8,128)(2,1)} %shard_map.482), calls=%async_computation.10 | async-start | bytes 917504 | tf_op jit(solution)/shard_map/all_to_all | solution.py:513
  304.1 15.4 %collective-permute-start.12 = (bf16[608,512]{1,0:T(8,128)(2,1)S(1)}, bf16[608,512]{1,0:T(8,128)(2,1)}, u32[]{:S(2)}, u32[]{:S(2)}) collective-permute-start(bf16[608,512]{1,0:T(8,128)(2,1)S(1)} %slice.141), channel_id=1, source_target_pairs={{0,16},{8,24},{16,0},{24,8},{1,17},{9,25},{17,1},{25,9},{2,18},{10... | collective-permute-start | bytes 1867784 | tf_op jit(solution)/shard_map/ppermute | solution.py:525
  323.2 6.3 %collective-permute-start.14 = (bf16[912,512]{1,0:T(8,128)(2,1)}, bf16[912,512]{1,0:T(8,128)(2,1)}, u32[]{:S(2)}, u32[]{:S(2)}) collective-permute-start(bf16[912,512]{1,0:T(8,128)(2,1)} %get-tuple-element.152), channel_id=1, source_target_pairs={{0,8},{8,0},{16,24},{24,16},{1,9},{9,1},{17,25},{25,17},{2,10},{10... | collective-permute-start | bytes 2801672 | tf_op jit(solution)/shard_map/ppermute | solution.py:525
  324.8 29.4 %all-to-all-start.11 = ((bf16[8,192,256]{2,1,0:T(8,128)(2,1)}), bf16[8,192,256]{2,1,0:T(8,128)(2,1)S(1)}, u32[]{:S(2)}, u32[]{:S(2)}) async-start(bf16[8,192,256]{2,1,0:T(8,128)(2,1)} %shard_map.484), calls=%async_computation.11 | async-start | bytes 1572864 | tf_op jit(solution)/shard_map/all_to_all | solution.py:513
  331.2 23.0 %collective-permute-start.15 = (bf16[608,512]{1,0:T(8,128)(2,1)S(1)}, bf16[608,512]{1,0:T(8,128)(2,1)}, u32[]{:S(2)}, u32[]{:S(2)}) collective-permute-start(bf16[608,512]{1,0:T(8,128)(2,1)S(1)} %slice.143), channel_id=1, source_target_pairs={{0,16},{8,24},{16,0},{24,8},{1,17},{9,25},{17,1},{25,9},{2,18},{10... | collective-permute-start | bytes 1867784 | tf_op jit(solution)/shard_map/ppermute | solution.py:525
  332.5 21.6 %collective-permute-start.13 = (bf16[304,512]{1,0:T(8,128)(2,1)S(1)}, bf16[304,512]{1,0:T(8,128)(2,1)}, u32[]{:S(2)}, u32[]{:S(2)}) collective-permute-start(bf16[304,512]{1,0:T(8,128)(2,1)S(1)} %slice.142), channel_id=1, source_target_pairs={{0,16},{8,24},{16,0},{24,8},{1,17},{9,25},{17,1},{25,9},{2,18},{10... | collective-permute-start | bytes 933896 | tf_op jit(solution)/shard_map/ppermute | solution.py:525
  359.6 11.2 %collective-permute-start.19 = (bf16[912,512]{1,0:T(8,128)(2,1)S(1)}, bf16[912,512]{1,0:T(8,128)(2,1)S(1)}, u32[]{:S(2)}, u32[]{:S(2)}) collective-permute-start(bf16[912,512]{1,0:T(8,128)(2,1)S(1)} %add_convert_fusion.2.part), channel_id=1, source_target_pairs={{0,8},{8,0},{16,24},{24,16},{1,9},{9,1},{17,25},{25,17},{2,10},{10... | collective-permute-start | bytes 2801672 | tf_op jit(solution)/shard_map/ppermute | solution.py:525
  360.7 10.1 %collective-permute-start.18 = (bf16[304,512]{1,0:T(8,128)(2,1)S(1)}, bf16[304,512]{1,0:T(8,128)(2,1)}, u32[]{:S(2)}, u32[]{:S(2)}) collective-permute-start(bf16[304,512]{1,0:T(8,128)(2,1)S(1)} %slice.144), channel_id=1, source_target_pairs={{0,16},{8,24},{16,0},{24,8},{1,17},{9,25},{17,1},{25,9},{2,18},{10... | collective-permute-start | bytes 933896 | tf_op jit(solution)/shard_map/ppermute | solution.py:525
  361.1 9.7 %collective-permute-start.16 = (f32[16,512]{1,0:T(8,128)S(1)}, f32[16,512]{1,0:T(8,128)S(1)}, u32[]{:S(2)}, u32[]{:S(2)}) collective-permute-start(f32[16,512]{1,0:T(8,128)S(1)} %copy-done.71), channel_id=1, source_target_pairs={{1,0},{2,1},{3,2},{4,3},{5,4},{6,5},{7,6},{9,8},{10,9},{11,10},{12... | collective-permute-start | bytes 98312 | tf_op jit(solution)/shard_map/ppermute | solution.py:873
  362.4 8.4 %collective-permute-start.17 = (f32[16,512]{1,0:T(8,128)S(1)}, f32[16,512]{1,0:T(8,128)S(1)}, u32[]{:S(2)}, u32[]{:S(2)}) collective-permute-start(f32[16,512]{1,0:T(8,128)S(1)} %copy-done.69), channel_id=1, source_target_pairs={{0,1},{1,2},{2,3},{3,4},{4,5},{5,6},{6,7},{8,9},{9,10},{10,11},{11... | collective-permute-start | bytes 98312 | tf_op jit(solution)/shard_map/ppermute | solution.py:874
  368.0 6.4 %collective-permute-start.20 = (bf16[176,512]{1,0:T(8,128)(2,1)S(1)}, bf16[176,512]{1,0:T(8,128)(2,1)S(1)}, u32[]{:S(2)}, u32[]{:S(2)}) collective-permute-start(bf16[176,512]{1,0:T(8,128)(2,1)S(1)} %slice_bitcast_fusion.1), channel_id=1, source_target_pairs={{0,16},{8,24},{16,0},{24,8},{1,17},{9,25},{17,1},{25,9},{2,18},{10... | collective-permute-start | bytes 540680 | tf_op jit(solution)/shard_map/ppermute | solution.py:525
  375.4 6.5 %collective-permute-start.22 = (bf16[160,512]{1,0:T(8,128)(2,1)S(1)}, bf16[160,512]{1,0:T(8,128)(2,1)S(1)}, u32[]{:S(2)}, u32[]{:S(2)}) collective-permute-start(bf16[160,512]{1,0:T(8,128)(2,1)S(1)} %get-tuple-element.198), channel_id=1, source_target_pairs={{0,16},{8,24},{16,0},{24,8},{1,17},{9,25},{17,1},{25,9},{2,18},{10... | collective-permute-start | bytes 491528 | tf_op jit(solution)/shard_map/ppermute | solution.py:525
  378.4 7.3 %collective-permute-start.21 = (bf16[912,512]{1,0:T(8,128)(2,1)S(1)}, bf16[912,512]{1,0:T(8,128)(2,1)S(1)}, u32[]{:S(2)}, u32[]{:S(2)}) collective-permute-start(bf16[912,512]{1,0:T(8,128)(2,1)S(1)} %add_convert_fusion.1.part), channel_id=1, source_target_pairs={{0,8},{8,0},{16,24},{24,16},{1,9},{9,1},{17,25},{25,17},{2,10},{10... | collective-permute-start | bytes 2801672 | tf_op jit(solution)/shard_map/ppermute | solution.py:525
  (86 other events, 659.7 us)
Sparse Core Ops, SparseCore 0:
  31.7 45.6 all-gather.2
  239.6 86.9 reduce-scatter.1

commit v3 on v2

--- a/solution.py
+++ b/solution.py
@@ -355,14 +355,15 @@
 
 def place_head(geo, order, pieces, merge, expand, project):
     m_rows, h_rows = geo["quarter_rows"][:2]
-    for first, begin, piece in pieces:
+    block = 0
+    for piece in pieces:
         for i in range(piece.shape[0]):
-            block = first + 2 * (begin + i)
             at = pl.multiple_of(order[block] * m_rows, m_rows)
             merge[pl.ds(at, m_rows), :] = piece[i, :m_rows, :]
             at = pl.ds(pl.multiple_of(order[block] * h_rows, h_rows), h_rows)
             expand[at, :] = piece[i, m_rows : m_rows + h_rows, :]
             project[at, :] = piece[i, m_rows + h_rows :, :]
+            block += 1
 
 
 def head_body(geo, *refs):
@@ -373,19 +374,18 @@
         expand_bias, project_bias, final_gain, final_shift,
     ) = refs[:12]
     refs = refs[12:]
+    grads = 2 if geo["fits"] else 3
     if geo["fits"]:
-        order, pieces, refs = refs[0], refs[1 : 1 + geo["pieces"]], refs[1 + geo["pieces"] :]
+        places, pieces, refs = refs[0], refs[1 : 1 + geo["pieces"]], refs[1 + geo["pieces"] :]
         merge_weight, expand_weight, project_weight = refs[-3:]
         refs = refs[:-3]
-        pieces = [(*at, piece) for at, piece in zip(geo["piece_starts"], pieces)]
-        place_head(geo, order, pieces, merge_weight, expand_weight, project_weight)
+        place_head(geo, places, pieces, merge_weight, expand_weight, project_weight)
     else:
         (merge_weight, expand_weight, project_weight), refs = refs[:3], refs[3:]
-    d_pays, outs = refs[:taps], refs[taps:]
-    (
-        result, d_res_out, merge_in, normed_out, activ_out, d_sum_out, d_pre_out, d_merged_out, sums, expand_sums,
-        slope,
-    ) = outs
+    d_pays, (result, d_res_out, sums), refs = refs[:taps], refs[taps : taps + 3], refs[taps + 3 :]
+    grad_outs, refs = refs[:grads], refs[grads:]
+    slope, merge_in, normed_out, activ_out, d_sum_out, d_pre_out, d_merged_out = refs
+    hidden_units = expand_weight.shape[0]
     rows, channels = cotangent.shape
     width = FFN_CHUNK
     chunks = expand_weight.shape[0] // width
@@ -426,7 +426,7 @@
     def backward_chunk(c, total):
         at = pl.ds(pl.multiple_of(c * width, width), width)
         d_pre = slope[c] * dot_nt(d_sum_out[...], project_weight[at, :])
-        expand_sums[:, at] = column_sum(d_pre)
+        sums[pl.ds(10 + c, 1), :] = column_sum(d_pre)
         d_pre_out[:, at] = d_pre.astype(BF)
         return total + dot(d_pre_out[:, at], expand_weight[at, :])
 
@@ -452,33 +452,27 @@
     sums[7:8, :] = shift_sum
     store_taps(geo, d_pays, d_taps)
 
-
-def head_grad_body(geo, *refs):
-    lefts = refs[:6]
-    merge_in, normed, activ, d_sum, d_pre, d_merged = lefts
-    pairs = ((merge_in, d_merged), (d_pre, normed), (activ, d_sum))
+    count = 10 + chunks
+    sums[count:, :] = jnp.zeros((SUM_ROWS - count, channels), F32)
+    pairs = ((merge_in, d_merged_out), (d_pre_out, normed_out), (activ_out, d_sum_out))
     if not geo["fits"]:
-        for out, (left, right) in zip(refs[6:], pairs):
+        for out, (left, right) in zip(grad_outs, pairs):
             out[...] = dot_tn(left[...], right[...]).astype(BF)
         return
-    sums, expand_sums, order, own, other, merge, hidden = refs[6:]
-    blocks, _, channels = own.shape
-    m_rows, h_rows = geo["quarter_rows"][:2]
-    at = m_rows + 2 * h_rows
-    count = sums.shape[0] + expand_sums.shape[0]
-    rows = jnp.concatenate(
-        [sums[...], expand_sums[...], jnp.zeros((SUM_ROWS - count, channels), F32)], axis=0
-    ).astype(BF)
     start = 0
-    for (left, right), grads, size in zip(pairs, (merge, hidden, hidden), (m_rows, h_rows, h_rows)):
-        grads[...] = dot_tn(left[...], right[...]).astype(BF)
-        for h, out in enumerate((own, other)):
+    for (left, right), grad, size in zip(
+        pairs, (merge_weight, expand_weight, project_weight), geo["quarter_rows"]
+    ):
+        grad[...] = dot_tn(left[...], right[...]).astype(BF)
+        for h, out in enumerate(grad_outs):
+            blocks = out.shape[0]
             for i in range(blocks):
-                begin = pl.multiple_of(order[h * blocks + i] * size, size)
-                out[i, start : start + size, :] = grads[pl.ds(begin, size), :]
+                begin = pl.multiple_of(places[h * blocks + i] * size, size)
+                out[i, start : start + size, :] = grad[pl.ds(begin, size), :]
         start += size
-    for out in (own, other):
-        out[:, at:, :] = jnp.broadcast_to(rows, (blocks, *rows.shape))
+    low = sums[...].astype(BF)
+    for out in grad_outs:
+        out[:, start:, :] = jnp.broadcast_to(low, (out.shape[0], *low.shape))
 
 
 def residual_body(d_res, info, out):
@@ -529,9 +523,29 @@
     return (lax.axis_index(axis) & bit) // bit
 
 
-def by_replica(x):
-    x = jnp.where(bit_of("series", 1) == 1, x[::-1], x)
-    return jnp.where(bit_of("series", 2) == 1, x[:, :, ::-1], x)
+def tm_bits():
+    return [1 << i for i in range(lax.axis_size("tm").bit_length() - 1)]
+
+
+def flipped(x):
+    bits = [("series", 1), ("series", 2)] + [("tm", b) for b in tm_bits()]
+    for at, (axis, bit) in enumerate(bits):
+        x = jnp.where(bit_of(axis, bit) == 1, jnp.flip(x, at), x)
+    return x
+
+
+def natural_rows(x):
+    bits = len(tm_bits())
+    x = flipped(x.reshape([2] * (bits + 2) + list(x.shape[1:])))
+    x = jnp.transpose(x, [*range(bits + 1, 1, -1), 1, 0, bits + 2, bits + 3])
+    return x.reshape(-1, x.shape[-1])
+
+
+def relative_blocks(x):
+    bits = len(tm_bits())
+    x = x.reshape([2] * (bits + 2) + [x.shape[0] >> (bits + 2), x.shape[1]])
+    x = jnp.transpose(x, [bits + 1, bits, *range(bits - 1, -1, -1), bits + 2, bits + 3])
+    return flipped(x).reshape(-1, *x.shape[-2:])
 
 
 def summed(*parts):
@@ -625,9 +639,14 @@
     stride_own = jnp.concatenate(stride_weights, axis=0)
     up_own = jnp.concatenate(up_weights, axis=0)
 
-    devices = jnp.arange(n, dtype=I32)
-    offset = jnp.asarray([[0, 2], [1, 3]], I32) ^ replica
-    order = (4 * devices[None, :, None] + offset[:, None, :]).reshape(-1)
+    far, bit = [0], half
+    while bit > 1:
+        far, bit = far + [o ^ bit for o in far], bit // 2
+    near = [o ^ 1 for o in far]
+    half_order = [(o, r) for r in (0, 2) for o in far + near]
+    relative = half_order + [(o, r ^ 1) for o, r in half_order]
+    order = jnp.stack([(me ^ o) * 4 + (replica ^ r) for o, r in relative]).astype(I32)
+
     iso_first = [(iso_slab[b] * me) // channels for b in range(2)]
     iso_offset = [iso_slab[b] * me - iso_first[b] * channels for b in range(2)]
     iso_wide = []
@@ -643,24 +662,40 @@
     tokens = inputs[0]
     step_block = [((n, sum(m), channels), BF)]
     own_steps = (sum(m), channels)
-    left = lax.ppermute(tokens[rows - HALO :], "tm", up_route)
-    right = lax.ppermute(tokens[:HALO], "tm", down_route)
+    blocks = quarter[None]
+    left, right, got = together(
+        lax.ppermute(tokens[rows - HALO :], "tm", up_route),
+        lax.ppermute(tokens[:HALO], "tm", down_route),
+        across(blocks, "tm", half),
+    )
+    blocks, bit = jnp.concatenate([blocks, got]), half // 2
+    while bit > 2:
+        blocks, bit = jnp.concatenate([blocks, across(blocks, "tm", bit)]), bit // 2
     windows = kernel_call(
         functools.partial(windows_body, geo), pay_outs, (tokens, left, right, *window_infos), 24
     )
-    windows = swap(as_payload(windows))
+    windows, got = together(swap(as_payload(windows)), across(blocks, "tm", bit))
+    blocks = jnp.concatenate([blocks, got])
+    middle = blocks.shape[0] // 2
     (partial,) = kernel_call(
         functools.partial(slab_in_body, geo), step_block, (windows, stride_own), 24
     )
-    partial = swap(partial)
+    low_blocks, high_blocks = blocks[:middle], blocks[middle:]
+    partial, x_low, y_high = together(
+        swap(partial), across(low_blocks, "tm", 1), across(high_blocks, "series", 2)
+    )
     hidden_one, hidden_low = kernel_call(
         functools.partial(hidden_one_body, geo),
         [(own_steps, F32), ((n, *own_steps), BF)],
         (partial, jnp.stack([stride_bias_twelve, stride_bias_sixteen])),
         8,
     )
-    blocks = lax.all_gather(quarter, "tm", axis=0)
-    hidden_all, blocks = together(swap(hidden_low), blocks)
+    hidden_all, x_high, y_low, blocks_core = together(
+        swap(hidden_low),
+        across(high_blocks, "tm", 1),
+        across(low_blocks, "series", 2),
+        across(blocks, "series", 1),
+    )
     (partial,) = kernel_call(
         functools.partial(iso_body, geo),
         step_block,
@@ -668,7 +703,13 @@
         32,
         scalars=(0,),
     )
-    partial, blocks_a = together(swap(partial), across(blocks[:half], "series", 2))
+    first = (x_low, x_high, y_low, y_high)
+    partial, blocks_a, blocks_b, *core_first = together(
+        swap(partial),
+        across(x_low, "series", 2),
+        across(y_high, "tm", 1),
+        *(across(f, "series", 1) for f in first),
+    )
     hidden_two, mixed_low = kernel_call(
         functools.partial(mix_body, geo),
         [(own_steps, F32), ((n, *own_steps), BF)],
@@ -684,17 +725,16 @@
     (season,) = kernel_call(
         season_body, [((2, rows, channels), F32)], (tokens, left, right, token_info), 24
     )
-    mixed_all, season, blocks_b, blocks_core = together(
-        swap(mixed_low), season, across(blocks[half:], "series", 2), across(blocks, "series", 1)
+    mixed_all, season, core_a, core_b = together(
+        swap(mixed_low), season, across(blocks_a, "series", 1), across(blocks_b, "series", 1)
     )
     (ups,) = kernel_call(
         functools.partial(slab_out_body, geo), [(pay_shape, BF)], (mixed_all, up_own), 24
     )
-    ups, core_a, core_b = together(
-        swap(ups), across(blocks_a, "series", 1), across(blocks_b, "series", 1)
-    )
-    head_pieces = [blocks, blocks_a, blocks_b, blocks_core, core_a, core_b]
-    geo["piece_starts"] = [(0, 0), (1, 0), (1, half), (2 * n, 0), (2 * n + 1, 0), (2 * n + 1, half)]
+    ups = swap(ups)
+    head_pieces = [
+        blocks, *first, blocks_a, blocks_b, blocks_core, *core_first, core_a, core_b,
+    ]
     geo["pieces"] = len(head_pieces)
     hidden_units = 4 * n * quarter_rows[1]
     head_args = [
@@ -702,7 +742,13 @@
         row(mix_gain), row(mix_shift), row(merge_bias), row(feed_gain), row(feed_shift),
         row(expand_bias), row(project_bias), row(final_gain), row(final_shift),
     ]
-    head_scratch = [pltpu.VMEM((hidden_units // FFN_CHUNK, rows, FFN_CHUNK), F32)]
+    head_scratch = [
+        pltpu.VMEM((hidden_units // FFN_CHUNK, rows, FFN_CHUNK), F32),
+        *(
+            pltpu.VMEM((rows, width), BF)
+            for width in (2 * channels, channels, hidden_units, channels, hidden_units, channels)
+        ),
+    ]
     scalars = ()
     if geo["fits"]:
         scalars = (len(head_args),)
@@ -710,69 +756,41 @@
         head_scratch += [pltpu.VMEM((2 * channels, channels), BF)]
         head_scratch += [pltpu.VMEM((hidden_units, channels), BF)] * 2
     else:
-        whole = [
-            jnp.stack([own, jnp.concatenate(other)], axis=1)
-            for own, *other in (head_pieces[:3], head_pieces[3:])
-        ]
-        whole = by_replica(jnp.stack(whole))
-        whole = jnp.moveaxis(whole, 0, 2).reshape(4 * n, *blocks.shape[1:])
         cuts = [quarter_rows[0], sum(quarter_rows[:2])]
-        head_args += [w.reshape(-1, channels) for w in jnp.split(whole, cuts, axis=1)]
+        head_args += [natural_rows(w) for w in jnp.split(jnp.concatenate(head_pieces), cuts, axis=1)]
+    half_blocks = (2 * n, sum(quarter_rows) + SUM_ROWS, channels)
     head = kernel_call(
         functools.partial(head_body, geo),
         [
             *pay_outs,
             ((rows, channels), BF),
             ((2, rows, channels), F32),
-            ((rows, 2 * channels), BF),
-            ((rows, channels), BF),
-            ((rows, hidden_units), BF),
-            ((rows, channels), BF),
-            ((rows, hidden_units), BF),
-            ((rows, channels), BF),
-            ((10, channels), F32),
-            ((1, hidden_units), F32),
+            ((SUM_ROWS, channels), F32),
+            *(
+                [(half_blocks, BF)] * 2
+                if geo["fits"]
+                else [((4 * r * n, channels), BF) for r in quarter_rows]
+            ),
         ],
         head_args,
-        44,
+        60,
         scalars=scalars,
         scratch=head_scratch,
     )
-    d_ups, head = head[: geo["taps"]], head[geo["taps"] :]
-    result, d_res, *head_lefts, head_sums, expand_sums = head
-    merge_in, normed_low, activ_low, d_sum_low, d_pre_low, d_merged_low = head_lefts
-
-    expand_sums = expand_sums.reshape(-1, channels)
-    half_blocks = (2 * n, sum(quarter_rows) + SUM_ROWS, channels)
+    d_ups, (result, d_res, head_sums, *head_grads) = head[: geo["taps"]], head[geo["taps"] :]
+
     if geo["fits"]:
-        head_own, head_other = kernel_call(
-            functools.partial(head_grad_body, geo),
-            [(half_blocks, BF)] * 2,
-            (*head_lefts, head_sums, expand_sums, order),
-            28,
-            scalars=(8,),
-            scratch=[
-                pltpu.VMEM((2 * channels, channels), BF),
-                pltpu.VMEM((hidden_units, channels), BF),
-            ],
-        )
+        head_own, head_other = head_grads
     else:
-        whole = kernel_call(
-            functools.partial(head_grad_body, geo), [((4 * r * n, channels), BF) for r in quarter_rows],
-            head_lefts, 48,
-        )
-        whole = [jnp.moveaxis(g.reshape(n, 2, 2, -1, channels), 2, 0) for g in whole]
-        whole = [by_replica(g).reshape(4 * n, -1, channels) for g in whole]
-        extra = jnp.concatenate([head_sums, expand_sums], axis=0).astype(BF)
-        extra = jnp.pad(extra, ((0, SUM_ROWS - extra.shape[0]), (0, 0)))
-        whole.append(jnp.broadcast_to(extra, (4 * n, *extra.shape)))
+        whole = [relative_blocks(g) for g in head_grads]
+        whole.append(jnp.broadcast_to(head_sums.astype(BF), (4 * n, *head_sums.shape)))
         head_own, head_other = jnp.split(jnp.concatenate(whole, axis=1), 2)
     (residual,) = kernel_call(
         residual_body, [((rows + 2 * HALO, channels), F32)], (d_res, token_info), 24
     )
-    d_ups, head_own, head_other, residual = together(
-        swap(as_payload(d_ups)), head_own, head_other, residual
-    )
+    head_sum = summed(head_own, across(head_other, "series", 1))
+    d_ups, head_sum, residual = together(swap(as_payload(d_ups)), head_sum, residual)
+    head_sum = head_sum.reshape(2, 2, 2, len(far) // 2, *half_blocks[1:])
     core = (replica & 1).reshape(1)
 
     def slab_grads(payload, steps):
@@ -786,16 +804,20 @@
             scratch=[pltpu.VMEM((2, *part), BF)],
         )
 
-    def cut(x):
-        at = x.shape[0] * 2 // 48 * 16
+    def cut(x, thirds=2):
+        at = x.shape[0] * thirds // 48 * 16
         return x[:at], x[at:]
 
     (partial,) = kernel_call(
         functools.partial(slab_in_body, geo), step_block, (d_ups, up_own), 24
     )
     up_mine, up_sent = slab_grads(d_ups, mixed_all)
-    partial, up_got, head_got, up_mine = together(
-        swap(partial), across(up_sent, "series", 1), across(head_other, "series", 1), up_mine
+    partial, x_1, y_1, up_mine, up_sent = together(
+        swap(partial),
+        across(head_sum[1, 1, 0], "tm", 1),
+        across(head_sum[1, 1, 1], "series", 2),
+        up_mine,
+        up_sent,
     )
     d_pair, d_iso = kernel_call(
         functools.partial(mix_back_body, geo),
@@ -803,10 +825,17 @@
         (partial, hidden_one, hidden_two, row(mix_gain)),
         8,
     )
-    up_part = summed(up_mine, up_got)
-    head_sum = summed(after(head_own, d_iso), head_got).reshape(n, 2, *half_blocks[1:])
-    head_sum = lax.psum_scatter(head_sum, "tm", scatter_dimension=0)
-    d_iso_all, up_got = together(swap(d_iso), across(up_part, "series", 2))
+    up_part = summed(up_mine, across(up_sent, "series", 1))
+    head_x = summed(head_sum[1, 0, 0], x_1)
+    head_y = summed(head_sum[0, 1, 1], y_1)
+    d_iso_all, up_part, x_0, y_0, head_x, head_y = together(
+        swap(d_iso),
+        up_part,
+        across(after(head_sum[0, 1, 0], d_iso), "tm", 1),
+        across(after(head_sum[1, 0, 1], d_iso), "series", 2),
+        head_x,
+        head_y,
+    )
     (partial,) = kernel_call(
         functools.partial(iso_back_body, geo),
         step_block,
@@ -826,17 +855,25 @@
             pltpu.VMEM((2, *part), BF),
         ],
     )
-    up_part = summed(up_part, up_got)
-    partial, iso_got, up_got, iso_mine = together(
-        swap(partial),
-        across(iso_sent, "series", 1),
-        across(up_part, "series", 1),
-        iso_mine,
+    head_sum = (
+        summed(head_sum[0, 0, 0], x_0, across(head_x, "series", 2)),
+        summed(head_sum[0, 0, 1], y_0, across(head_y, "tm", 1)),
+    )
+    up_low, up_high = cut(up_part, 1)
+    partial, iso_mine, iso_sent, up_a, *head_sum = together(
+        swap(partial), iso_mine, iso_sent, across(up_low, "series", 2), *head_sum
     )
     (d_conv,) = kernel_call(
         functools.partial(conv_back_body, geo), [((n, *own_steps), BF)], (partial, d_pair, hidden_one), 8
     )
-    iso_part = summed(iso_mine, iso_got)
+    iso_part = summed(after(iso_mine, d_conv), across(iso_sent, "series", 1))
+    head_sum, bit = summed(head_sum[0], across(after(head_sum[1], d_conv), "tm", 2)), 4
+    while bit < half:
+        head_sum, got = jnp.split(head_sum, 2)
+        head_sum, bit = summed(head_sum, across(got, "tm", bit)), 2 * bit
+    d_conv_all, up_b, head_sum, iso_part = together(
+        swap(d_conv), across(up_high, "series", 2), head_sum, iso_part
+    )
 
     def grads_of(part, got, sizes):
         return kernel_call(
@@ -847,19 +884,20 @@
             scalars=(0,),
         )
 
-    ups = grads_of(after(up_part, d_conv), up_got, slab)
-    d_conv_all, iso_a, *ups = together(
-        swap(d_conv), across(cut(iso_part)[0], "series", 2), *ups
-    )
     (d_windows,) = kernel_call(
         functools.partial(slab_out_body, geo), [(pay_shape, BF)], (d_conv_all, stride_own), 24
     )
     stride_mine, stride_sent = slab_grads(windows, d_conv_all)
     stride_part = summed(stride_mine, across(stride_sent, "series", 1))
-    d_windows, iso_b, stride_a = together(
+    at = sum(quarter_rows)
+    up_part = summed(after(up_part, d_windows), jnp.concatenate([up_a, up_b]))
+    iso_low, iso_high = cut(after(iso_part, d_windows))
+    d_windows, iso_a, stride_a, up_part, up_got = together(
         swap(d_windows),
-        across(cut(iso_part)[1], "series", 2),
-        across(cut(stride_part)[0], "series", 2),
+        across(iso_low, "series", 2),
+        across(cut(stride_part, 1)[0], "series", 2),
+        up_part,
+        across(up_part, "series", 1),
     )
     edge = ((HALO, channels), F32)
     own, to_left, to_right = kernel_call(
@@ -868,21 +906,22 @@
         (*as_taps(d_windows), *window_infos, residual),
         24,
     )
+    iso_b = across(iso_high, "series", 2)
     iso_part = summed(after(iso_part, own), jnp.concatenate([iso_a, iso_b]))
-    from_right, from_left, stride_b, iso_got, head_got = together(
+    head_mine = summed(head_sum[0], across(after(head_sum[1], own), "tm", half))
+    from_right, from_left, stride_b, iso_part, head_mine = together(
         lax.ppermute(to_left, "tm", down_route),
         lax.ppermute(to_right, "tm", up_route),
-        across(cut(stride_part)[1], "series", 2),
-        across(iso_part, "series", 1),
-        across(head_sum[1], "series", 2),
-    )
+        across(cut(stride_part, 1)[1], "series", 2),
+        iso_part,
+        head_mine,
+    )
+    ups = grads_of(after(up_part, own), up_got, slab)
     input_grad = jnp.concatenate(
         [own[:HALO] + from_left, own[HALO : rows - HALO], own[rows - HALO :] + from_right], axis=0
     ).astype(BF)
     stride_part = summed(stride_part, jnp.concatenate([stride_a, stride_b]))
-    stride_got = across(stride_part, "series", 1)
-    head_mine = summed(head_sum[0], head_got)
-    at = sum(quarter_rows)
+    stride_got, iso_got = across(stride_part, "series", 1), across(iso_part, "series", 1)
     head_y = across(head_mine[:at], "series", 2)
     head_y = jnp.where(
         bit_of("series", 2) == 0, jnp.stack([head_mine[:at], head_y]), jnp.stack([head_y, head_mine[:at]])

time: 398 us -> 383 us (0.962)
  blocking collectives: 65.6 us -> 0 us
  starting transfers between devices: 67.3 us -> 102 us
  waiting for transfers between devices: 116 us -> 135 us
  between operations: 15.2 us -> 1.75 us
  other arithmetic: 18.5 us -> 30.7 us
    all_to_all x3 -> x0, blocking collectives: 65.6 us -> none  [swap(): return lax.all_to_all(x, 'tm', 0, 0)]
    ppermute x20 -> x38, waiting for transfers between devices: 57.1 us -> 97.9 us  [across(): lax.ppermute(x, axis, [(i, i ^ bit) for i in range(lax.axis_size(axis))])]
    ppermute x20 -> x38, starting transfers between devices: 13.6 us -> 36.5 us  [across(): lax.ppermute(x, axis, [(i, i ^ bit) for i in range(lax.axis_size(axis))])]
    all_to_all x9 -> x12, waiting for transfers between devices: 56.5 us -> 34.3 us  [swap(): return lax.all_to_all(x, 'tm', 0, 0)]
    all_to_all x9 -> x12, starting transfers between devices: 41.4 us -> 54.6 us  [swap(): return lax.all_to_all(x, 'tm', 0, 0)]
    convert_element_type x8 -> x11, other arithmetic: 12 us -> 22.2 us  [summed(): return sum((p.astype(F32) for p in parts)).astype(BF)]
    unnamed x170 -> x148, local copies, waits for them, and re-layouts: 42 us -> 36.9 us
    slice x4 -> x6, local copies, waits for them, and re-layouts: 2.06 us -> 6.29 us  [cut(): return (x[:at], x[at:])]
  transfers between devices with their start and end apart: 35 -> 54, of which waited for: 15 -> 22; matrix products, arithmetic and copies ran while one was open for 8% -> 13% of each run, Pallas kernels for 7% -> 5%
where the time goes in v3:
time: 383 us; the launch traced here: 381 us
  waiting for transfers between devices  135 us (35%)
  starting transfers between devices  102 us (27%)
  Pallas kernels  55.8 us (15%)
  local copies, waits for them, and re-layouts  55.7 us (15%)
  other arithmetic  30.7 us (8%)
    ppermute x38, waiting for transfers between devices, across(): lax.ppermute(x, axis, [(i, i ^ bit) for i in range(lax.axis_size(axis))])  97.9 us
    pallas_call x21, Pallas kernels, kernel_call(): pl.pallas_call(body, out_shape=[jax.ShapeDtypeStruct(shape, dtype) for sh...  55.8 us
    all_to_all x12, starting transfers between devices, swap(): return lax.all_to_all(x, 'tm', 0, 0)  54.6 us
    unnamed x148, local copies, waits for them, and re-layouts  36.9 us
    ppermute x38, starting transfers between devices, across(): lax.ppermute(x, axis, [(i, i ^ bit) for i in range(lax.axis_size(axis))])  36.5 us
    all_to_all x12, waiting for transfers between devices, swap(): return lax.all_to_all(x, 'tm', 0, 0)  34.3 us
    convert_element_type x11, other arithmetic, summed(): return sum((p.astype(F32) for p in parts)).astype(BF)  22.2 us
  transfers between devices with their start and end apart: 54, of which 22 were waited for; matrix products, arithmetic and copies ran while one was open for 13% of the time, Pallas kernels for 5%

profile of v3, /device:TPU:0, one launch (start us, length us, event | category | flops | bytes accessed | tf_op | source)
XLA Modules:
  0.0 380.5 jit_solution(9951202546645348377)
XLA Ops:
  2.5 4.1 %collective-permute-start.2 = (bf16[1,160,512]{2,1,0:T(8,128)(2,1)S(1)}, bf16[1,160,512]{2,1,0:T(8,128)(2,1)S(1)}, u32[]{:S(2)}, u32[]{:S(2)}) collective-permute-start(bf16[1,160,512]{2,1,0:T(8,128)(2,1)S(1)} %maximum_bitcast_fusion), channel_id=1, source_target_pairs={{0,4},{1,5},{2,6},{3,7},{4,0},{5,1},{6,2},{7,3},{8,12},{9,13},{10,... | collective-permute-start | bytes 491528 | tf_op jit(solution)/shard_map/ppermute | solution.py:519
  7.3 3.4 collective-permute-start
  20.3 3.8 all-to-all-start
  28.3 18.1 %collective-permute-done.3 = bf16[2,160,512]{2,1,0:T(8,128)(2,1)} collective-permute-done((bf16[2,160,512]{2,1,0:T(8,128)(2,1)}, bf16[2,160,512]{2,1,0:T(8,128)(2,1)}, u32[]{:S(2)}, u32[]{:S(2)}) %collective-permute-start.3) | collective-permute-done | bytes 327712 | tf_op jit(solution)/shard_map/ppermute | solution.py:519
  47.7 4.5 %all-to-all-start.1 = ((bf16[8,56,512]{2,1,0:T(8,128)(2,1)}), bf16[8,56,512]{2,1,0:T(8,128)(2,1)S(1)}, u32[]{:S(2)}, u32[]{:S(2)}) async-start(bf16[8,56,512]{2,1,0:T(8,128)(2,1)} %shard_map.459), calls=%async_computation.1 | async-start | bytes 917504 | tf_op jit(solution)/shard_map/all_to_all | solution.py:507
  56.8 9.2 %collective-permute-done.4.refs_15_ = bf16[2,160,512]{2,1,0:T(8,128)(2,1)S(1)} collective-permute-done((bf16[2,160,512]{2,1,0:T(8,128)(2,1)}, bf16[2,160,512]{2,1,0:T(8,128)(2,1)S(1)}, u32[]{:S(2)}, u32[]{:S(2)}) %collective-permute-start.4) | collective-permute-done | bytes 327712 | tf_op jit(solution)/shard_map/ppermute | solution.py:519
  67.6 4.6 %all-to-all-start.2 = ((bf16[8,56,512]{2,1,0:T(8,128)(2,1)}), bf16[8,56,512]{2,1,0:T(8,128)(2,1)S(1)}, u32[]{:S(2)}, u32[]{:S(2)}) async-start(bf16[8,56,512]{2,1,0:T(8,128)(2,1)} %get-tuple-element.126), calls=%async_computation.2 | async-start | bytes 917504 | tf_op jit(solution)/shard_map/all_to_all | solution.py:507
  81.1 4.4 %collective-permute-done.7.refs_17_ = bf16[2,160,512]{2,1,0:T(8,128)(2,1)S(1)} collective-permute-done((bf16[2,160,512]{2,1,0:T(8,128)(2,1)}, bf16[2,160,512]{2,1,0:T(8,128)(2,1)S(1)}, u32[]{:S(2)}, u32[]{:S(2)}) %collective-permute-start.7) | collective-permute-done | bytes 327712 | tf_op jit(solution)/shard_map/ppermute | solution.py:519
  93.6 5.2 %all-to-all-start.3 = ((bf16[8,56,512]{2,1,0:T(8,128)(2,1)}), bf16[8,56,512]{2,1,0:T(8,128)(2,1)}, u32[]{:S(2)}, u32[]{:S(2)}) async-start(bf16[8,56,512]{2,1,0:T(8,128)(2,1)} %copy-done.15), calls=%async_computation.3 | async-start | bytes 917504 | tf_op jit(solution)/shard_map/all_to_all | solution.py:507
  101.9 10.9 %collective-permute-done.10.refs_20_ = bf16[2,160,512]{2,1,0:T(8,128)(2,1)S(1)} collective-permute-done((bf16[2,160,512]{2,1,0:T(8,128)(2,1)}, bf16[2,160,512]{2,1,0:T(8,128)(2,1)S(1)}, u32[]{:S(2)}, u32[]{:S(2)}) %collective-permute-start.10) | collective-permute-done | bytes 327712 | tf_op jit(solution)/shard_map/ppermute | solution.py:519
  118.4 4.5 %all-to-all-start.4 = ((bf16[8,56,512]{2,1,0:T(8,128)(2,1)}), bf16[8,56,512]{2,1,0:T(8,128)(2,1)S(1)}, u32[]{:S(2)}, u32[]{:S(2)}) async-start(bf16[8,56,512]{2,1,0:T(8,128)(2,1)} %copy-done.40), calls=%async_computation.4 | async-start | bytes 917504 | tf_op jit(solution)/shard_map/all_to_all | solution.py:507
  131.3 5.0 %all-to-all-done.4.steps = bf16[8,56,512]{2,1,0:T(8,128)(2,1)S(1)} async-done(((bf16[8,56,512]{2,1,0:T(8,128)(2,1)}), bf16[8,56,512]{2,1,0:T(8,128)(2,1)S(1)}, u32[]{:S(2)}, u32[]{:S(2)}) %all-to-all-start.4) | async-done | bytes 458784 | tf_op jit(solution)/shard_map/all_to_all | solution.py:507
  139.4 4.4 %all-to-all-start.5 = ((bf16[8,192,256]{2,1,0:T(8,128)(2,1)}), bf16[8,192,256]{2,1,0:T(8,128)(2,1)}, u32[]{:S(2)}, u32[]{:S(2)}) async-start(bf16[8,192,256]{2,1,0:T(8,128)(2,1)} %copy-done.14), calls=%async_computation.5 | async-start | bytes 1572864 | tf_op jit(solution)/shard_map/all_to_all | solution.py:507
  145.1 18.5 %all-to-all-done.5.refs_0_ = bf16[8,192,256]{2,1,0:T(8,128)(2,1)} async-done(((bf16[8,192,256]{2,1,0:T(8,128)(2,1)}), bf16[8,192,256]{2,1,0:T(8,128)(2,1)}, u32[]{:S(2)}, u32[]{:S(2)}) %all-to-all-start.5) | async-done | bytes 786464 | tf_op jit(solution)/shard_map/all_to_all | solution.py:507
  163.5 20.4 %shard_map.465 = (bf16[8,192,256]{2,1,0:T(8,128)(2,1)}, bf16[384,512]{1,0:T(8,128)(2,1)}, f32[2,384,512]{2,1,0:T(8,128)}, f32[16,512]{1,0:T(8,128)}, bf16[16,176...) custom-call(bf16[8,192,256]{2,1,0:T(8,128)(2,1)} %all-to-all-done.5.refs_0_, f32[2,384,512]{2,1,0:T(8,128)} %copy-done.7, ...), custom_call_target="tpu_custom_call" | custom-call | tf_op jit(solution)/shard_map/pallas_call | solution.py:42
  184.0 4.2 %all-to-all-start.6 = ((bf16[8,192,256]{2,1,0:T(8,128)(2,1)}), bf16[8,192,256]{2,1,0:T(8,128)(2,1)}, u32[]{:S(2)}, u32[]{:S(2)}) async-start(bf16[8,192,256]{2,1,0:T(8,128)(2,1)} %get-tuple-element.147), calls=%async_computation.6 | async-start | bytes 1572864 | tf_op jit(solution)/shard_map/all_to_all | solution.py:507
  193.3 5.2 %add_convert_fusion = bf16[16,176,512]{2,1,0:T(8,128)(2,1)} fusion(bf16[16,176,512]{2,1,0:T(8,128)(2,1)} %collective-permute-done.17, bf16[16,176,512]{2,1,0:T(8,128)(2,1)} %get-tuple-element.148), kind=kLoop, calls=%fused_computation | loop fusion | flops 5767168 | bytes 8650752 | tf_op jit(solution)/shard_map/convert_element_type | solution.py:552
  198.5 10.8 %all-to-all-done.6.payload = bf16[8,192,256]{2,1,0:T(8,128)(2,1)} async-done(((bf16[8,192,256]{2,1,0:T(8,128)(2,1)}), bf16[8,192,256]{2,1,0:T(8,128)(2,1)}, u32[]{:S(2)}, u32[]{:S(2)}) %all-to-all-start.6) | async-done | bytes 786464 | tf_op jit(solution)/shard_map/all_to_all | solution.py:507
  213.3 4.3 %all-to-all-start.7 = ((bf16[8,56,512]{2,1,0:T(8,128)(2,1)}), bf16[8,56,512]{2,1,0:T(8,128)(2,1)}, u32[]{:S(2)}, u32[]{:S(2)}) async-start(bf16[8,56,512]{2,1,0:T(8,128)(2,1)} %copy-done.17), calls=%async_computation.7 | async-start | bytes 917504 | tf_op jit(solution)/shard_map/all_to_all | solution.py:507
  225.9 7.3 %collective-permute-done.18 = bf16[2,176,512]{2,1,0:T(8,128)(2,1)} collective-permute-done((bf16[2,176,512]{2,1,0:T(8,128)(2,1)S(1)}, bf16[2,176,512]{2,1,0:T(8,128)(2,1)}, u32[]{:S(2)}, u32[]{:S(2)}) %collective-permute-start.18) | collective-permute-done | bytes 360480 | tf_op jit(solution)/shard_map/ppermute | solution.py:519
  237.8 4.4 %all-to-all-start.8 = ((bf16[8,64,512]{2,1,0:T(8,128)(2,1)}), bf16[8,64,512]{2,1,0:T(8,128)(2,1)S(1)}, u32[]{:S(2)}, u32[]{:S(2)}) async-start(bf16[8,64,512]{2,1,0:T(8,128)(2,1)} %copy-done.39), calls=%async_computation.8 | async-start | bytes 1048576 | tf_op jit(solution)/shard_map/all_to_all | solution.py:507
  249.4 3.6 collective-permute-done.22
  253.7 4.9 %collective-permute-done.21 = bf16[2,176,512]{2,1,0:T(8,128)(2,1)} collective-permute-done((bf16[2,176,512]{2,1,0:T(8,128)(2,1)}, bf16[2,176,512]{2,1,0:T(8,128)(2,1)}, u32[]{:S(2)}, u32[]{:S(2)}) %collective-permute-start.21) | collective-permute-done | bytes 360480 | tf_op jit(solution)/shard_map/ppermute | solution.py:519
  263.2 4.5 %all-to-all-start.9 = ((bf16[8,56,512]{2,1,0:T(8,128)(2,1)}), bf16[8,56,512]{2,1,0:T(8,128)(2,1)S(1)}, u32[]{:S(2)}, u32[]{:S(2)}) async-start(bf16[8,56,512]{2,1,0:T(8,128)(2,1)} %copy-done.16), calls=%async_computation.9 | async-start | bytes 917504 | tf_op jit(solution)/shard_map/all_to_all | solution.py:507
  289.2 4.3 %all-to-all-start.10 = ((bf16[8,56,512]{2,1,0:T(8,128)(2,1)}), bf16[8,56,512]{2,1,0:T(8,128)(2,1)S(1)}, u32[]{:S(2)}, u32[]{:S(2)}) async-start(bf16[8,56,512]{2,1,0:T(8,128)(2,1)} %shard_map.472), calls=%async_computation.10 | async-start | bytes 917504 | tf_op jit(solution)/shard_map/all_to_all | solution.py:507
  294.2 5.7 %collective-permute-done.27 = bf16[2,176,512]{2,1,0:T(8,128)(2,1)} collective-permute-done((bf16[2,176,512]{2,1,0:T(8,128)(2,1)}, bf16[2,176,512]{2,1,0:T(8,128)(2,1)}, u32[]{:S(2)}, u32[]{:S(2)}) %collective-permute-start.27) | collective-permute-done | bytes 360480 | tf_op jit(solution)/shard_map/ppermute | solution.py:519
  303.7 5.9 %collective-permute-done.26 = bf16[608,512]{1,0:T(8,128)(2,1)} collective-permute-done((bf16[608,512]{1,0:T(8,128)(2,1)S(1)}, bf16[608,512]{1,0:T(8,128)(2,1)}, u32[]{:S(2)}, u32[]{:S(2)}) %collective-permute-start.26) | collective-permute-done | bytes 622624 | tf_op jit(solution)/shard_map/ppermute | solution.py:519
  313.8 5.8 %all-to-all-start.11 = ((bf16[8,192,256]{2,1,0:T(8,128)(2,1)}), bf16[8,192,256]{2,1,0:T(8,128)(2,1)S(1)}, u32[]{:S(2)}, u32[]{:S(2)}) async-start(bf16[8,192,256]{2,1,0:T(8,128)(2,1)} %shard_map.473), calls=%async_computation.11 | async-start | bytes 1572864 | tf_op jit(solution)/shard_map/all_to_all | solution.py:507
  334.1 5.6 %collective-permute-done.29 = bf16[608,512]{1,0:T(8,128)(2,1)} collective-permute-done((bf16[608,512]{1,0:T(8,128)(2,1)}, bf16[608,512]{1,0:T(8,128)(2,1)}, u32[]{:S(2)}, u32[]{:S(2)}) %collective-permute-start.29) | collective-permute-done | bytes 622624 | tf_op jit(solution)/shard_map/ppermute | solution.py:519
  339.8 6.7 %collective-permute-done.31 = bf16[304,512]{1,0:T(8,128)(2,1)} collective-permute-done((bf16[304,512]{1,0:T(8,128)(2,1)}, bf16[304,512]{1,0:T(8,128)(2,1)}, u32[]{:S(2)}, u32[]{:S(2)}) %collective-permute-start.31) | collective-permute-done | bytes 311328 | tf_op jit(solution)/shard_map/ppermute | solution.py:519
  353.0 4.8 %collective-permute-start.34 = (f32[16,512]{1,0:T(8,128)S(1)}, f32[16,512]{1,0:T(8,128)S(1)}, u32[]{:S(2)}, u32[]{:S(2)}) collective-permute-start(f32[16,512]{1,0:T(8,128)S(1)} %get-tuple-element.192), channel_id=1, source_target_pairs={{0,1},{1,2},{2,3},{3,4},{4,5},{5,6},{6,7},{8,9},{9,10},{10,11},{11... | collective-permute-start | bytes 98312 | tf_op jit(solution)/shard_map/ppermute | solution.py:914
  359.3 3.3 shard_map.478
  (328 shorter events, 166.4 us)
Async XLA Ops:
  2.5 13.9 %collective-permute-start.2 = (bf16[1,160,512]{2,1,0:T(8,128)(2,1)S(1)}, bf16[1,160,512]{2,1,0:T(8,128)(2,1)S(1)}, u32[]{:S(2)}, u32[]{:S(2)}) collective-permute-start(bf16[1,160,512]{2,1,0:T(8,128)(2,1)S(1)} %maximum_bitcast_fusion), channel_id=1, source_target_pairs={{0,4},{1,5},{2,6},{3,7},{4,0},{5,1},{6,2},{7,3},{8,12},{9,13},{10,... | collective-permute-start | bytes 491528 | tf_op jit(solution)/shard_map/ppermute | solution.py:519
  20.3 26.0 %all-to-all-start = ((bf16[8,192,256]{2,1,0:T(8,128)(2,1)}), bf16[8,192,256]{2,1,0:T(8,128)(2,1)S(1)}, u32[]{:S(2)}, u32[]{:S(2)}) async-start(bf16[8,192,256]{2,1,0:T(8,128)(2,1)} %shard_map.458), calls=%async_computation | async-start | bytes 1572864 | tf_op jit(solution)/shard_map/all_to_all | solution.py:507
  24.9 21.5 %collective-permute-start.3 = (bf16[2,160,512]{2,1,0:T(8,128)(2,1)}, bf16[2,160,512]{2,1,0:T(8,128)(2,1)}, u32[]{:S(2)}, u32[]{:S(2)}) collective-permute-start(bf16[2,160,512]{2,1,0:T(8,128)(2,1)} %pad_maximum_fusion.2), channel_id=1, source_target_pairs={{0,2},{1,3},{2,0},{3,1},{4,6},{5,7},{6,4},{7,5},{8,10},{9,11},{10,... | collective-permute-start | bytes 983048 | tf_op jit(solution)/shard_map/ppermute | solution.py:519
  47.7 18.3 %all-to-all-start.1 = ((bf16[8,56,512]{2,1,0:T(8,128)(2,1)}), bf16[8,56,512]{2,1,0:T(8,128)(2,1)S(1)}, u32[]{:S(2)}, u32[]{:S(2)}) async-start(bf16[8,56,512]{2,1,0:T(8,128)(2,1)} %shard_map.459), calls=%async_computation.1 | async-start | bytes 917504 | tf_op jit(solution)/shard_map/all_to_all | solution.py:507
  53.2 12.8 %collective-permute-start.4 = (bf16[2,160,512]{2,1,0:T(8,128)(2,1)}, bf16[2,160,512]{2,1,0:T(8,128)(2,1)S(1)}, u32[]{:S(2)}, u32[]{:S(2)}) collective-permute-start(bf16[2,160,512]{2,1,0:T(8,128)(2,1)} %pad_maximum_fusion.2), channel_id=1, source_target_pairs={{0,1},{1,0},{2,3},{3,2},{4,5},{5,4},{6,7},{7,6},{8,9},{9,8},{10,11... | collective-permute-start | bytes 983048 | tf_op jit(solution)/shard_map/ppermute | solution.py:519
  67.6 21.4 %all-to-all-start.2 = ((bf16[8,56,512]{2,1,0:T(8,128)(2,1)}), bf16[8,56,512]{2,1,0:T(8,128)(2,1)S(1)}, u32[]{:S(2)}, u32[]{:S(2)}) async-start(bf16[8,56,512]{2,1,0:T(8,128)(2,1)} %get-tuple-element.126), calls=%async_computation.2 | async-start | bytes 917504 | tf_op jit(solution)/shard_map/all_to_all | solution.py:507
  74.2 14.8 %collective-permute-start.8 = (bf16[4,160,512]{2,1,0:T(8,128)(2,1)}, bf16[4,160,512]{2,1,0:T(8,128)(2,1)}, u32[]{:S(2)}, u32[]{:S(2)}) collective-permute-start(bf16[4,160,512]{2,1,0:T(8,128)(2,1)} %pad_maximum_fusion.refs_14_), channel_id=1, source_target_pairs={{0,8},{8,0},{16,24},{24,16},{1,9},{9,1},{17,25},{25,17},{2,10},{10... | collective-permute-start | bytes 1966088 | tf_op jit(solution)/shard_map/ppermute | solution.py:519
  93.6 21.2 %all-to-all-start.3 = ((bf16[8,56,512]{2,1,0:T(8,128)(2,1)}), bf16[8,56,512]{2,1,0:T(8,128)(2,1)}, u32[]{:S(2)}, u32[]{:S(2)}) async-start(bf16[8,56,512]{2,1,0:T(8,128)(2,1)} %copy-done.15), calls=%async_computation.3 | async-start | bytes 917504 | tf_op jit(solution)/shard_map/all_to_all | solution.py:507
  98.8 14.0 %collective-permute-start.10 = (bf16[2,160,512]{2,1,0:T(8,128)(2,1)}, bf16[2,160,512]{2,1,0:T(8,128)(2,1)S(1)}, u32[]{:S(2)}, u32[]{:S(2)}) collective-permute-start(bf16[2,160,512]{2,1,0:T(8,128)(2,1)} %copy-done.61), channel_id=1, source_target_pairs={{0,1},{1,0},{2,3},{3,2},{4,5},{5,4},{6,7},{7,6},{8,9},{9,8},{10,11... | collective-permute-start | bytes 983048 | tf_op jit(solution)/shard_map/ppermute | solution.py:519
  100.8 12.7 %collective-permute-start.14 = (bf16[2,160,512]{2,1,0:T(8,128)(2,1)}, bf16[2,160,512]{2,1,0:T(8,128)(2,1)}, u32[]{:S(2)}, u32[]{:S(2)}) collective-permute-start(bf16[2,160,512]{2,1,0:T(8,128)(2,1)} %copy-done.61), channel_id=1, source_target_pairs={{0,8},{8,0},{16,24},{24,16},{1,9},{9,1},{17,25},{25,17},{2,10},{10... | collective-permute-start | bytes 983048 | tf_op jit(solution)/shard_map/ppermute | solution.py:519
  100.8 12.7 %collective-permute-start.11 = (bf16[2,160,512]{2,1,0:T(8,128)(2,1)}, bf16[2,160,512]{2,1,0:T(8,128)(2,1)}, u32[]{:S(2)}, u32[]{:S(2)}) collective-permute-start(bf16[2,160,512]{2,1,0:T(8,128)(2,1)} %copy-done.60), channel_id=1, source_target_pairs={{0,8},{8,0},{16,24},{24,16},{1,9},{9,1},{17,25},{25,17},{2,10},{10... | collective-permute-start | bytes 983048 | tf_op jit(solution)/shard_map/ppermute | solution.py:519
  118.4 17.9 %all-to-all-start.4 = ((bf16[8,56,512]{2,1,0:T(8,128)(2,1)}), bf16[8,56,512]{2,1,0:T(8,128)(2,1)S(1)}, u32[]{:S(2)}, u32[]{:S(2)}) async-start(bf16[8,56,512]{2,1,0:T(8,128)(2,1)} %copy-done.40), calls=%async_computation.4 | async-start | bytes 917504 | tf_op jit(solution)/shard_map/all_to_all | solution.py:507
  139.4 24.2 %all-to-all-start.5 = ((bf16[8,192,256]{2,1,0:T(8,128)(2,1)}), bf16[8,192,256]{2,1,0:T(8,128)(2,1)}, u32[]{:S(2)}, u32[]{:S(2)}) async-start(bf16[8,192,256]{2,1,0:T(8,128)(2,1)} %copy-done.14), calls=%async_computation.5 | async-start | bytes 1572864 | tf_op jit(solution)/shard_map/all_to_all | solution.py:507
  184.0 25.3 %all-to-all-start.6 = ((bf16[8,192,256]{2,1,0:T(8,128)(2,1)}), bf16[8,192,256]{2,1,0:T(8,128)(2,1)}, u32[]{:S(2)}, u32[]{:S(2)}) async-start(bf16[8,192,256]{2,1,0:T(8,128)(2,1)} %get-tuple-element.147), calls=%async_computation.6 | async-start | bytes 1572864 | tf_op jit(solution)/shard_map/all_to_all | solution.py:507
  213.3 19.9 %all-to-all-start.7 = ((bf16[8,56,512]{2,1,0:T(8,128)(2,1)}), bf16[8,56,512]{2,1,0:T(8,128)(2,1)}, u32[]{:S(2)}, u32[]{:S(2)}) async-start(bf16[8,56,512]{2,1,0:T(8,128)(2,1)} %copy-done.17), calls=%async_computation.7 | async-start | bytes 917504 | tf_op jit(solution)/shard_map/all_to_all | solution.py:507
  219.9 13.3 %collective-permute-start.18 = (bf16[2,176,512]{2,1,0:T(8,128)(2,1)S(1)}, bf16[2,176,512]{2,1,0:T(8,128)(2,1)}, u32[]{:S(2)}, u32[]{:S(2)}) collective-permute-start(bf16[2,176,512]{2,1,0:T(8,128)(2,1)S(1)} %get-tuple-element.231), channel_id=1, source_target_pairs={{0,1},{1,0},{2,3},{3,2},{4,5},{5,4},{6,7},{7,6},{8,9},{9,8},{10,11... | collective-permute-start | bytes 1081352 | tf_op jit(solution)/shard_map/ppermute | solution.py:519
  233.2 13.9 %collective-permute-start.20 = (bf16[912,512]{1,0:T(8,128)(2,1)}, bf16[912,512]{1,0:T(8,128)(2,1)}, u32[]{:S(2)}, u32[]{:S(2)}) collective-permute-start(bf16[912,512]{1,0:T(8,128)(2,1)} %copy-done.49), channel_id=1, source_target_pairs={{0,8},{8,0},{16,24},{24,16},{1,9},{9,1},{17,25},{25,17},{2,10},{10... | collective-permute-start | bytes 2801672 | tf_op jit(solution)/shard_map/ppermute | solution.py:519
  237.8 20.9 %all-to-all-start.8 = ((bf16[8,64,512]{2,1,0:T(8,128)(2,1)}), bf16[8,64,512]{2,1,0:T(8,128)(2,1)S(1)}, u32[]{:S(2)}, u32[]{:S(2)}) async-start(bf16[8,64,512]{2,1,0:T(8,128)(2,1)} %copy-done.39), calls=%async_computation.8 | async-start | bytes 1048576 | tf_op jit(solution)/shard_map/all_to_all | solution.py:507
  242.7 15.9 %collective-permute-start.21 = (bf16[2,176,512]{2,1,0:T(8,128)(2,1)}, bf16[2,176,512]{2,1,0:T(8,128)(2,1)}, u32[]{:S(2)}, u32[]{:S(2)}) collective-permute-start(bf16[2,176,512]{2,1,0:T(8,128)(2,1)} %get-tuple-element.160), channel_id=1, source_target_pairs={{0,1},{1,0},{2,3},{3,2},{4,5},{5,4},{6,7},{7,6},{8,9},{9,8},{10,11... | collective-permute-start | bytes 1081352 | tf_op jit(solution)/shard_map/ppermute | solution.py:519
  263.2 21.8 %all-to-all-start.9 = ((bf16[8,56,512]{2,1,0:T(8,128)(2,1)}), bf16[8,56,512]{2,1,0:T(8,128)(2,1)S(1)}, u32[]{:S(2)}, u32[]{:S(2)}) async-start(bf16[8,56,512]{2,1,0:T(8,128)(2,1)} %copy-done.16), calls=%async_computation.9 | async-start | bytes 917504 | tf_op jit(solution)/shard_map/all_to_all | solution.py:507
  268.3 14.4 %collective-permute-start.25 = (bf16[2,176,512]{2,1,0:T(8,128)(2,1)}, bf16[2,176,512]{2,1,0:T(8,128)(2,1)S(1)}, u32[]{:S(2)}, u32[]{:S(2)}) collective-permute-start(bf16[2,176,512]{2,1,0:T(8,128)(2,1)} %get-tuple-element.171), channel_id=1, source_target_pairs={{0,1},{1,0},{2,3},{3,2},{4,5},{5,4},{6,7},{7,6},{8,9},{9,8},{10,11... | collective-permute-start | bytes 1081352 | tf_op jit(solution)/shard_map/ppermute | solution.py:519
  271.2 13.8 %collective-permute-start.23 = (bf16[304,512]{1,0:T(8,128)(2,1)S(1)}, bf16[304,512]{1,0:T(8,128)(2,1)}, u32[]{:S(2)}, u32[]{:S(2)}) collective-permute-start(bf16[304,512]{1,0:T(8,128)(2,1)S(1)} %slice.139), channel_id=1, source_target_pairs={{0,16},{8,24},{16,0},{24,8},{1,17},{9,25},{17,1},{25,9},{2,18},{10... | collective-permute-start | bytes 933896 | tf_op jit(solution)/shard_map/ppermute | solution.py:519
  285.0 16.1 %collective-permute-start.28 = (bf16[912,512]{1,0:T(8,128)(2,1)}, bf16[912,512]{1,0:T(8,128)(2,1)}, u32[]{:S(2)}, u32[]{:S(2)}) collective-permute-start(bf16[912,512]{1,0:T(8,128)(2,1)} %copy-done.48), channel_id=1, source_target_pairs={{0,8},{8,0},{16,24},{24,16},{1,9},{9,1},{17,25},{25,17},{2,10},{10... | collective-permute-start | bytes 2801672 | tf_op jit(solution)/shard_map/ppermute | solution.py:519
  289.2 20.4 %all-to-all-start.10 = ((bf16[8,56,512]{2,1,0:T(8,128)(2,1)}), bf16[8,56,512]{2,1,0:T(8,128)(2,1)S(1)}, u32[]{:S(2)}, u32[]{:S(2)}) async-start(bf16[8,56,512]{2,1,0:T(8,128)(2,1)} %shard_map.472), calls=%async_computation.10 | async-start | bytes 917504 | tf_op jit(solution)/shard_map/all_to_all | solution.py:507
  293.5 16.1 %collective-permute-start.26 = (bf16[608,512]{1,0:T(8,128)(2,1)S(1)}, bf16[608,512]{1,0:T(8,128)(2,1)}, u32[]{:S(2)}, u32[]{:S(2)}) collective-permute-start(bf16[608,512]{1,0:T(8,128)(2,1)S(1)} %slice.142), channel_id=1, source_target_pairs={{0,16},{8,24},{16,0},{24,8},{1,17},{9,25},{17,1},{25,9},{2,18},{10... | collective-permute-start | bytes 1867784 | tf_op jit(solution)/shard_map/ppermute | solution.py:519
  313.8 32.6 %all-to-all-start.11 = ((bf16[8,192,256]{2,1,0:T(8,128)(2,1)}), bf16[8,192,256]{2,1,0:T(8,128)(2,1)S(1)}, u32[]{:S(2)}, u32[]{:S(2)}) async-start(bf16[8,192,256]{2,1,0:T(8,128)(2,1)} %shard_map.473), calls=%async_computation.11 | async-start | bytes 1572864 | tf_op jit(solution)/shard_map/all_to_all | solution.py:507
  321.4 18.3 %collective-permute-start.32 = (bf16[912,512]{1,0:T(8,128)(2,1)S(1)}, bf16[912,512]{1,0:T(8,128)(2,1)}, u32[]{:S(2)}, u32[]{:S(2)}) collective-permute-start(bf16[912,512]{1,0:T(8,128)(2,1)S(1)} %add_convert_fusion.3.part), channel_id=1, source_target_pairs={{0,8},{8,0},{16,24},{24,16},{1,9},{9,1},{17,25},{25,17},{2,10},{10... | collective-permute-start | bytes 2801672 | tf_op jit(solution)/shard_map/ppermute | solution.py:519
  322.6 17.2 %collective-permute-start.29 = (bf16[608,512]{1,0:T(8,128)(2,1)}, bf16[608,512]{1,0:T(8,128)(2,1)}, u32[]{:S(2)}, u32[]{:S(2)}) collective-permute-start(bf16[608,512]{1,0:T(8,128)(2,1)} %slice.143), channel_id=1, source_target_pairs={{0,16},{8,24},{16,0},{24,8},{1,17},{9,25},{17,1},{25,9},{2,18},{10... | collective-permute-start | bytes 1867784 | tf_op jit(solution)/shard_map/ppermute | solution.py:519
  326.5 19.9 %collective-permute-start.31 = (bf16[304,512]{1,0:T(8,128)(2,1)}, bf16[304,512]{1,0:T(8,128)(2,1)}, u32[]{:S(2)}, u32[]{:S(2)}) collective-permute-start(bf16[304,512]{1,0:T(8,128)(2,1)} %slice.179), channel_id=1, source_target_pairs={{0,16},{8,24},{16,0},{24,8},{1,17},{9,25},{17,1},{25,9},{2,18},{10... | collective-permute-start | bytes 933896 | tf_op jit(solution)/shard_map/ppermute | solution.py:519
  329.5 28.4 %collective-permute-start.36 = (bf16[304,512]{1,0:T(8,128)(2,1)}, bf16[304,512]{1,0:T(8,128)(2,1)}, u32[]{:S(2)}, u32[]{:S(2)}) collective-permute-start(bf16[304,512]{1,0:T(8,128)(2,1)} %slice.147), channel_id=1, source_target_pairs={{0,16},{8,24},{16,0},{24,8},{1,17},{9,25},{17,1},{25,9},{2,18},{10... | collective-permute-start | bytes 933896 | tf_op jit(solution)/shard_map/ppermute | solution.py:519
  332.9 32.9 %collective-permute-start.35 = (bf16[608,512]{1,0:T(8,128)(2,1)}, bf16[608,512]{1,0:T(8,128)(2,1)}, u32[]{:S(2)}, u32[]{:S(2)}) collective-permute-start(bf16[608,512]{1,0:T(8,128)(2,1)} %slice.180), channel_id=1, source_target_pairs={{0,16},{8,24},{16,0},{24,8},{1,17},{9,25},{17,1},{25,9},{2,18},{10... | collective-permute-start | bytes 1867784 | tf_op jit(solution)/shard_map/ppermute | solution.py:519
  349.0 13.7 %collective-permute-start.37 = (bf16[176,512]{1,0:T(8,128)(2,1)S(1)}, bf16[176,512]{1,0:T(8,128)(2,1)S(1)}, u32[]{:S(2)}, u32[]{:S(2)}) collective-permute-start(bf16[176,512]{1,0:T(8,128)(2,1)S(1)} %copy-done.65), channel_id=1, source_target_pairs={{0,4},{1,5},{2,6},{3,7},{4,0},{5,1},{6,2},{7,3},{8,12},{9,13},{10,... | collective-permute-start | bytes 540680 | tf_op jit(solution)/shard_map/ppermute | solution.py:519
  (94 other events, 730.0 us)

commit v4 on v3

--- a/solution.py
+++ b/solution.py
@@ -162,12 +162,15 @@
     return [t.astype(BF) for t in split_payload(geo, whole, channels)]
 
 
-def windows_body(geo, tok, left, right, info_one, info_two, *outs):
+def matrices_body(info_one, info_two, matrices, orders):
+    for b, info in enumerate((info_one, info_two)):
+        matrices[b] = season_matrix(info[...], AVERAGES[b], matrices.shape[2])
+        orders[b] = token_order(orders.shape[1], SCALES[b])
+
+
+def windows_body(geo, tok, left, right, matrices, *outs):
     x = jnp.concatenate([left[...], tok[...], right[...]], axis=0)
-    parts = []
-    for b, info in enumerate((info_one, info_two)):
-        matrix = season_matrix(info[...], AVERAGES[b], x.shape[0])
-        parts.append(dot(matrix, x) * (1.0 / AVERAGES[b]))
+    parts = [dot(matrices[b], x) * (1.0 / AVERAGES[b]) for b in range(2)]
     store_taps(geo, outs, parts)
 
 
@@ -371,9 +374,9 @@
     pays, refs = refs[:taps], refs[taps:]
     (
         season, cotangent, up_bias, mix_gain, mix_shift, merge_bias, feed_gain, feed_shift,
-        expand_bias, project_bias, final_gain, final_shift,
-    ) = refs[:12]
-    refs = refs[12:]
+        expand_bias, project_bias, final_gain, final_shift, orders,
+    ) = refs[:13]
+    refs = refs[13:]
     grads = 2 if geo["fits"] else 3
     if geo["fits"]:
         places, pieces, refs = refs[0], refs[1 : 1 + geo["pieces"]], refs[1 + geo["pieces"] :]
@@ -392,8 +395,7 @@
     taps = load_taps(geo, pays, channels)
     ups, kept = [], []
     for b in range(2):
-        order = token_order(rows, SCALES[b])
-        up = jnp.tanh(dot(order, taps[b]) + up_bias[b : b + 1, :])
+        up = jnp.tanh(dot(orders[b], taps[b]) + up_bias[b : b + 1, :])
         xhat, rstd = norm_stats(up + season[b])
         ups.append(up)
         kept.append((xhat, rstd))
@@ -447,7 +449,7 @@
         d_res_out[b] = d_res
         d_up = (1.0 - ups[b] * ups[b]) * d_res
         sums[8 + b : 9 + b, :] = column_sum(d_up)
-        d_taps.append(dot_tn(token_order(rows, SCALES[b]), d_up.astype(BF)))
+        d_taps.append(dot_tn(orders[b], d_up.astype(BF)))
     sums[6:7, :] = gain_sum
     sums[7:8, :] = shift_sum
     store_taps(geo, d_pays, d_taps)
@@ -490,14 +492,13 @@
 
 def input_back_body(geo, *refs):
     pays = refs[: geo["taps"]]
-    info_one, info_two, residual, own, left, right = refs[geo["taps"] :]
+    matrices, residual, own, left, right = refs[geo["taps"] :]
     columns, channels = residual.shape
     rows = columns - 2 * HALO
     taps = load_taps(geo, pays, channels)
     total = residual[...]
-    for b, info in enumerate((info_one, info_two)):
-        matrix = season_matrix(info[...], AVERAGES[b], columns)
-        total = total + dot_tn(matrix, taps[b]) * (1.0 / AVERAGES[b])
+    for b in range(2):
+        total = total + dot_tn(matrices[b], taps[b]) * (1.0 / AVERAGES[b])
     left[...] = total[0:HALO]
     own[...] = total[HALO : HALO + rows]
     right[...] = total[HALO + rows :]
@@ -671,8 +672,14 @@
     blocks, bit = jnp.concatenate([blocks, got]), half // 2
     while bit > 2:
         blocks, bit = jnp.concatenate([blocks, across(blocks, "tm", bit)]), bit // 2
+    matrices, orders = kernel_call(
+        matrices_body,
+        [((2, rows, rows + 2 * HALO), BF), ((2, rows, rows), BF)],
+        window_infos,
+        24,
+    )
     windows = kernel_call(
-        functools.partial(windows_body, geo), pay_outs, (tokens, left, right, *window_infos), 24
+        functools.partial(windows_body, geo), pay_outs, (tokens, left, right, matrices), 24
     )
     windows, got = together(swap(as_payload(windows)), across(blocks, "tm", bit))
     blocks = jnp.concatenate([blocks, got])
@@ -690,11 +697,8 @@
         (partial, jnp.stack([stride_bias_twelve, stride_bias_sixteen])),
         8,
     )
-    hidden_all, x_high, y_low, blocks_core = together(
-        swap(hidden_low),
-        across(high_blocks, "tm", 1),
-        across(low_blocks, "series", 2),
-        across(blocks, "series", 1),
+    hidden_all, x_high, y_low = together(
+        swap(hidden_low), across(high_blocks, "tm", 1), across(low_blocks, "series", 2)
     )
     (partial,) = kernel_call(
         functools.partial(iso_body, geo),
@@ -704,11 +708,8 @@
         scalars=(0,),
     )
     first = (x_low, x_high, y_low, y_high)
-    partial, blocks_a, blocks_b, *core_first = together(
-        swap(partial),
-        across(x_low, "series", 2),
-        across(y_high, "tm", 1),
-        *(across(f, "series", 1) for f in first),
+    partial, blocks_a, blocks_b = together(
+        swap(partial), across(x_low, "series", 2), across(y_high, "tm", 1)
     )
     hidden_two, mixed_low = kernel_call(
         functools.partial(mix_body, geo),
@@ -725,22 +726,19 @@
     (season,) = kernel_call(
         season_body, [((2, rows, channels), F32)], (tokens, left, right, token_info), 24
     )
-    mixed_all, season, core_a, core_b = together(
-        swap(mixed_low), season, across(blocks_a, "series", 1), across(blocks_b, "series", 1)
-    )
+    mixed_all, season = together(swap(mixed_low), season)
     (ups,) = kernel_call(
         functools.partial(slab_out_body, geo), [(pay_shape, BF)], (mixed_all, up_own), 24
     )
-    ups = swap(ups)
-    head_pieces = [
-        blocks, *first, blocks_a, blocks_b, blocks_core, *core_first, core_a, core_b,
-    ]
+    head_pieces = [blocks, *first, blocks_a, blocks_b]
+    ups, *other_pieces = together(swap(ups), *(across(p, "series", 1) for p in head_pieces))
+    head_pieces += other_pieces
     geo["pieces"] = len(head_pieces)
     hidden_units = 4 * n * quarter_rows[1]
     head_args = [
         *as_taps(ups), season, cotangent[0], jnp.stack([upsample_bias_twelve, upsample_bias_sixteen]),
         row(mix_gain), row(mix_shift), row(merge_bias), row(feed_gain), row(feed_shift),
-        row(expand_bias), row(project_bias), row(final_gain), row(final_shift),
+        row(expand_bias), row(project_bias), row(final_gain), row(final_shift), orders,
     ]
     head_scratch = [
         pltpu.VMEM((hidden_units // FFN_CHUNK, rows, FFN_CHUNK), F32),
@@ -789,8 +787,14 @@
         residual_body, [((rows + 2 * HALO, channels), F32)], (d_res, token_info), 24
     )
     head_sum = summed(head_own, across(head_other, "series", 1))
-    d_ups, head_sum, residual = together(swap(as_payload(d_ups)), head_sum, residual)
     head_sum = head_sum.reshape(2, 2, 2, len(far) // 2, *half_blocks[1:])
+    d_ups, head_sum, residual, x_1, y_1 = together(
+        swap(as_payload(d_ups)),
+        head_sum,
+        residual,
+        across(head_sum[1, 1, 0], "tm", 1),
+        across(head_sum[1, 1, 1], "series", 2),
+    )
     core = (replica & 1).reshape(1)
 
     def slab_grads(payload, steps):
@@ -812,12 +816,16 @@
         functools.partial(slab_in_body, geo), step_block, (d_ups, up_own), 24
     )
     up_mine, up_sent = slab_grads(d_ups, mixed_all)
-    partial, x_1, y_1, up_mine, up_sent = together(
+    head_x = summed(head_sum[1, 0, 0], x_1)
+    head_y = summed(head_sum[0, 1, 1], y_1)
+    partial, x_0, y_0, up_mine, up_sent, head_x, head_y = together(
         swap(partial),
-        across(head_sum[1, 1, 0], "tm", 1),
-        across(head_sum[1, 1, 1], "series", 2),
+        across(head_sum[0, 1, 0], "tm", 1),
+        across(head_sum[1, 0, 1], "series", 2),
         up_mine,
         up_sent,
+        head_x,
+        head_y,
     )
     d_pair, d_iso = kernel_call(
         functools.partial(mix_back_body, geo),
@@ -826,16 +834,11 @@
         8,
     )
     up_part = summed(up_mine, across(up_sent, "series", 1))
-    head_x = summed(head_sum[1, 0, 0], x_1)
-    head_y = summed(head_sum[0, 1, 1], y_1)
-    d_iso_all, up_part, x_0, y_0, head_x, head_y = together(
-        swap(d_iso),
-        up_part,
-        across(after(head_sum[0, 1, 0], d_iso), "tm", 1),
-        across(after(head_sum[1, 0, 1], d_iso), "series", 2),
-        head_x,
-        head_y,
-    )
+    head_sum = (
+        summed(head_sum[0, 0, 0], x_0, across(after(head_x, d_iso), "series", 2)),
+        summed(head_sum[0, 0, 1], y_0, across(after(head_y, d_iso), "tm", 1)),
+    )
+    d_iso_all, up_part, *head_sum = together(swap(d_iso), up_part, *head_sum)
     (partial,) = kernel_call(
         functools.partial(iso_back_body, geo),
         step_block,
@@ -855,24 +858,21 @@
             pltpu.VMEM((2, *part), BF),
         ],
     )
-    head_sum = (
-        summed(head_sum[0, 0, 0], x_0, across(head_x, "series", 2)),
-        summed(head_sum[0, 0, 1], y_0, across(head_y, "tm", 1)),
-    )
-    up_low, up_high = cut(up_part, 1)
-    partial, iso_mine, iso_sent, up_a, *head_sum = together(
-        swap(partial), iso_mine, iso_sent, across(up_low, "series", 2), *head_sum
-    )
-    (d_conv,) = kernel_call(
-        functools.partial(conv_back_body, geo), [((n, *own_steps), BF)], (partial, d_pair, hidden_one), 8
-    )
-    iso_part = summed(after(iso_mine, d_conv), across(iso_sent, "series", 1))
-    head_sum, bit = summed(head_sum[0], across(after(head_sum[1], d_conv), "tm", 2)), 4
+    head_sum, bit = summed(head_sum[0], across(after(head_sum[1], partial), "tm", 2)), 4
     while bit < half:
         head_sum, got = jnp.split(head_sum, 2)
         head_sum, bit = summed(head_sum, across(got, "tm", bit)), 2 * bit
-    d_conv_all, up_b, head_sum, iso_part = together(
-        swap(d_conv), across(up_high, "series", 2), head_sum, iso_part
+    partial, iso_mine, iso_sent, up_a, head_sum = together(
+        swap(partial), iso_mine, iso_sent, across(up_part, "series", 2), head_sum
+    )
+    (d_conv,) = kernel_call(
+        functools.partial(conv_back_body, geo), [((n, *own_steps), BF)], (partial, d_pair, hidden_one), 8
+    )
+    iso_part = summed(after(iso_mine, d_conv), across(iso_sent, "series", 1))
+    up_part = summed(after(up_part, d_conv), up_a)
+    iso_low, iso_high = cut(iso_part, 1)
+    d_conv_all, up_part, iso_part, iso_high, iso_a = together(
+        swap(d_conv), up_part, iso_part, iso_high, across(iso_low, "series", 2)
     )
 
     def grads_of(part, got, sizes):
@@ -889,40 +889,31 @@
     )
     stride_mine, stride_sent = slab_grads(windows, d_conv_all)
     stride_part = summed(stride_mine, across(stride_sent, "series", 1))
-    at = sum(quarter_rows)
-    up_part = summed(after(up_part, d_windows), jnp.concatenate([up_a, up_b]))
-    iso_low, iso_high = cut(after(iso_part, d_windows))
-    d_windows, iso_a, stride_a, up_part, up_got = together(
-        swap(d_windows),
-        across(iso_low, "series", 2),
-        across(cut(stride_part, 1)[0], "series", 2),
-        up_part,
-        across(up_part, "series", 1),
+    iso_b = across(iso_high, "series", 2)
+    stride_y = across(stride_part, "series", 2)
+    d_windows, up_part, up_got = together(
+        swap(d_windows), up_part, across(up_part, "series", 1)
     )
     edge = ((HALO, channels), F32)
     own, to_left, to_right = kernel_call(
         functools.partial(input_back_body, geo),
         [((rows, channels), F32), edge, edge],
-        (*as_taps(d_windows), *window_infos, residual),
+        (*as_taps(d_windows), matrices, residual),
         24,
     )
-    iso_b = across(iso_high, "series", 2)
     iso_part = summed(after(iso_part, own), jnp.concatenate([iso_a, iso_b]))
-    head_mine = summed(head_sum[0], across(after(head_sum[1], own), "tm", half))
-    from_right, from_left, stride_b, iso_part, head_mine = together(
-        lax.ppermute(to_left, "tm", down_route),
-        lax.ppermute(to_right, "tm", up_route),
-        across(cut(stride_part, 1)[1], "series", 2),
-        iso_part,
-        head_mine,
+    head_mine = summed(head_sum[0], across(after(head_sum[1], d_windows), "tm", half))
+    at = sum(quarter_rows)
+    head_y = across(head_mine[:at], "series", 2)
+    from_right, from_left = together(
+        lax.ppermute(to_left, "tm", down_route), lax.ppermute(to_right, "tm", up_route)
     )
     ups = grads_of(after(up_part, own), up_got, slab)
     input_grad = jnp.concatenate(
         [own[:HALO] + from_left, own[HALO : rows - HALO], own[rows - HALO :] + from_right], axis=0
     ).astype(BF)
-    stride_part = summed(stride_part, jnp.concatenate([stride_a, stride_b]))
+    stride_part = summed(stride_part, stride_y)
     stride_got, iso_got = across(stride_part, "series", 1), across(iso_part, "series", 1)
-    head_y = across(head_mine[:at], "series", 2)
     head_y = jnp.where(
         bit_of("series", 2) == 0, jnp.stack([head_mine[:at], head_y]), jnp.stack([head_y, head_mine[:at]])
     )

time: 383 us -> 363 us (0.948)
  waiting for transfers between devices: 135 us -> 126 us
  local copies, waits for them, and re-layouts: 55.7 us -> 50.5 us
    ppermute x38 -> x36, waiting for transfers between devices: 97.9 us -> 81.4 us  [across(): lax.ppermute(x, axis, [(i, i ^ bit) for i in range(lax.axis_size(axis))])]
    all_to_all x12, waiting for transfers between devices: 34.3 us -> 44.5 us  [swap(): return lax.all_to_all(x, 'tm', 0, 0)]
    slice x6 -> x2, local copies, waits for them, and re-layouts: 6.29 us -> 0.89 us  [cut(): return (x[:at], x[at:])]
    ppermute x38 -> x36, starting transfers between devices: 36.5 us -> 33.5 us  [across(): lax.ppermute(x, axis, [(i, i ^ bit) for i in range(lax.axis_size(axis))])]
    pallas_call x21 -> x22, Pallas kernels: 55.8 us -> 54.2 us  [kernel_call(): pl.pallas_call(body, out_shape=[jax.ShapeDtypeStruct(shape, dtype) for sh...]
    unnamed x148 -> x152, local copies, waits for them, and re-layouts: 36.9 us -> 36.3 us
  transfers between devices with their start and end apart: 54 -> 52, of which waited for: 22 -> 22; matrix products, arithmetic and copies ran while one was open for 13% -> 12% of each run, Pallas kernels for 5% -> 6%
where the time goes in v4:
time: 363 us; the launch traced here: 361 us
  waiting for transfers between devices  126 us (35%)
  starting transfers between devices  99.8 us (27%)
  Pallas kernels  54.2 us (15%)
  local copies, waits for them, and re-layouts  50.5 us (14%)
  other arithmetic  28.8 us (8%)
    ppermute x36, waiting for transfers between devices, across(): lax.ppermute(x, axis, [(i, i ^ bit) for i in range(lax.axis_size(axis))])  81.4 us
    all_to_all x12, starting transfers between devices, swap(): return lax.all_to_all(x, 'tm', 0, 0)  55.8 us
    pallas_call x22, Pallas kernels, kernel_call(): pl.pallas_call(body, out_shape=[jax.ShapeDtypeStruct(shape, dtype) for sh...  54.2 us
    all_to_all x12, waiting for transfers between devices, swap(): return lax.all_to_all(x, 'tm', 0, 0)  44.5 us
    unnamed x152, local copies, waits for them, and re-layouts  36.3 us
    ppermute x36, starting transfers between devices, across(): lax.ppermute(x, axis, [(i, i ^ bit) for i in range(lax.axis_size(axis))])  33.5 us
    convert_element_type x11, other arithmetic, summed(): return sum((p.astype(F32) for p in parts)).astype(BF)  22.7 us
  transfers between devices with their start and end apart: 52, of which 22 were waited for; matrix products, arithmetic and copies ran while one was open for 12% of the time, Pallas kernels for 6%

profile of v4, /device:TPU:0, one launch (start us, length us, event | category | flops | bytes accessed | tf_op | source)
XLA Modules:
  0.0 360.8 jit_solution(13435508310431362260)
XLA Ops:
  2.5 4.1 %collective-permute-start.2 = (bf16[1,160,512]{2,1,0:T(8,128)(2,1)S(1)}, bf16[1,160,512]{2,1,0:T(8,128)(2,1)S(1)}, u32[]{:S(2)}, u32[]{:S(2)}) collective-permute-start(bf16[1,160,512]{2,1,0:T(8,128)(2,1)S(1)} %maximum_bitcast_fusion), channel_id=1, source_target_pairs={{0,4},{1,5},{2,6},{3,7},{4,0},{5,1},{6,2},{7,3},{8,12},{9,13},{10,... | collective-permute-start | bytes 491528 | tf_op jit(solution)/shard_map/ppermute | solution.py:520
  18.8 4.9 %all-to-all-start = ((bf16[8,192,256]{2,1,0:T(8,128)(2,1)}), bf16[8,192,256]{2,1,0:T(8,128)(2,1)S(1)}, u32[]{:S(2)}, u32[]{:S(2)}) async-start(bf16[8,192,256]{2,1,0:T(8,128)(2,1)} %shard_map.459), calls=%async_computation | async-start | bytes 1572864 | tf_op jit(solution)/shard_map/all_to_all | solution.py:508
  27.4 18.3 %collective-permute-done.3 = bf16[2,160,512]{2,1,0:T(8,128)(2,1)} collective-permute-done((bf16[2,160,512]{2,1,0:T(8,128)(2,1)S(1)}, bf16[2,160,512]{2,1,0:T(8,128)(2,1)}, u32[]{:S(2)}, u32[]{:S(2)}) %collective-permute-start.3) | collective-permute-done | bytes 327712 | tf_op jit(solution)/shard_map/ppermute | solution.py:520
  47.0 4.0 %all-to-all-start.1 = ((bf16[8,56,512]{2,1,0:T(8,128)(2,1)}), bf16[8,56,512]{2,1,0:T(8,128)(2,1)S(1)}, u32[]{:S(2)}, u32[]{:S(2)}) async-start(bf16[8,56,512]{2,1,0:T(8,128)(2,1)} %shard_map.460), calls=%async_computation.1 | async-start | bytes 917504 | tf_op jit(solution)/shard_map/all_to_all | solution.py:508
  55.8 8.5 %collective-permute-done.4.refs_16_ = bf16[2,160,512]{2,1,0:T(8,128)(2,1)S(1)} collective-permute-done((bf16[2,160,512]{2,1,0:T(8,128)(2,1)S(1)}, bf16[2,160,512]{2,1,0:T(8,128)(2,1)S(1)}, u32[]{:S(2)}, u32[]{:S(2)}) %collective-permute-start.4) | collective-permute-done | bytes 327712 | tf_op jit(solution)/shard_map/ppermute | solution.py:520
  65.9 4.6 %all-to-all-start.2 = ((bf16[8,56,512]{2,1,0:T(8,128)(2,1)}), bf16[8,56,512]{2,1,0:T(8,128)(2,1)S(1)}, u32[]{:S(2)}, u32[]{:S(2)}) async-start(bf16[8,56,512]{2,1,0:T(8,128)(2,1)} %get-tuple-element.126), calls=%async_computation.2 | async-start | bytes 917504 | tf_op jit(solution)/shard_map/all_to_all | solution.py:508
  76.2 3.6 %collective-permute-done.7.refs_18_ = bf16[2,160,512]{2,1,0:T(8,128)(2,1)S(1)} collective-permute-done((bf16[2,160,512]{2,1,0:T(8,128)(2,1)}, bf16[2,160,512]{2,1,0:T(8,128)(2,1)S(1)}, u32[]{:S(2)}, u32[]{:S(2)}) %collective-permute-start.7) | collective-permute-done | bytes 327712 | tf_op jit(solution)/shard_map/ppermute | solution.py:520
  80.6 4.5 %collective-permute-done.6.refs_17_ = bf16[2,160,512]{2,1,0:T(8,128)(2,1)} collective-permute-done((bf16[2,160,512]{2,1,0:T(8,128)(2,1)}, bf16[2,160,512]{2,1,0:T(8,128)(2,1)}, u32[]{:S(2)}, u32[]{:S(2)}) %collective-permute-start.6) | collective-permute-done | bytes 327712 | tf_op jit(solution)/shard_map/ppermute | solution.py:520
  89.7 4.3 %all-to-all-start.3 = ((bf16[8,56,512]{2,1,0:T(8,128)(2,1)}), bf16[8,56,512]{2,1,0:T(8,128)(2,1)}, u32[]{:S(2)}, u32[]{:S(2)}) async-start(bf16[8,56,512]{2,1,0:T(8,128)(2,1)} %copy-done.21), calls=%async_computation.3 | async-start | bytes 917504 | tf_op jit(solution)/shard_map/all_to_all | solution.py:508
  97.3 5.7 %collective-permute-done.8.refs_20_ = bf16[2,160,512]{2,1,0:T(8,128)(2,1)S(1)} collective-permute-done((bf16[2,160,512]{2,1,0:T(8,128)(2,1)}, bf16[2,160,512]{2,1,0:T(8,128)(2,1)S(1)}, u32[]{:S(2)}, u32[]{:S(2)}) %collective-permute-start.8) | collective-permute-done | bytes 327712 | tf_op jit(solution)/shard_map/ppermute | solution.py:520
  103.0 5.1 %collective-permute-done.9.refs_21_ = bf16[2,160,512]{2,1,0:T(8,128)(2,1)} collective-permute-done((bf16[2,160,512]{2,1,0:T(8,128)(2,1)}, bf16[2,160,512]{2,1,0:T(8,128)(2,1)}, u32[]{:S(2)}, u32[]{:S(2)}) %collective-permute-start.9) | collective-permute-done | bytes 327712 | tf_op jit(solution)/shard_map/ppermute | solution.py:520
  111.7 4.6 %all-to-all-start.4 = ((bf16[8,56,512]{2,1,0:T(8,128)(2,1)}), bf16[8,56,512]{2,1,0:T(8,128)(2,1)S(1)}, u32[]{:S(2)}, u32[]{:S(2)}) async-start(bf16[8,56,512]{2,1,0:T(8,128)(2,1)} %copy-done.41), calls=%async_computation.4 | async-start | bytes 917504 | tf_op jit(solution)/shard_map/all_to_all | solution.py:508
  124.1 4.6 %all-to-all-done.4.steps = bf16[8,56,512]{2,1,0:T(8,128)(2,1)S(1)} async-done(((bf16[8,56,512]{2,1,0:T(8,128)(2,1)}), bf16[8,56,512]{2,1,0:T(8,128)(2,1)S(1)}, u32[]{:S(2)}, u32[]{:S(2)}) %all-to-all-start.4) | async-done | bytes 458784 | tf_op jit(solution)/shard_map/all_to_all | solution.py:508
  131.8 4.5 %all-to-all-start.5 = ((bf16[8,192,256]{2,1,0:T(8,128)(2,1)}), bf16[8,192,256]{2,1,0:T(8,128)(2,1)}, u32[]{:S(2)}, u32[]{:S(2)}) async-start(bf16[8,192,256]{2,1,0:T(8,128)(2,1)} %copy-done.15), calls=%async_computation.5 | async-start | bytes 1572864 | tf_op jit(solution)/shard_map/all_to_all | solution.py:508
  144.6 10.7 %all-to-all-done.5.refs_0_ = bf16[8,192,256]{2,1,0:T(8,128)(2,1)} async-done(((bf16[8,192,256]{2,1,0:T(8,128)(2,1)}), bf16[8,192,256]{2,1,0:T(8,128)(2,1)}, u32[]{:S(2)}, u32[]{:S(2)}) %all-to-all-start.5) | async-done | bytes 786464 | tf_op jit(solution)/shard_map/all_to_all | solution.py:508
  155.3 20.5 %shard_map.466 = (bf16[8,192,256]{2,1,0:T(8,128)(2,1)}, bf16[384,512]{1,0:T(8,128)(2,1)}, f32[2,384,512]{2,1,0:T(8,128)}, f32[16,512]{1,0:T(8,128)}, bf16[16,176...) custom-call(bf16[8,192,256]{2,1,0:T(8,128)(2,1)} %all-to-all-done.5.refs_0_, f32[2,384,512]{2,1,0:T(8,128)} %copy-done.7, ...), custom_call_target="tpu_custom_call" | custom-call | tf_op jit(solution)/shard_map/pallas_call | solution.py:42
  175.9 4.4 %all-to-all-start.6 = ((bf16[8,192,256]{2,1,0:T(8,128)(2,1)}), bf16[8,192,256]{2,1,0:T(8,128)(2,1)}, u32[]{:S(2)}, u32[]{:S(2)}) async-start(bf16[8,192,256]{2,1,0:T(8,128)(2,1)} %get-tuple-element.149), calls=%async_computation.6 | async-start | bytes 1572864 | tf_op jit(solution)/shard_map/all_to_all | solution.py:508
  181.5 3.7 %add_convert_fusion = bf16[16,176,512]{2,1,0:T(8,128)(2,1)S(1)} fusion(bf16[16,176,512]{2,1,0:T(8,128)(2,1)} %collective-permute-done.17, bf16[16,176,512]{2,1,0:T(8,128)(2,1)} %get-tuple-element.150), kind=kLoop, calls=%fused_computation | loop fusion | flops 5767168 | bytes 8650752 | tf_op jit(solution)/shard_map/convert_element_type | solution.py:553
  191.3 9.9 %all-to-all-done.6.payload = bf16[8,192,256]{2,1,0:T(8,128)(2,1)} async-done(((bf16[8,192,256]{2,1,0:T(8,128)(2,1)}), bf16[8,192,256]{2,1,0:T(8,128)(2,1)}, u32[]{:S(2)}, u32[]{:S(2)}) %all-to-all-start.6) | async-done | bytes 786464 | tf_op jit(solution)/shard_map/all_to_all | solution.py:508
  205.2 4.9 %all-to-all-start.7 = ((bf16[8,56,512]{2,1,0:T(8,128)(2,1)}), bf16[8,56,512]{2,1,0:T(8,128)(2,1)}, u32[]{:S(2)}, u32[]{:S(2)}) async-start(bf16[8,56,512]{2,1,0:T(8,128)(2,1)} %copy-done.19), calls=%async_computation.7 | async-start | bytes 917504 | tf_op jit(solution)/shard_map/all_to_all | solution.py:508
  220.4 5.4 %collective-permute-done.20 = bf16[2,176,512]{2,1,0:T(8,128)(2,1)} collective-permute-done((bf16[2,176,512]{2,1,0:T(8,128)(2,1)S(1)}, bf16[2,176,512]{2,1,0:T(8,128)(2,1)}, u32[]{:S(2)}, u32[]{:S(2)}) %collective-permute-start.20) | collective-permute-done | bytes 360480 | tf_op jit(solution)/shard_map/ppermute | solution.py:520
  231.7 5.5 %all-to-all-start.8 = ((bf16[8,64,512]{2,1,0:T(8,128)(2,1)}), bf16[8,64,512]{2,1,0:T(8,128)(2,1)S(1)}, u32[]{:S(2)}, u32[]{:S(2)}) async-start(bf16[8,64,512]{2,1,0:T(8,128)(2,1)} %copy-done.40), calls=%async_computation.8 | async-start | bytes 1048576 | tf_op jit(solution)/shard_map/all_to_all | solution.py:508
  237.3 4.2 %collective-permute-done.23 = bf16[2,176,512]{2,1,0:T(8,128)(2,1)} collective-permute-done((bf16[2,176,512]{2,1,0:T(8,128)(2,1)}, bf16[2,176,512]{2,1,0:T(8,128)(2,1)}, u32[]{:S(2)}, u32[]{:S(2)}) %collective-permute-start.23) | collective-permute-done | bytes 360480 | tf_op jit(solution)/shard_map/ppermute | solution.py:520
  241.4 3.8 %collective-permute-done.24 = bf16[2,176,512]{2,1,0:T(8,128)(2,1)} collective-permute-done((bf16[2,176,512]{2,1,0:T(8,128)(2,1)}, bf16[2,176,512]{2,1,0:T(8,128)(2,1)}, u32[]{:S(2)}, u32[]{:S(2)}) %collective-permute-start.24) | collective-permute-done | bytes 360480 | tf_op jit(solution)/shard_map/ppermute | solution.py:520
  257.5 4.8 %all-to-all-start.9 = ((bf16[8,56,512]{2,1,0:T(8,128)(2,1)}), bf16[8,56,512]{2,1,0:T(8,128)(2,1)S(1)}, u32[]{:S(2)}, u32[]{:S(2)}) async-start(bf16[8,56,512]{2,1,0:T(8,128)(2,1)} %copy-done.20), calls=%async_computation.9 | async-start | bytes 917504 | tf_op jit(solution)/shard_map/all_to_all | solution.py:508
  270.3 8.2 %collective-permute-done.26 = bf16[2,176,512]{2,1,0:T(8,128)(2,1)S(1)} collective-permute-done((bf16[2,176,512]{2,1,0:T(8,128)(2,1)}, bf16[2,176,512]{2,1,0:T(8,128)(2,1)S(1)}, u32[]{:S(2)}, u32[]{:S(2)}) %collective-permute-start.26) | collective-permute-done | bytes 360480 | tf_op jit(solution)/shard_map/ppermute | solution.py:520
  283.0 4.6 %all-to-all-start.10 = ((bf16[8,56,512]{2,1,0:T(8,128)(2,1)}), bf16[8,56,512]{2,1,0:T(8,128)(2,1)S(1)}, u32[]{:S(2)}, u32[]{:S(2)}) async-start(bf16[8,56,512]{2,1,0:T(8,128)(2,1)} %shard_map.473), calls=%async_computation.10 | async-start | bytes 917504 | tf_op jit(solution)/shard_map/all_to_all | solution.py:508
  293.5 7.9 %all-to-all-done.10.steps = bf16[8,56,512]{2,1,0:T(8,128)(2,1)S(1)} async-done(((bf16[8,56,512]{2,1,0:T(8,128)(2,1)}), bf16[8,56,512]{2,1,0:T(8,128)(2,1)S(1)}, u32[]{:S(2)}, u32[]{:S(2)}) %all-to-all-start.10) | async-done | bytes 458784 | tf_op jit(solution)/shard_map/all_to_all | solution.py:508
  302.9 4.6 %all-to-all-start.11 = ((bf16[8,192,256]{2,1,0:T(8,128)(2,1)}), bf16[8,192,256]{2,1,0:T(8,128)(2,1)}, u32[]{:S(2)}, u32[]{:S(2)}) async-start(bf16[8,192,256]{2,1,0:T(8,128)(2,1)} %copy-done.16), calls=%async_computation.11 | async-start | bytes 1572864 | tf_op jit(solution)/shard_map/all_to_all | solution.py:508
  317.3 10.0 %all-to-all-done.11.refs_0_ = bf16[8,192,256]{2,1,0:T(8,128)(2,1)} async-done(((bf16[8,192,256]{2,1,0:T(8,128)(2,1)}), bf16[8,192,256]{2,1,0:T(8,128)(2,1)}, u32[]{:S(2)}, u32[]{:S(2)}) %all-to-all-start.11) | async-done | bytes 786464 | tf_op jit(solution)/shard_map/all_to_all | solution.py:508
  330.5 4.5 %collective-permute-start.31 = (f32[16,512]{1,0:T(8,128)S(1)}, f32[16,512]{1,0:T(8,128)S(1)}, u32[]{:S(2)}, u32[]{:S(2)}) collective-permute-start(f32[16,512]{1,0:T(8,128)S(1)} %get-tuple-element.190), channel_id=1, source_target_pairs={{0,1},{1,2},{2,3},{3,4},{4,5},{5,6},{6,7},{8,9},{9,10},{10,11},{11... | collective-permute-start | bytes 98312 | tf_op jit(solution)/shard_map/ppermute | solution.py:909
  340.6 9.9 %collective-permute-done.38 = bf16[160,512]{1,0:T(8,128)(2,1)S(1)} collective-permute-done((bf16[160,512]{1,0:T(8,128)(2,1)S(1)}, bf16[160,512]{1,0:T(8,128)(2,1)S(1)}, u32[]{:S(2)}, u32[]{:S(2)}) %collective-permute-start.38) | collective-permute-done | bytes 163872 | tf_op jit(solution)/shard_map/ppermute | solution.py:520
  (326 shorter events, 150.3 us)
Async XLA Ops:
  2.5 14.8 %collective-permute-start.2 = (bf16[1,160,512]{2,1,0:T(8,128)(2,1)S(1)}, bf16[1,160,512]{2,1,0:T(8,128)(2,1)S(1)}, u32[]{:S(2)}, u32[]{:S(2)}) collective-permute-start(bf16[1,160,512]{2,1,0:T(8,128)(2,1)S(1)} %maximum_bitcast_fusion), channel_id=1, source_target_pairs={{0,4},{1,5},{2,6},{3,7},{4,0},{5,1},{6,2},{7,3},{8,12},{9,13},{10,... | collective-permute-start | bytes 491528 | tf_op jit(solution)/shard_map/ppermute | solution.py:520
  18.8 26.9 %all-to-all-start = ((bf16[8,192,256]{2,1,0:T(8,128)(2,1)}), bf16[8,192,256]{2,1,0:T(8,128)(2,1)S(1)}, u32[]{:S(2)}, u32[]{:S(2)}) async-start(bf16[8,192,256]{2,1,0:T(8,128)(2,1)} %shard_map.459), calls=%async_computation | async-start | bytes 1572864 | tf_op jit(solution)/shard_map/all_to_all | solution.py:508
  23.8 21.9 %collective-permute-start.3 = (bf16[2,160,512]{2,1,0:T(8,128)(2,1)S(1)}, bf16[2,160,512]{2,1,0:T(8,128)(2,1)}, u32[]{:S(2)}, u32[]{:S(2)}) collective-permute-start(bf16[2,160,512]{2,1,0:T(8,128)(2,1)S(1)} %pad_maximum_fusion.2), channel_id=1, source_target_pairs={{0,2},{1,3},{2,0},{3,1},{4,6},{5,7},{6,4},{7,5},{8,10},{9,11},{10,... | collective-permute-start | bytes 983048 | tf_op jit(solution)/shard_map/ppermute | solution.py:520
  47.0 17.3 %all-to-all-start.1 = ((bf16[8,56,512]{2,1,0:T(8,128)(2,1)}), bf16[8,56,512]{2,1,0:T(8,128)(2,1)S(1)}, u32[]{:S(2)}, u32[]{:S(2)}) async-start(bf16[8,56,512]{2,1,0:T(8,128)(2,1)} %shard_map.460), calls=%async_computation.1 | async-start | bytes 917504 | tf_op jit(solution)/shard_map/all_to_all | solution.py:508
  51.9 12.4 %collective-permute-start.4 = (bf16[2,160,512]{2,1,0:T(8,128)(2,1)S(1)}, bf16[2,160,512]{2,1,0:T(8,128)(2,1)S(1)}, u32[]{:S(2)}, u32[]{:S(2)}) collective-permute-start(bf16[2,160,512]{2,1,0:T(8,128)(2,1)S(1)} %copy-done.67), channel_id=1, source_target_pairs={{0,1},{1,0},{2,3},{3,2},{4,5},{5,4},{6,7},{7,6},{8,9},{9,8},{10,11... | collective-permute-start | bytes 983048 | tf_op jit(solution)/shard_map/ppermute | solution.py:520
  65.9 19.2 %all-to-all-start.2 = ((bf16[8,56,512]{2,1,0:T(8,128)(2,1)}), bf16[8,56,512]{2,1,0:T(8,128)(2,1)S(1)}, u32[]{:S(2)}, u32[]{:S(2)}) async-start(bf16[8,56,512]{2,1,0:T(8,128)(2,1)} %get-tuple-element.126), calls=%async_computation.2 | async-start | bytes 917504 | tf_op jit(solution)/shard_map/all_to_all | solution.py:508
  72.8 12.3 %collective-permute-start.6 = (bf16[2,160,512]{2,1,0:T(8,128)(2,1)}, bf16[2,160,512]{2,1,0:T(8,128)(2,1)}, u32[]{:S(2)}, u32[]{:S(2)}) collective-permute-start(bf16[2,160,512]{2,1,0:T(8,128)(2,1)} %collective-permute-done.3), channel_id=1, source_target_pairs={{0,1},{1,0},{2,3},{3,2},{4,5},{5,4},{6,7},{7,6},{8,9},{9,8},{10,11... | collective-permute-start | bytes 983048 | tf_op jit(solution)/shard_map/ppermute | solution.py:520
  89.7 18.4 %all-to-all-start.3 = ((bf16[8,56,512]{2,1,0:T(8,128)(2,1)}), bf16[8,56,512]{2,1,0:T(8,128)(2,1)}, u32[]{:S(2)}, u32[]{:S(2)}) async-start(bf16[8,56,512]{2,1,0:T(8,128)(2,1)} %copy-done.21), calls=%async_computation.3 | async-start | bytes 917504 | tf_op jit(solution)/shard_map/all_to_all | solution.py:508
  95.2 12.9 %collective-permute-start.9 = (bf16[2,160,512]{2,1,0:T(8,128)(2,1)}, bf16[2,160,512]{2,1,0:T(8,128)(2,1)}, u32[]{:S(2)}, u32[]{:S(2)}) collective-permute-start(bf16[2,160,512]{2,1,0:T(8,128)(2,1)} %copy-done.63), channel_id=1, source_target_pairs={{0,1},{1,0},{2,3},{3,2},{4,5},{5,4},{6,7},{7,6},{8,9},{9,8},{10,11... | collective-permute-start | bytes 983048 | tf_op jit(solution)/shard_map/ppermute | solution.py:520
  111.7 17.0 %all-to-all-start.4 = ((bf16[8,56,512]{2,1,0:T(8,128)(2,1)}), bf16[8,56,512]{2,1,0:T(8,128)(2,1)S(1)}, u32[]{:S(2)}, u32[]{:S(2)}) async-start(bf16[8,56,512]{2,1,0:T(8,128)(2,1)} %copy-done.41), calls=%async_computation.4 | async-start | bytes 917504 | tf_op jit(solution)/shard_map/all_to_all | solution.py:508
  131.8 23.5 %all-to-all-start.5 = ((bf16[8,192,256]{2,1,0:T(8,128)(2,1)}), bf16[8,192,256]{2,1,0:T(8,128)(2,1)}, u32[]{:S(2)}, u32[]{:S(2)}) async-start(bf16[8,192,256]{2,1,0:T(8,128)(2,1)} %copy-done.15), calls=%async_computation.5 | async-start | bytes 1572864 | tf_op jit(solution)/shard_map/all_to_all | solution.py:508
  175.9 25.3 %all-to-all-start.6 = ((bf16[8,192,256]{2,1,0:T(8,128)(2,1)}), bf16[8,192,256]{2,1,0:T(8,128)(2,1)}, u32[]{:S(2)}, u32[]{:S(2)}) async-start(bf16[8,192,256]{2,1,0:T(8,128)(2,1)} %get-tuple-element.149), calls=%async_computation.6 | async-start | bytes 1572864 | tf_op jit(solution)/shard_map/all_to_all | solution.py:508
  186.2 15.0 %collective-permute-start.18 = (bf16[2,176,512]{2,1,0:T(8,128)(2,1)}, bf16[2,176,512]{2,1,0:T(8,128)(2,1)}, u32[]{:S(2)}, u32[]{:S(2)}) collective-permute-start(bf16[2,176,512]{2,1,0:T(8,128)(2,1)} %get-tuple-element.229), channel_id=1, source_target_pairs={{0,1},{1,0},{2,3},{3,2},{4,5},{5,4},{6,7},{7,6},{8,9},{9,8},{10,11... | collective-permute-start | bytes 1081352 | tf_op jit(solution)/shard_map/ppermute | solution.py:520
  187.5 13.7 %collective-permute-start.19 = (bf16[2,176,512]{2,1,0:T(8,128)(2,1)}, bf16[2,176,512]{2,1,0:T(8,128)(2,1)}, u32[]{:S(2)}, u32[]{:S(2)}) collective-permute-start(bf16[2,176,512]{2,1,0:T(8,128)(2,1)} %get-tuple-element.228), channel_id=1, source_target_pairs={{0,16},{8,24},{16,0},{24,8},{1,17},{9,25},{17,1},{25,9},{2,18},{10... | collective-permute-start | bytes 1081352 | tf_op jit(solution)/shard_map/ppermute | solution.py:520
  205.2 20.6 %all-to-all-start.7 = ((bf16[8,56,512]{2,1,0:T(8,128)(2,1)}), bf16[8,56,512]{2,1,0:T(8,128)(2,1)}, u32[]{:S(2)}, u32[]{:S(2)}) async-start(bf16[8,56,512]{2,1,0:T(8,128)(2,1)} %copy-done.19), calls=%async_computation.7 | async-start | bytes 917504 | tf_op jit(solution)/shard_map/all_to_all | solution.py:508
  211.2 14.6 %collective-permute-start.20 = (bf16[2,176,512]{2,1,0:T(8,128)(2,1)S(1)}, bf16[2,176,512]{2,1,0:T(8,128)(2,1)}, u32[]{:S(2)}, u32[]{:S(2)}) collective-permute-start(bf16[2,176,512]{2,1,0:T(8,128)(2,1)S(1)} %get-tuple-element.227), channel_id=1, source_target_pairs={{0,1},{1,0},{2,3},{3,2},{4,5},{5,4},{6,7},{7,6},{8,9},{9,8},{10,11... | collective-permute-start | bytes 1081352 | tf_op jit(solution)/shard_map/ppermute | solution.py:520
  213.3 12.5 %collective-permute-start.21 = (bf16[2,176,512]{2,1,0:T(8,128)(2,1)S(1)}, bf16[2,176,512]{2,1,0:T(8,128)(2,1)}, u32[]{:S(2)}, u32[]{:S(2)}) collective-permute-start(bf16[2,176,512]{2,1,0:T(8,128)(2,1)S(1)} %get-tuple-element.226), channel_id=1, source_target_pairs={{0,16},{8,24},{16,0},{24,8},{1,17},{9,25},{17,1},{25,9},{2,18},{10... | collective-permute-start | bytes 1081352 | tf_op jit(solution)/shard_map/ppermute | solution.py:520
  225.7 22.2 %collective-permute-start.22 = (bf16[912,512]{1,0:T(8,128)(2,1)}, bf16[912,512]{1,0:T(8,128)(2,1)}, u32[]{:S(2)}, u32[]{:S(2)}) collective-permute-start(bf16[912,512]{1,0:T(8,128)(2,1)} %copy-done.49), channel_id=1, source_target_pairs={{0,8},{8,0},{16,24},{24,16},{1,9},{9,1},{17,25},{25,17},{2,10},{10... | collective-permute-start | bytes 2801672 | tf_op jit(solution)/shard_map/ppermute | solution.py:520
  230.3 11.1 %collective-permute-start.23 = (bf16[2,176,512]{2,1,0:T(8,128)(2,1)}, bf16[2,176,512]{2,1,0:T(8,128)(2,1)}, u32[]{:S(2)}, u32[]{:S(2)}) collective-permute-start(bf16[2,176,512]{2,1,0:T(8,128)(2,1)} %get-tuple-element.166), channel_id=1, source_target_pairs={{0,16},{8,24},{16,0},{24,8},{1,17},{9,25},{17,1},{25,9},{2,18},{10... | collective-permute-start | bytes 1081352 | tf_op jit(solution)/shard_map/ppermute | solution.py:520
  231.3 14.0 %collective-permute-start.24 = (bf16[2,176,512]{2,1,0:T(8,128)(2,1)}, bf16[2,176,512]{2,1,0:T(8,128)(2,1)}, u32[]{:S(2)}, u32[]{:S(2)}) collective-permute-start(bf16[2,176,512]{2,1,0:T(8,128)(2,1)} %get-tuple-element.169), channel_id=1, source_target_pairs={{0,1},{1,0},{2,3},{3,2},{4,5},{5,4},{6,7},{7,6},{8,9},{9,8},{10,11... | collective-permute-start | bytes 1081352 | tf_op jit(solution)/shard_map/ppermute | solution.py:520
  231.7 20.1 %all-to-all-start.8 = ((bf16[8,64,512]{2,1,0:T(8,128)(2,1)}), bf16[8,64,512]{2,1,0:T(8,128)(2,1)S(1)}, u32[]{:S(2)}, u32[]{:S(2)}) async-start(bf16[8,64,512]{2,1,0:T(8,128)(2,1)} %copy-done.40), calls=%async_computation.8 | async-start | bytes 1048576 | tf_op jit(solution)/shard_map/all_to_all | solution.py:508
  251.9 28.5 %collective-permute-start.25 = (bf16[912,512]{1,0:T(8,128)(2,1)}, bf16[912,512]{1,0:T(8,128)(2,1)}, u32[]{:S(2)}, u32[]{:S(2)}) collective-permute-start(bf16[912,512]{1,0:T(8,128)(2,1)} %add_convert_fusion.6), channel_id=1, source_target_pairs={{0,16},{8,24},{16,0},{24,8},{1,17},{9,25},{17,1},{25,9},{2,18},{10... | collective-permute-start | bytes 2801672 | tf_op jit(solution)/shard_map/ppermute | solution.py:520
  257.5 22.9 %all-to-all-start.9 = ((bf16[8,56,512]{2,1,0:T(8,128)(2,1)}), bf16[8,56,512]{2,1,0:T(8,128)(2,1)S(1)}, u32[]{:S(2)}, u32[]{:S(2)}) async-start(bf16[8,56,512]{2,1,0:T(8,128)(2,1)} %copy-done.20), calls=%async_computation.9 | async-start | bytes 917504 | tf_op jit(solution)/shard_map/all_to_all | solution.py:508
  262.2 16.2 %collective-permute-start.26 = (bf16[2,176,512]{2,1,0:T(8,128)(2,1)}, bf16[2,176,512]{2,1,0:T(8,128)(2,1)S(1)}, u32[]{:S(2)}, u32[]{:S(2)}) collective-permute-start(bf16[2,176,512]{2,1,0:T(8,128)(2,1)} %get-tuple-element.176), channel_id=1, source_target_pairs={{0,2},{1,3},{2,0},{3,1},{4,6},{5,7},{6,4},{7,5},{8,10},{9,11},{10,... | collective-permute-start | bytes 1081352 | tf_op jit(solution)/shard_map/ppermute | solution.py:520
  283.0 18.3 %all-to-all-start.10 = ((bf16[8,56,512]{2,1,0:T(8,128)(2,1)}), bf16[8,56,512]{2,1,0:T(8,128)(2,1)S(1)}, u32[]{:S(2)}, u32[]{:S(2)}) async-start(bf16[8,56,512]{2,1,0:T(8,128)(2,1)} %shard_map.473), calls=%async_computation.10 | async-start | bytes 917504 | tf_op jit(solution)/shard_map/all_to_all | solution.py:508
  289.2 12.2 %collective-permute-start.28 = (bf16[304,512]{1,0:T(8,128)(2,1)S(1)}, bf16[304,512]{1,0:T(8,128)(2,1)}, u32[]{:S(2)}, u32[]{:S(2)}) collective-permute-start(bf16[304,512]{1,0:T(8,128)(2,1)S(1)} %slice.158), channel_id=1, source_target_pairs={{0,16},{8,24},{16,0},{24,8},{1,17},{9,25},{17,1},{25,9},{2,18},{10... | collective-permute-start | bytes 933896 | tf_op jit(solution)/shard_map/ppermute | solution.py:520
  302.9 24.3 %all-to-all-start.11 = ((bf16[8,192,256]{2,1,0:T(8,128)(2,1)}), bf16[8,192,256]{2,1,0:T(8,128)(2,1)}, u32[]{:S(2)}, u32[]{:S(2)}) async-start(bf16[8,192,256]{2,1,0:T(8,128)(2,1)} %copy-done.16), calls=%async_computation.11 | async-start | bytes 1572864 | tf_op jit(solution)/shard_map/all_to_all | solution.py:508
  310.7 24.3 %collective-permute-start.35 = (bf16[608,512]{1,0:T(8,128)(2,1)}, bf16[608,512]{1,0:T(8,128)(2,1)}, u32[]{:S(2)}, u32[]{:S(2)}) collective-permute-start(bf16[608,512]{1,0:T(8,128)(2,1)} %slice.157), channel_id=1, source_target_pairs={{0,16},{8,24},{16,0},{24,8},{1,17},{9,25},{17,1},{25,9},{2,18},{10... | collective-permute-start | bytes 1867784 | tf_op jit(solution)/shard_map/ppermute | solution.py:520
  316.3 34.3 %collective-permute-start.33 = (bf16[912,512]{1,0:T(8,128)(2,1)}, bf16[912,512]{1,0:T(8,128)(2,1)}, u32[]{:S(2)}, u32[]{:S(2)}) collective-permute-start(bf16[912,512]{1,0:T(8,128)(2,1)} %add_convert_fusion.3), channel_id=1, source_target_pairs={{0,16},{8,24},{16,0},{24,8},{1,17},{9,25},{17,1},{25,9},{2,18},{10... | collective-permute-start | bytes 2801672 | tf_op jit(solution)/shard_map/ppermute | solution.py:520
  327.3 12.2 %collective-permute-start.37 = (bf16[176,512]{1,0:T(8,128)(2,1)}, bf16[176,512]{1,0:T(8,128)(2,1)S(1)}, u32[]{:S(2)}, u32[]{:S(2)}) collective-permute-start(bf16[176,512]{1,0:T(8,128)(2,1)} %slice_bitcast_fusion.4), channel_id=1, source_target_pairs={{0,4},{1,5},{2,6},{3,7},{4,0},{5,1},{6,2},{7,3},{8,12},{9,13},{10,... | collective-permute-start | bytes 540680 | tf_op jit(solution)/shard_map/ppermute | solution.py:520
  336.5 19.1 %collective-permute-start.36 = (bf16[912,512]{1,0:T(8,128)(2,1)S(1)}, bf16[912,512]{1,0:T(8,128)(2,1)S(1)}, u32[]{:S(2)}, u32[]{:S(2)}) collective-permute-start(bf16[912,512]{1,0:T(8,128)(2,1)S(1)} %add_convert_fusion.1.part), channel_id=1, source_target_pairs={{0,8},{8,0},{16,24},{24,16},{1,9},{9,1},{17,25},{25,17},{2,10},{10... | collective-permute-start | bytes 2801672 | tf_op jit(solution)/shard_map/ppermute | solution.py:520
  339.5 11.0 %collective-permute-start.38 = (bf16[160,512]{1,0:T(8,128)(2,1)S(1)}, bf16[160,512]{1,0:T(8,128)(2,1)S(1)}, u32[]{:S(2)}, u32[]{:S(2)}) collective-permute-start(bf16[160,512]{1,0:T(8,128)(2,1)S(1)} %get-tuple-element.238), channel_id=1, source_target_pairs={{0,16},{8,24},{16,0},{24,8},{1,17},{9,25},{17,1},{25,9},{2,18},{10... | collective-permute-start | bytes 491528 | tf_op jit(solution)/shard_map/ppermute | solution.py:520
  (94 other events, 570.1 us)

commit v5 on v4

--- a/solution.py
+++ b/solution.py
@@ -697,9 +697,7 @@
         (partial, jnp.stack([stride_bias_twelve, stride_bias_sixteen])),
         8,
     )
-    hidden_all, x_high, y_low = together(
-        swap(hidden_low), across(high_blocks, "tm", 1), across(low_blocks, "series", 2)
-    )
+    hidden_all, y_low = together(swap(hidden_low), across(low_blocks, "series", 2))
     (partial,) = kernel_call(
         functools.partial(iso_body, geo),
         step_block,
@@ -707,10 +705,8 @@
         32,
         scalars=(0,),
     )
+    partial, x_high = together(swap(partial), across(after(high_blocks, partial), "tm", 1))
     first = (x_low, x_high, y_low, y_high)
-    partial, blocks_a, blocks_b = together(
-        swap(partial), across(x_low, "series", 2), across(y_high, "tm", 1)
-    )
     hidden_two, mixed_low = kernel_call(
         functools.partial(mix_body, geo),
         [(own_steps, F32), ((n, *own_steps), BF)],
@@ -726,7 +722,12 @@
     (season,) = kernel_call(
         season_body, [((2, rows, channels), F32)], (tokens, left, right, token_info), 24
     )
-    mixed_all, season = together(swap(mixed_low), season)
+    mixed_all, season, blocks_a, blocks_b = together(
+        swap(mixed_low),
+        season,
+        across(after(x_low, mixed_low), "series", 2),
+        across(after(y_high, mixed_low), "tm", 1),
+    )
     (ups,) = kernel_call(
         functools.partial(slab_out_body, geo), [(pay_shape, BF)], (mixed_all, up_own), 24
     )

time: 363 us -> 361 us (level)
  waiting for transfers between devices: 126 us -> 121 us
    unnamed x152 -> x150, local copies, waits for them, and re-layouts: 36.3 us -> 35.7 us
  transfers between devices with their start and end apart: 52 -> 52, of which waited for: 22 -> 20; matrix products, arithmetic and copies ran while one was open for 12% -> 12% of each run, Pallas kernels for 6% -> 6%
where the time goes in v5:
time: 361 us; the launch traced here: 359 us
  waiting for transfers between devices  121 us (34%)
  starting transfers between devices  103 us (29%)
  Pallas kernels  54.2 us (15%)
  local copies, waits for them, and re-layouts  49.9 us (14%)
  other arithmetic  28.8 us (8%)
    ppermute x36, waiting for transfers between devices, across(): lax.ppermute(x, axis, [(i, i ^ bit) for i in range(lax.axis_size(axis))])  80 us
    all_to_all x12, starting transfers between devices, swap(): return lax.all_to_all(x, 'tm', 0, 0)  55.7 us
    pallas_call x22, Pallas kernels, kernel_call(): pl.pallas_call(body, out_shape=[jax.ShapeDtypeStruct(shape, dtype) for sh...  54.2 us
    all_to_all x12, waiting for transfers between devices, swap(): return lax.all_to_all(x, 'tm', 0, 0)  41.5 us
    ppermute x36, starting transfers between devices, across(): lax.ppermute(x, axis, [(i, i ^ bit) for i in range(lax.axis_size(axis))])  36.7 us
    unnamed x150, local copies, waits for them, and re-layouts  35.7 us
    convert_element_type x11, other arithmetic, summed(): return sum((p.astype(F32) for p in parts)).astype(BF)  22.7 us
  transfers between devices with their start and end apart: 52, of which 20 were waited for; matrix products, arithmetic and copies ran while one was open for 12% of the time, Pallas kernels for 6%

profile of v5, /device:TPU:0, one launch (start us, length us, event | category | flops | bytes accessed | tf_op | source)
XLA Modules:
  0.0 359.0 jit_solution(8616397422703267251)
XLA Ops:
  2.5 4.1 %collective-permute-start.2 = (bf16[1,160,512]{2,1,0:T(8,128)(2,1)S(1)}, bf16[1,160,512]{2,1,0:T(8,128)(2,1)S(1)}, u32[]{:S(2)}, u32[]{:S(2)}) collective-permute-start(bf16[1,160,512]{2,1,0:T(8,128)(2,1)S(1)} %maximum_bitcast_fusion), channel_id=1, source_target_pairs={{0,4},{1,5},{2,6},{3,7},{4,0},{5,1},{6,2},{7,3},{8,12},{9,13},{10,... | collective-permute-start | bytes 491528 | tf_op jit(solution)/shard_map/ppermute | solution.py:520
  7.3 3.4 collective-permute-start
  18.8 4.9 %all-to-all-start = ((bf16[8,192,256]{2,1,0:T(8,128)(2,1)}), bf16[8,192,256]{2,1,0:T(8,128)(2,1)S(1)}, u32[]{:S(2)}, u32[]{:S(2)}) async-start(bf16[8,192,256]{2,1,0:T(8,128)(2,1)} %shard_map.459), calls=%async_computation | async-start | bytes 1572864 | tf_op jit(solution)/shard_map/all_to_all | solution.py:508
  27.4 18.3 %collective-permute-done.3 = bf16[2,160,512]{2,1,0:T(8,128)(2,1)} collective-permute-done((bf16[2,160,512]{2,1,0:T(8,128)(2,1)S(1)}, bf16[2,160,512]{2,1,0:T(8,128)(2,1)}, u32[]{:S(2)}, u32[]{:S(2)}) %collective-permute-start.3) | collective-permute-done | bytes 327712 | tf_op jit(solution)/shard_map/ppermute | solution.py:520
  47.0 4.0 %all-to-all-start.1 = ((bf16[8,56,512]{2,1,0:T(8,128)(2,1)}), bf16[8,56,512]{2,1,0:T(8,128)(2,1)S(1)}, u32[]{:S(2)}, u32[]{:S(2)}) async-start(bf16[8,56,512]{2,1,0:T(8,128)(2,1)} %shard_map.460), calls=%async_computation.1 | async-start | bytes 917504 | tf_op jit(solution)/shard_map/all_to_all | solution.py:508
  55.8 8.5 %collective-permute-done.4.refs_16_ = bf16[2,160,512]{2,1,0:T(8,128)(2,1)S(1)} collective-permute-done((bf16[2,160,512]{2,1,0:T(8,128)(2,1)S(1)}, bf16[2,160,512]{2,1,0:T(8,128)(2,1)S(1)}, u32[]{:S(2)}, u32[]{:S(2)}) %collective-permute-start.4) | collective-permute-done | bytes 327712 | tf_op jit(solution)/shard_map/ppermute | solution.py:520
  65.9 4.6 %all-to-all-start.2 = ((bf16[8,56,512]{2,1,0:T(8,128)(2,1)}), bf16[8,56,512]{2,1,0:T(8,128)(2,1)S(1)}, u32[]{:S(2)}, u32[]{:S(2)}) async-start(bf16[8,56,512]{2,1,0:T(8,128)(2,1)} %get-tuple-element.129), calls=%async_computation.2 | async-start | bytes 917504 | tf_op jit(solution)/shard_map/all_to_all | solution.py:508
  74.2 5.8 %collective-permute-done.6.refs_18_ = bf16[2,160,512]{2,1,0:T(8,128)(2,1)} collective-permute-done((bf16[2,160,512]{2,1,0:T(8,128)(2,1)}, bf16[2,160,512]{2,1,0:T(8,128)(2,1)}, u32[]{:S(2)}, u32[]{:S(2)}) %collective-permute-start.6) | collective-permute-done | bytes 327712 | tf_op jit(solution)/shard_map/ppermute | solution.py:520
  80.0 2.9 all-to-all-done.2.steps
  87.5 4.1 %all-to-all-start.3 = ((bf16[8,56,512]{2,1,0:T(8,128)(2,1)}), bf16[8,56,512]{2,1,0:T(8,128)(2,1)}, u32[]{:S(2)}, u32[]{:S(2)}) async-start(bf16[8,56,512]{2,1,0:T(8,128)(2,1)} %copy-done.21), calls=%async_computation.3 | async-start | bytes 917504 | tf_op jit(solution)/shard_map/all_to_all | solution.py:508
  93.5 11.3 %collective-permute-done.7.refs_17_ = bf16[2,160,512]{2,1,0:T(8,128)(2,1)S(1)} collective-permute-done((bf16[2,160,512]{2,1,0:T(8,128)(2,1)}, bf16[2,160,512]{2,1,0:T(8,128)(2,1)S(1)}, u32[]{:S(2)}, u32[]{:S(2)}) %collective-permute-start.7) | collective-permute-done | bytes 327712 | tf_op jit(solution)/shard_map/ppermute | solution.py:520
  108.5 4.5 %all-to-all-start.4 = ((bf16[8,56,512]{2,1,0:T(8,128)(2,1)}), bf16[8,56,512]{2,1,0:T(8,128)(2,1)S(1)}, u32[]{:S(2)}, u32[]{:S(2)}) async-start(bf16[8,56,512]{2,1,0:T(8,128)(2,1)} %copy-done.41), calls=%async_computation.4 | async-start | bytes 917504 | tf_op jit(solution)/shard_map/all_to_all | solution.py:508
  129.5 4.7 %all-to-all-start.5 = ((bf16[8,192,256]{2,1,0:T(8,128)(2,1)}), bf16[8,192,256]{2,1,0:T(8,128)(2,1)}, u32[]{:S(2)}, u32[]{:S(2)}) async-start(bf16[8,192,256]{2,1,0:T(8,128)(2,1)} %copy-done.15), calls=%async_computation.5 | async-start | bytes 1572864 | tf_op jit(solution)/shard_map/all_to_all | solution.py:508
  142.4 11.0 %all-to-all-done.5.refs_0_ = bf16[8,192,256]{2,1,0:T(8,128)(2,1)} async-done(((bf16[8,192,256]{2,1,0:T(8,128)(2,1)}), bf16[8,192,256]{2,1,0:T(8,128)(2,1)}, u32[]{:S(2)}, u32[]{:S(2)}) %all-to-all-start.5) | async-done | bytes 786464 | tf_op jit(solution)/shard_map/all_to_all | solution.py:508
  153.4 20.5 %shard_map.466 = (bf16[8,192,256]{2,1,0:T(8,128)(2,1)}, bf16[384,512]{1,0:T(8,128)(2,1)}, f32[2,384,512]{2,1,0:T(8,128)}, f32[16,512]{1,0:T(8,128)}, bf16[16,176...) custom-call(bf16[8,192,256]{2,1,0:T(8,128)(2,1)} %all-to-all-done.5.refs_0_, f32[2,384,512]{2,1,0:T(8,128)} %copy-done.7, ...), custom_call_target="tpu_custom_call" | custom-call | tf_op jit(solution)/shard_map/pallas_call | solution.py:42
  174.0 4.4 %all-to-all-start.6 = ((bf16[8,192,256]{2,1,0:T(8,128)(2,1)}), bf16[8,192,256]{2,1,0:T(8,128)(2,1)}, u32[]{:S(2)}, u32[]{:S(2)}) async-start(bf16[8,192,256]{2,1,0:T(8,128)(2,1)} %get-tuple-element.155), calls=%async_computation.6 | async-start | bytes 1572864 | tf_op jit(solution)/shard_map/all_to_all | solution.py:508
  179.6 3.7 %add_convert_fusion = bf16[16,176,512]{2,1,0:T(8,128)(2,1)S(1)} fusion(bf16[16,176,512]{2,1,0:T(8,128)(2,1)} %collective-permute-done.17, bf16[16,176,512]{2,1,0:T(8,128)(2,1)} %get-tuple-element.156), kind=kLoop, calls=%fused_computation | loop fusion | flops 5767168 | bytes 8650752 | tf_op jit(solution)/shard_map/convert_element_type | solution.py:553
  190.0 9.3 %all-to-all-done.6.payload = bf16[8,192,256]{2,1,0:T(8,128)(2,1)} async-done(((bf16[8,192,256]{2,1,0:T(8,128)(2,1)}), bf16[8,192,256]{2,1,0:T(8,128)(2,1)}, u32[]{:S(2)}, u32[]{:S(2)}) %all-to-all-start.6) | async-done | bytes 786464 | tf_op jit(solution)/shard_map/all_to_all | solution.py:508
  203.3 4.9 %all-to-all-start.7 = ((bf16[8,56,512]{2,1,0:T(8,128)(2,1)}), bf16[8,56,512]{2,1,0:T(8,128)(2,1)}, u32[]{:S(2)}, u32[]{:S(2)}) async-start(bf16[8,56,512]{2,1,0:T(8,128)(2,1)} %copy-done.19), calls=%async_computation.7 | async-start | bytes 917504 | tf_op jit(solution)/shard_map/all_to_all | solution.py:508
  219.1 4.8 %collective-permute-done.20 = bf16[2,176,512]{2,1,0:T(8,128)(2,1)} collective-permute-done((bf16[2,176,512]{2,1,0:T(8,128)(2,1)S(1)}, bf16[2,176,512]{2,1,0:T(8,128)(2,1)}, u32[]{:S(2)}, u32[]{:S(2)}) %collective-permute-start.20) | collective-permute-done | bytes 360480 | tf_op jit(solution)/shard_map/ppermute | solution.py:520
  230.4 5.5 %all-to-all-start.8 = ((bf16[8,64,512]{2,1,0:T(8,128)(2,1)}), bf16[8,64,512]{2,1,0:T(8,128)(2,1)S(1)}, u32[]{:S(2)}, u32[]{:S(2)}) async-start(bf16[8,64,512]{2,1,0:T(8,128)(2,1)} %copy-done.40), calls=%async_computation.8 | async-start | bytes 1048576 | tf_op jit(solution)/shard_map/all_to_all | solution.py:508
  236.0 3.6 %collective-permute-done.23 = bf16[2,176,512]{2,1,0:T(8,128)(2,1)} collective-permute-done((bf16[2,176,512]{2,1,0:T(8,128)(2,1)}, bf16[2,176,512]{2,1,0:T(8,128)(2,1)}, u32[]{:S(2)}, u32[]{:S(2)}) %collective-permute-start.23) | collective-permute-done | bytes 360480 | tf_op jit(solution)/shard_map/ppermute | solution.py:520
  239.6 4.4 %collective-permute-done.24 = bf16[2,176,512]{2,1,0:T(8,128)(2,1)} collective-permute-done((bf16[2,176,512]{2,1,0:T(8,128)(2,1)}, bf16[2,176,512]{2,1,0:T(8,128)(2,1)}, u32[]{:S(2)}, u32[]{:S(2)}) %collective-permute-start.24) | collective-permute-done | bytes 360480 | tf_op jit(solution)/shard_map/ppermute | solution.py:520
  244.0 2.7 fusion.1
  255.6 4.8 %all-to-all-start.9 = ((bf16[8,56,512]{2,1,0:T(8,128)(2,1)}), bf16[8,56,512]{2,1,0:T(8,128)(2,1)S(1)}, u32[]{:S(2)}, u32[]{:S(2)}) async-start(bf16[8,56,512]{2,1,0:T(8,128)(2,1)} %copy-done.20), calls=%async_computation.9 | async-start | bytes 917504 | tf_op jit(solution)/shard_map/all_to_all | solution.py:508
  268.5 8.2 %collective-permute-done.26 = bf16[2,176,512]{2,1,0:T(8,128)(2,1)S(1)} collective-permute-done((bf16[2,176,512]{2,1,0:T(8,128)(2,1)}, bf16[2,176,512]{2,1,0:T(8,128)(2,1)S(1)}, u32[]{:S(2)}, u32[]{:S(2)}) %collective-permute-start.26) | collective-permute-done | bytes 360480 | tf_op jit(solution)/shard_map/ppermute | solution.py:520
  281.2 4.6 %all-to-all-start.10 = ((bf16[8,56,512]{2,1,0:T(8,128)(2,1)}), bf16[8,56,512]{2,1,0:T(8,128)(2,1)S(1)}, u32[]{:S(2)}, u32[]{:S(2)}) async-start(bf16[8,56,512]{2,1,0:T(8,128)(2,1)} %shard_map.473), calls=%async_computation.10 | async-start | bytes 917504 | tf_op jit(solution)/shard_map/all_to_all | solution.py:508
  292.2 7.3 %all-to-all-done.10.steps = bf16[8,56,512]{2,1,0:T(8,128)(2,1)S(1)} async-done(((bf16[8,56,512]{2,1,0:T(8,128)(2,1)}), bf16[8,56,512]{2,1,0:T(8,128)(2,1)S(1)}, u32[]{:S(2)}, u32[]{:S(2)}) %all-to-all-start.10) | async-done | bytes 458784 | tf_op jit(solution)/shard_map/all_to_all | solution.py:508
  301.1 4.6 %all-to-all-start.11 = ((bf16[8,192,256]{2,1,0:T(8,128)(2,1)}), bf16[8,192,256]{2,1,0:T(8,128)(2,1)}, u32[]{:S(2)}, u32[]{:S(2)}) async-start(bf16[8,192,256]{2,1,0:T(8,128)(2,1)} %copy-done.16), calls=%async_computation.11 | async-start | bytes 1572864 | tf_op jit(solution)/shard_map/all_to_all | solution.py:508
  316.0 9.4 %all-to-all-done.11.refs_0_ = bf16[8,192,256]{2,1,0:T(8,128)(2,1)} async-done(((bf16[8,192,256]{2,1,0:T(8,128)(2,1)}), bf16[8,192,256]{2,1,0:T(8,128)(2,1)}, u32[]{:S(2)}, u32[]{:S(2)}) %all-to-all-start.11) | async-done | bytes 786464 | tf_op jit(solution)/shard_map/all_to_all | solution.py:508
  328.6 4.5 %collective-permute-start.31 = (f32[16,512]{1,0:T(8,128)S(1)}, f32[16,512]{1,0:T(8,128)S(1)}, u32[]{:S(2)}, u32[]{:S(2)}) collective-permute-start(f32[16,512]{1,0:T(8,128)S(1)} %get-tuple-element.196), channel_id=1, source_target_pairs={{0,1},{1,2},{2,3},{3,4},{4,5},{5,6},{6,7},{8,9},{9,10},{10,11},{11... | collective-permute-start | bytes 98312 | tf_op jit(solution)/shard_map/ppermute | solution.py:910
  339.3 9.4 %collective-permute-done.38 = bf16[160,512]{1,0:T(8,128)(2,1)S(1)} collective-permute-done((bf16[160,512]{1,0:T(8,128)(2,1)S(1)}, bf16[160,512]{1,0:T(8,128)(2,1)S(1)}, u32[]{:S(2)}, u32[]{:S(2)}) %collective-permute-start.38) | collective-permute-done | bytes 163872 | tf_op jit(solution)/shard_map/ppermute | solution.py:520
  (324 shorter events, 148.5 us)
Async XLA Ops:
  2.5 14.8 %collective-permute-start.2 = (bf16[1,160,512]{2,1,0:T(8,128)(2,1)S(1)}, bf16[1,160,512]{2,1,0:T(8,128)(2,1)S(1)}, u32[]{:S(2)}, u32[]{:S(2)}) collective-permute-start(bf16[1,160,512]{2,1,0:T(8,128)(2,1)S(1)} %maximum_bitcast_fusion), channel_id=1, source_target_pairs={{0,4},{1,5},{2,6},{3,7},{4,0},{5,1},{6,2},{7,3},{8,12},{9,13},{10,... | collective-permute-start | bytes 491528 | tf_op jit(solution)/shard_map/ppermute | solution.py:520
  18.8 26.9 %all-to-all-start = ((bf16[8,192,256]{2,1,0:T(8,128)(2,1)}), bf16[8,192,256]{2,1,0:T(8,128)(2,1)S(1)}, u32[]{:S(2)}, u32[]{:S(2)}) async-start(bf16[8,192,256]{2,1,0:T(8,128)(2,1)} %shard_map.459), calls=%async_computation | async-start | bytes 1572864 | tf_op jit(solution)/shard_map/all_to_all | solution.py:508
  23.8 21.9 %collective-permute-start.3 = (bf16[2,160,512]{2,1,0:T(8,128)(2,1)S(1)}, bf16[2,160,512]{2,1,0:T(8,128)(2,1)}, u32[]{:S(2)}, u32[]{:S(2)}) collective-permute-start(bf16[2,160,512]{2,1,0:T(8,128)(2,1)S(1)} %pad_maximum_fusion.2), channel_id=1, source_target_pairs={{0,2},{1,3},{2,0},{3,1},{4,6},{5,7},{6,4},{7,5},{8,10},{9,11},{10,... | collective-permute-start | bytes 983048 | tf_op jit(solution)/shard_map/ppermute | solution.py:520
  47.0 17.3 %all-to-all-start.1 = ((bf16[8,56,512]{2,1,0:T(8,128)(2,1)}), bf16[8,56,512]{2,1,0:T(8,128)(2,1)S(1)}, u32[]{:S(2)}, u32[]{:S(2)}) async-start(bf16[8,56,512]{2,1,0:T(8,128)(2,1)} %shard_map.460), calls=%async_computation.1 | async-start | bytes 917504 | tf_op jit(solution)/shard_map/all_to_all | solution.py:508
  51.9 12.4 %collective-permute-start.4 = (bf16[2,160,512]{2,1,0:T(8,128)(2,1)S(1)}, bf16[2,160,512]{2,1,0:T(8,128)(2,1)S(1)}, u32[]{:S(2)}, u32[]{:S(2)}) collective-permute-start(bf16[2,160,512]{2,1,0:T(8,128)(2,1)S(1)} %copy-done.66), channel_id=1, source_target_pairs={{0,1},{1,0},{2,3},{3,2},{4,5},{5,4},{6,7},{7,6},{8,9},{9,8},{10,11... | collective-permute-start | bytes 983048 | tf_op jit(solution)/shard_map/ppermute | solution.py:520
  65.9 16.9 %all-to-all-start.2 = ((bf16[8,56,512]{2,1,0:T(8,128)(2,1)}), bf16[8,56,512]{2,1,0:T(8,128)(2,1)S(1)}, u32[]{:S(2)}, u32[]{:S(2)}) async-start(bf16[8,56,512]{2,1,0:T(8,128)(2,1)} %get-tuple-element.129), calls=%async_computation.2 | async-start | bytes 917504 | tf_op jit(solution)/shard_map/all_to_all | solution.py:508
  87.5 17.3 %all-to-all-start.3 = ((bf16[8,56,512]{2,1,0:T(8,128)(2,1)}), bf16[8,56,512]{2,1,0:T(8,128)(2,1)}, u32[]{:S(2)}, u32[]{:S(2)}) async-start(bf16[8,56,512]{2,1,0:T(8,128)(2,1)} %copy-done.21), calls=%async_computation.3 | async-start | bytes 917504 | tf_op jit(solution)/shard_map/all_to_all | solution.py:508
  91.6 13.2 %collective-permute-start.7 = (bf16[2,160,512]{2,1,0:T(8,128)(2,1)}, bf16[2,160,512]{2,1,0:T(8,128)(2,1)S(1)}, u32[]{:S(2)}, u32[]{:S(2)}) collective-permute-start(bf16[2,160,512]{2,1,0:T(8,128)(2,1)} %collective-permute-done.3), channel_id=1, source_target_pairs={{0,1},{1,0},{2,3},{3,2},{4,5},{5,4},{6,7},{7,6},{8,9},{9,8},{10,11... | collective-permute-start | bytes 983048 | tf_op jit(solution)/shard_map/ppermute | solution.py:520
  108.5 17.9 %all-to-all-start.4 = ((bf16[8,56,512]{2,1,0:T(8,128)(2,1)}), bf16[8,56,512]{2,1,0:T(8,128)(2,1)S(1)}, u32[]{:S(2)}, u32[]{:S(2)}) async-start(bf16[8,56,512]{2,1,0:T(8,128)(2,1)} %copy-done.41), calls=%async_computation.4 | async-start | bytes 917504 | tf_op jit(solution)/shard_map/all_to_all | solution.py:508
  113.1 13.3 %collective-permute-start.9 = (bf16[2,160,512]{2,1,0:T(8,128)(2,1)}, bf16[2,160,512]{2,1,0:T(8,128)(2,1)}, u32[]{:S(2)}, u32[]{:S(2)}) collective-permute-start(bf16[2,160,512]{2,1,0:T(8,128)(2,1)} %copy-done.63), channel_id=1, source_target_pairs={{0,1},{1,0},{2,3},{3,2},{4,5},{5,4},{6,7},{7,6},{8,9},{9,8},{10,11... | collective-permute-start | bytes 983048 | tf_op jit(solution)/shard_map/ppermute | solution.py:520
  115.2 11.2 %collective-permute-start.8 = (bf16[2,160,512]{2,1,0:T(8,128)(2,1)}, bf16[2,160,512]{2,1,0:T(8,128)(2,1)}, u32[]{:S(2)}, u32[]{:S(2)}) collective-permute-start(bf16[2,160,512]{2,1,0:T(8,128)(2,1)} %copy-done.62), channel_id=1, source_target_pairs={{0,16},{8,24},{16,0},{24,8},{1,17},{9,25},{17,1},{25,9},{2,18},{10... | collective-permute-start | bytes 983048 | tf_op jit(solution)/shard_map/ppermute | solution.py:520
  129.5 23.9 %all-to-all-start.5 = ((bf16[8,192,256]{2,1,0:T(8,128)(2,1)}), bf16[8,192,256]{2,1,0:T(8,128)(2,1)}, u32[]{:S(2)}, u32[]{:S(2)}) async-start(bf16[8,192,256]{2,1,0:T(8,128)(2,1)} %copy-done.15), calls=%async_computation.5 | async-start | bytes 1572864 | tf_op jit(solution)/shard_map/all_to_all | solution.py:508
  174.0 25.3 %all-to-all-start.6 = ((bf16[8,192,256]{2,1,0:T(8,128)(2,1)}), bf16[8,192,256]{2,1,0:T(8,128)(2,1)}, u32[]{:S(2)}, u32[]{:S(2)}) async-start(bf16[8,192,256]{2,1,0:T(8,128)(2,1)} %get-tuple-element.155), calls=%async_computation.6 | async-start | bytes 1572864 | tf_op jit(solution)/shard_map/all_to_all | solution.py:508
  184.3 15.0 %collective-permute-start.18 = (bf16[2,176,512]{2,1,0:T(8,128)(2,1)}, bf16[2,176,512]{2,1,0:T(8,128)(2,1)}, u32[]{:S(2)}, u32[]{:S(2)}) collective-permute-start(bf16[2,176,512]{2,1,0:T(8,128)(2,1)} %get-tuple-element.235), channel_id=1, source_target_pairs={{0,1},{1,0},{2,3},{3,2},{4,5},{5,4},{6,7},{7,6},{8,9},{9,8},{10,11... | collective-permute-start | bytes 1081352 | tf_op jit(solution)/shard_map/ppermute | solution.py:520
  185.7 13.7 %collective-permute-start.19 = (bf16[2,176,512]{2,1,0:T(8,128)(2,1)}, bf16[2,176,512]{2,1,0:T(8,128)(2,1)}, u32[]{:S(2)}, u32[]{:S(2)}) collective-permute-start(bf16[2,176,512]{2,1,0:T(8,128)(2,1)} %get-tuple-element.234), channel_id=1, source_target_pairs={{0,16},{8,24},{16,0},{24,8},{1,17},{9,25},{17,1},{25,9},{2,18},{10... | collective-permute-start | bytes 1081352 | tf_op jit(solution)/shard_map/ppermute | solution.py:520
  203.3 20.6 %all-to-all-start.7 = ((bf16[8,56,512]{2,1,0:T(8,128)(2,1)}), bf16[8,56,512]{2,1,0:T(8,128)(2,1)}, u32[]{:S(2)}, u32[]{:S(2)}) async-start(bf16[8,56,512]{2,1,0:T(8,128)(2,1)} %copy-done.19), calls=%async_computation.7 | async-start | bytes 917504 | tf_op jit(solution)/shard_map/all_to_all | solution.py:508
  209.3 14.6 %collective-permute-start.20 = (bf16[2,176,512]{2,1,0:T(8,128)(2,1)S(1)}, bf16[2,176,512]{2,1,0:T(8,128)(2,1)}, u32[]{:S(2)}, u32[]{:S(2)}) collective-permute-start(bf16[2,176,512]{2,1,0:T(8,128)(2,1)S(1)} %get-tuple-element.233), channel_id=1, source_target_pairs={{0,1},{1,0},{2,3},{3,2},{4,5},{5,4},{6,7},{7,6},{8,9},{9,8},{10,11... | collective-permute-start | bytes 1081352 | tf_op jit(solution)/shard_map/ppermute | solution.py:520
  211.4 12.5 %collective-permute-start.21 = (bf16[2,176,512]{2,1,0:T(8,128)(2,1)S(1)}, bf16[2,176,512]{2,1,0:T(8,128)(2,1)}, u32[]{:S(2)}, u32[]{:S(2)}) collective-permute-start(bf16[2,176,512]{2,1,0:T(8,128)(2,1)S(1)} %get-tuple-element.232), channel_id=1, source_target_pairs={{0,16},{8,24},{16,0},{24,8},{1,17},{9,25},{17,1},{25,9},{2,18},{10... | collective-permute-start | bytes 1081352 | tf_op jit(solution)/shard_map/ppermute | solution.py:520
  223.9 22.7 %collective-permute-start.22 = (bf16[912,512]{1,0:T(8,128)(2,1)}, bf16[912,512]{1,0:T(8,128)(2,1)}, u32[]{:S(2)}, u32[]{:S(2)}) collective-permute-start(bf16[912,512]{1,0:T(8,128)(2,1)} %copy-done.49), channel_id=1, source_target_pairs={{0,8},{8,0},{16,24},{24,16},{1,9},{9,1},{17,25},{25,17},{2,10},{10... | collective-permute-start | bytes 2801672 | tf_op jit(solution)/shard_map/ppermute | solution.py:520
  228.5 11.1 %collective-permute-start.23 = (bf16[2,176,512]{2,1,0:T(8,128)(2,1)}, bf16[2,176,512]{2,1,0:T(8,128)(2,1)}, u32[]{:S(2)}, u32[]{:S(2)}) collective-permute-start(bf16[2,176,512]{2,1,0:T(8,128)(2,1)} %get-tuple-element.172), channel_id=1, source_target_pairs={{0,16},{8,24},{16,0},{24,8},{1,17},{9,25},{17,1},{25,9},{2,18},{10... | collective-permute-start | bytes 1081352 | tf_op jit(solution)/shard_map/ppermute | solution.py:520
  230.0 14.0 %collective-permute-start.24 = (bf16[2,176,512]{2,1,0:T(8,128)(2,1)}, bf16[2,176,512]{2,1,0:T(8,128)(2,1)}, u32[]{:S(2)}, u32[]{:S(2)}) collective-permute-start(bf16[2,176,512]{2,1,0:T(8,128)(2,1)} %get-tuple-element.175), channel_id=1, source_target_pairs={{0,1},{1,0},{2,3},{3,2},{4,5},{5,4},{6,7},{7,6},{8,9},{9,8},{10,11... | collective-permute-start | bytes 1081352 | tf_op jit(solution)/shard_map/ppermute | solution.py:520
  230.4 20.1 %all-to-all-start.8 = ((bf16[8,64,512]{2,1,0:T(8,128)(2,1)}), bf16[8,64,512]{2,1,0:T(8,128)(2,1)S(1)}, u32[]{:S(2)}, u32[]{:S(2)}) async-start(bf16[8,64,512]{2,1,0:T(8,128)(2,1)} %copy-done.40), calls=%async_computation.8 | async-start | bytes 1048576 | tf_op jit(solution)/shard_map/all_to_all | solution.py:508
  250.6 27.9 %collective-permute-start.25 = (bf16[912,512]{1,0:T(8,128)(2,1)}, bf16[912,512]{1,0:T(8,128)(2,1)}, u32[]{:S(2)}, u32[]{:S(2)}) collective-permute-start(bf16[912,512]{1,0:T(8,128)(2,1)} %add_convert_fusion.6), channel_id=1, source_target_pairs={{0,16},{8,24},{16,0},{24,8},{1,17},{9,25},{17,1},{25,9},{2,18},{10... | collective-permute-start | bytes 2801672 | tf_op jit(solution)/shard_map/ppermute | solution.py:520
  255.6 22.9 %all-to-all-start.9 = ((bf16[8,56,512]{2,1,0:T(8,128)(2,1)}), bf16[8,56,512]{2,1,0:T(8,128)(2,1)S(1)}, u32[]{:S(2)}, u32[]{:S(2)}) async-start(bf16[8,56,512]{2,1,0:T(8,128)(2,1)} %copy-done.20), calls=%async_computation.9 | async-start | bytes 917504 | tf_op jit(solution)/shard_map/all_to_all | solution.py:508
  260.4 16.2 %collective-permute-start.26 = (bf16[2,176,512]{2,1,0:T(8,128)(2,1)}, bf16[2,176,512]{2,1,0:T(8,128)(2,1)S(1)}, u32[]{:S(2)}, u32[]{:S(2)}) collective-permute-start(bf16[2,176,512]{2,1,0:T(8,128)(2,1)} %get-tuple-element.182), channel_id=1, source_target_pairs={{0,2},{1,3},{2,0},{3,1},{4,6},{5,7},{6,4},{7,5},{8,10},{9,11},{10,... | collective-permute-start | bytes 1081352 | tf_op jit(solution)/shard_map/ppermute | solution.py:520
  281.2 18.3 %all-to-all-start.10 = ((bf16[8,56,512]{2,1,0:T(8,128)(2,1)}), bf16[8,56,512]{2,1,0:T(8,128)(2,1)S(1)}, u32[]{:S(2)}, u32[]{:S(2)}) async-start(bf16[8,56,512]{2,1,0:T(8,128)(2,1)} %shard_map.473), calls=%async_computation.10 | async-start | bytes 917504 | tf_op jit(solution)/shard_map/all_to_all | solution.py:508
  287.3 12.2 %collective-permute-start.28 = (bf16[304,512]{1,0:T(8,128)(2,1)S(1)}, bf16[304,512]{1,0:T(8,128)(2,1)}, u32[]{:S(2)}, u32[]{:S(2)}) collective-permute-start(bf16[304,512]{1,0:T(8,128)(2,1)S(1)} %slice.158), channel_id=1, source_target_pairs={{0,16},{8,24},{16,0},{24,8},{1,17},{9,25},{17,1},{25,9},{2,18},{10... | collective-permute-start | bytes 933896 | tf_op jit(solution)/shard_map/ppermute | solution.py:520
  301.1 24.3 %all-to-all-start.11 = ((bf16[8,192,256]{2,1,0:T(8,128)(2,1)}), bf16[8,192,256]{2,1,0:T(8,128)(2,1)}, u32[]{:S(2)}, u32[]{:S(2)}) async-start(bf16[8,192,256]{2,1,0:T(8,128)(2,1)} %copy-done.16), calls=%async_computation.11 | async-start | bytes 1572864 | tf_op jit(solution)/shard_map/all_to_all | solution.py:508
  308.9 24.3 %collective-permute-start.35 = (bf16[608,512]{1,0:T(8,128)(2,1)}, bf16[608,512]{1,0:T(8,128)(2,1)}, u32[]{:S(2)}, u32[]{:S(2)}) collective-permute-start(bf16[608,512]{1,0:T(8,128)(2,1)} %slice.157), channel_id=1, source_target_pairs={{0,16},{8,24},{16,0},{24,8},{1,17},{9,25},{17,1},{25,9},{2,18},{10... | collective-permute-start | bytes 1867784 | tf_op jit(solution)/shard_map/ppermute | solution.py:520
  314.7 34.1 %collective-permute-start.33 = (bf16[912,512]{1,0:T(8,128)(2,1)}, bf16[912,512]{1,0:T(8,128)(2,1)}, u32[]{:S(2)}, u32[]{:S(2)}) collective-permute-start(bf16[912,512]{1,0:T(8,128)(2,1)} %add_convert_fusion.3), channel_id=1, source_target_pairs={{0,16},{8,24},{16,0},{24,8},{1,17},{9,25},{17,1},{25,9},{2,18},{10... | collective-permute-start | bytes 2801672 | tf_op jit(solution)/shard_map/ppermute | solution.py:520
  325.4 12.2 %collective-permute-start.37 = (bf16[176,512]{1,0:T(8,128)(2,1)}, bf16[176,512]{1,0:T(8,128)(2,1)S(1)}, u32[]{:S(2)}, u32[]{:S(2)}) collective-permute-start(bf16[176,512]{1,0:T(8,128)(2,1)} %slice_bitcast_fusion.4), channel_id=1, source_target_pairs={{0,4},{1,5},{2,6},{3,7},{4,0},{5,1},{6,2},{7,3},{8,12},{9,13},{10,... | collective-permute-start | bytes 540680 | tf_op jit(solution)/shard_map/ppermute | solution.py:520
  334.7 19.1 %collective-permute-start.36 = (bf16[912,512]{1,0:T(8,128)(2,1)S(1)}, bf16[912,512]{1,0:T(8,128)(2,1)S(1)}, u32[]{:S(2)}, u32[]{:S(2)}) collective-permute-start(bf16[912,512]{1,0:T(8,128)(2,1)S(1)} %add_convert_fusion.1.part), channel_id=1, source_target_pairs={{0,8},{8,0},{16,24},{24,16},{1,9},{9,1},{17,25},{25,17},{2,10},{10... | collective-permute-start | bytes 2801672 | tf_op jit(solution)/shard_map/ppermute | solution.py:520
  (93 other events, 560.4 us)
